TPU v7x, 32 devices: a whole 2x2x4 slice. The times are simulated.
32 devices in a mesh: row: 8 (over z, core), col: 4 (over y, x).
Axes of the slice: x: 2, y: 2, z: 4, core: 2. Of those that a mesh axis runs over, the one named last changes fastest.
Arguments:
- tokens: bfloat16 [2048, 14336], P('row'), may hold values from -6 to 6
- qkv_weight: bfloat16 [14336, 4, 8, 336], P(None, 'col', 'row'), may hold values from -0.046875 to 0.046875
- qkv_bias: float32 [10752], P('col'), may hold values from -6 to 6
Outputs:
- joined_qkv: bfloat16 [2048, 10752], P('row', 'col')
All inputs are finite; a program needn't handle non-finite values.
Results may differ from a plain program's by a relative error of at most 0.01.
Values may be sent and summed in bfloat16 or wider, within the bound.
No kernel may reach another device: no remote copies, remote signals or barrier semaphores. Data moves between devices by JAX's collectives and lax.ppermute only.
A program may use at most 128 MiB of HBM per device.

v0:
```python
import jax
import jax.numpy as jnp
from jax import lax
from jax.sharding import PartitionSpec as P


def shards(tokens, qkv_weight, qkv_bias):
    groups = lax.axis_size("row")
    local_w = qkv_weight.reshape(qkv_weight.shape[0], qkv_weight.shape[3])
    w_tile = lax.all_to_all(local_w, "row", split_axis=0, concat_axis=1, tiled=True)
    col_count = lax.axis_size("col")
    tok_rows = tokens.shape[0]
    feat_count = tokens.shape[1]
    layered = tokens.reshape(tok_rows, groups, col_count, feat_count // (groups * col_count))
    own_slice = lax.dynamic_slice_in_dim(layered, lax.axis_index("col"), 1, 2)
    own_slice = own_slice.reshape(tok_rows, feat_count // col_count)
    slivers = lax.all_to_all(own_slice, "row", split_axis=1, concat_axis=0, tiled=True)
    act_panel = lax.all_gather(slivers, "col", axis=1, tiled=True)
    summed = lax.psum_scatter(
        jnp.dot(act_panel, w_tile, preferred_element_type=jnp.float32).astype(jnp.bfloat16),
        "row",
        scatter_dimension=0,
        tiled=True,
    ).astype(jnp.float32)
    return (summed + qkv_bias[None, :]).astype(jnp.bfloat16)


def solution(mesh):
    return jax.shard_map(
        shards,
        mesh=mesh,
        in_specs=(P("row", None), P(None, "col", "row", None), P("col")),
        out_specs=P("row", "col"),
        check_vma=False,
    )
```

profile of v0, /device:TPU:0, one launch (start us, length us, event | category | flops | bytes accessed | tf_op | source)
XLA Modules:
  0.0 435.6 jit_solution(8433576158741325816)
XLA Ops:
  6.5 10.2 %copy.9 = bf16[256,14336]{0,1:T(8,128)(2,1)} copy(bf16[256,14336]{1,0:T(8,128)(2,1)} %param.3) | data formatting | bytes 14680064 | tf_op args[0]
  16.7 2.9 dynamic-slice_bitcast_fusion
  19.6 6.3 %all-to-all-start = ((bf16[256,8,448]{0,2,1:T(8,128)(2,1)}), bf16[256,8,448]{0,2,1:T(8,128)(2,1)S(1)}, u32[]{:S(2)}, u32[]{:S(2)}) async-start(bf16[256,8,448]{0,2,1:T(8,128)(2,1)} %dynamic-slice_bitcast_fusion), calls=%async_computation | async-start | bytes 3670016 | tf_op jit(solution)/shard_map/all_to_all | solution.py:17
  25.9 10.3 %copy.13 = bf16[42,8,8,1792]{3,2,1,0:T(8,128)(2,1)} copy(bf16[42,8,8,1792]{3,1,2,0:T(8,128)(2,1)} %bitcast.19) | data formatting | bytes 19267584
  36.2 9.3 %copy.11 = bf16[8,1792,336]{1,2,0:T(8,128)(2,1)} copy(bf16[8,1792,336]{1,0,2:T(8,128)(2,1)} %bitcast.17) | data formatting | bytes 19267584 | tf_op jit(solution)/shard_map/all_to_all | solution.py:10
  45.5 23.9 %all-to-all-done = bf16[256,8,448]{0,2,1:T(8,128)(2,1)S(1)} async-done(((bf16[256,8,448]{0,2,1:T(8,128)(2,1)}), bf16[256,8,448]{0,2,1:T(8,128)(2,1)S(1)}, u32[]{:S(2)}, u32[]{:S(2)}) %all-to-all-start) | async-done | bytes 1835040 | tf_op jit(solution)/shard_map/all_to_all | solution.py:17
  69.4 5.1 %all-to-all-start.1 = ((bf16[8,1792,336]{1,2,0:T(8,128)(2,1)}), bf16[8,1792,336]{1,2,0:T(8,128)(2,1)}, u32[]{:S(2)}, u32[]{:S(2)}) async-start(bf16[8,1792,336]{1,2,0:T(8,128)(2,1)} %copy.11), calls=%async_computation.1 | async-start | bytes 19267584 | tf_op jit(solution)/shard_map/all_to_all | solution.py:10
  74.4 0.0 all-gather.2.cloned.1.call-start
  74.5 1.5 copy.12
  76.0 0.0 all-gather.2.cloned.1.call-update
  76.0 0.0 reduce-scatter.2.cloned.1.call-start
  76.1 81.3 %all-gather.2.cloned.1.call-done = bf16[2048,1792]{0,1:T(8,128)(2,1)} async-done(((bf16[2048,448]{0,1:T(8,128)(2,1)}), bf16[2048,1792]{0,1:T(8,128)(2,1)}) %all-gather.2.cloned.1.call-update) | async-done | bytes 7340048 | tf_op jit(solution)/shard_map/all_gather | solution.py:18
  157.4 127.6 %all-to-all-done.1 = bf16[8,1792,336]{1,2,0:T(8,128)(2,1)} async-done(((bf16[8,1792,336]{1,2,0:T(8,128)(2,1)}), bf16[8,1792,336]{1,2,0:T(8,128)(2,1)}, u32[]{:S(2)}, u32[]{:S(2)}) %all-to-all-start.1) | async-done | bytes 9633824 | tf_op jit(solution)/shard_map/all_to_all | solution.py:10
  285.0 27.7 %convolution_convert_fusion = bf16[2048,2688]{1,0:T(8,128)(2,1)} fusion(bf16[2048,1792]{0,1:T(8,128)(2,1)} %all-gather.2.cloned.1.call-done, bf16[1792,2688]{0,1:T(8,128)(2,1)} %bitcast.4), kind=kOutput, calls=%fused_computation | convolution fusion | flops 19735511040 | bytes 27983872 | tf_op jit(solution)/shard_map/dot_general | solution.py:20
  312.7 0.0 copy-start
  312.7 0.0 reduce-scatter.2.cloned.1.call-update
  312.7 113.4 %reduce-scatter.2.cloned.1.call-done = bf16[256,2688]{1,0:T(8,128)(2,1)} async-done(((bf16[2048,2688]{1,0:T(8,128)(2,1)}), bf16[256,2688]{1,0:T(8,128)(2,1)}) %reduce-scatter.2.cloned.1.call-update) | async-done | bytes 1376272 | tf_op jit(solution)/shard_map/reduce_scatter | solution.py:19
  426.1 0.0 copy-done
  426.1 2.6 add_convert_fusion
Async XLA Ops:
  19.6 49.8 %all-to-all-start = ((bf16[256,8,448]{0,2,1:T(8,128)(2,1)}), bf16[256,8,448]{0,2,1:T(8,128)(2,1)S(1)}, u32[]{:S(2)}, u32[]{:S(2)}) async-start(bf16[256,8,448]{0,2,1:T(8,128)(2,1)} %dynamic-slice_bitcast_fusion), calls=%async_computation | async-start | bytes 3670016 | tf_op jit(solution)/shard_map/all_to_all | solution.py:17
  69.4 215.6 %all-to-all-start.1 = ((bf16[8,1792,336]{1,2,0:T(8,128)(2,1)}), bf16[8,1792,336]{1,2,0:T(8,128)(2,1)}, u32[]{:S(2)}, u32[]{:S(2)}) async-start(bf16[8,1792,336]{1,2,0:T(8,128)(2,1)} %copy.11), calls=%async_computation.1 | async-start | bytes 19267584 | tf_op jit(solution)/shard_map/all_to_all | solution.py:10
  74.4 83.0 %all-gather.2.cloned.1.call-start = ((), (), s32[]{:S(2)}) async-start(), calls=%async_computation.3 | async-start | bytes 9175040 | tf_op jit(solution)/shard_map/all_gather | solution.py:18
  76.0 350.1 %reduce-scatter.2.cloned.1.call-start = ((), (), s32[]{:S(2)}) async-start(), calls=%async_computation.4 | async-start | bytes 12386304 | tf_op jit(solution)/shard_map/reduce_scatter | solution.py:19
  312.7 113.4 %copy-start = (f32[2688]{0:T(1024)S(1)}, f32[2688]{0:T(1024)}, u32[]{:S(2)}) copy-start(f32[2688]{0:T(1024)} %param.5) | copy-start | bytes 32260
Sparse Core Ops, SparseCore 0:
  77.1 80.2 all-gather.1
  312.8 113.2 reduce-scatter.1
where the time goes:
time: 436 us
  waiting for transfers between devices  346 us (79%)
  local copies, waits for them, and re-layouts  34.2 us (8%)
  matrix products  27.7 us (6%)
  between operations  13.4 us (3%)
  starting transfers between devices  11.5 us (3%)
    all_to_all x1, waiting for transfers between devices, shards(): lax.all_to_all(local_w, 'row', split_axis=0, concat_axis=1, tiled=True)  128 us
    reduce_scatter x1, waiting for transfers between devices, shards(): lax.psum_scatter(jnp.dot(act_panel, w_tile, preferred_element_type=jnp.fl...  113 us
    all_gather x1, waiting for transfers between devices, shards(): act_panel = lax.all_gather(slivers, 'col', axis=1, tiled=True)  81.3 us
    dot_general x1, matrix products, shards(): jnp.dot(act_panel, w_tile, preferred_element_type=jnp.float32)  27.7 us
    all_to_all x1, waiting for transfers between devices, shards(): lax.all_to_all(own_slice, 'row', split_axis=1, concat_axis=0, tiled=True)  23.9 us
    unnamed x4, local copies, waits for them, and re-layouts  20.5 us
    all_to_all x1, local copies, waits for them, and re-layouts, shards(): lax.all_to_all(local_w, 'row', split_axis=0, concat_axis=1, tiled=True)  9.3 us
  transfers between devices with their start and end apart: 4, of which 4 were waited for; matrix products, arithmetic and copies ran while one was open for 5% of the time, Pallas kernels for 0%

commit v1 on v0

v1 whole, which is shorter than its diff:
```python
import functools

import jax
import jax.numpy as jnp
from jax import lax
from jax.experimental import pallas as pl
from jax.experimental.pallas import tpu as pltpu
from jax.sharding import PartitionSpec as P

VMEM = 56 * 1024 * 1024


def divisor(size, most):
    return max(d for d in range(128, most + 1, 128) if size % d == 0)


def product_kernel(n_w, n_t, *refs):
    w_refs, t_refs = refs[:n_w], refs[n_w : n_w + n_t]
    out_ref, total = refs[-2], refs[-1]
    step = pl.program_id(0)

    @pl.when(step == 0)
    def _():
        total[...] = jnp.zeros_like(total)

    rows = t_refs[0].shape[0]
    for i, w in enumerate(w_refs):
        for k, t in enumerate(t_refs):
            total[i, :, k * rows : (k + 1) * rows] += lax.dot_general(
                w[...], t[...], (((1,), (1,)), ((), ())), preferred_element_type=jnp.float32
            )

    @pl.when(step == pl.num_programs(0) - 1)
    def _():
        out_ref[...] = total[...].astype(out_ref.dtype)


def products(ws, ts, dtype):
    m, depth = ws[0].shape
    rows = ts[0].shape[0]
    block = divisor(depth, 1024)
    shape = (len(ws), m, rows * len(ts))
    return pl.pallas_call(
        functools.partial(product_kernel, len(ws), len(ts)),
        grid=(depth // block,),
        in_specs=[pl.BlockSpec((m, block), lambda i: (0, i)) for _ in ws]
        + [pl.BlockSpec((rows, block), lambda i: (0, i)) for _ in ts],
        out_specs=pl.BlockSpec(shape, lambda i: (0, 0, 0)),
        out_shape=jax.ShapeDtypeStruct(shape, dtype),
        scratch_shapes=[pltpu.VMEM(shape, jnp.float32)],
        compiler_params=pltpu.CompilerParams(vmem_limit_bytes=VMEM),
        cost_estimate=pl.CostEstimate(
            flops=2 * len(ws) * m * rows * len(ts) * depth,
            bytes_accessed=2 * depth * (m * len(ws) + rows * len(ts)) + 2 * len(ws) * m * rows * len(ts),
            transcendentals=0,
        ),
    )(*ws, *ts)


def join_kernel(n, *refs):
    part_refs, bias_ref, out_ref, joined = refs[:n], refs[n], refs[n + 1], refs[n + 2]
    m = part_refs[0].shape[0]
    me = lax.axis_index("row")
    for j, part in enumerate(part_refs):
        joined[pl.ds(pl.multiple_of((me ^ j) * m, 8), m), :] = part[...].astype(jnp.float32)
    block = divisor(out_ref.shape[1], 512)
    for i in range(out_ref.shape[1] // block):
        cols = slice(i * block, (i + 1) * block)
        out_ref[:, cols] = (joined[cols, :].T + bias_ref[:, cols]).astype(out_ref.dtype)


def join(parts, bias):
    m, rows = parts[0].shape
    n = len(parts)
    return pl.pallas_call(
        functools.partial(join_kernel, n),
        out_shape=jax.ShapeDtypeStruct((rows, n * m), jnp.bfloat16),
        in_specs=[pl.BlockSpec(memory_space=pltpu.VMEM)] * (n + 1),
        out_specs=pl.BlockSpec(memory_space=pltpu.VMEM),
        scratch_shapes=[pltpu.VMEM((n * m, rows), jnp.float32)],
        compiler_params=pltpu.CompilerParams(vmem_limit_bytes=VMEM),
        cost_estimate=pl.CostEstimate(flops=n * m * rows, bytes_accessed=4 * n * m * rows, transcendentals=0),
    )(*parts, bias[None, :])


def shards(tokens, qkv_weight, qkv_bias):
    n_row, n_col = lax.axis_size("row"), lax.axis_size("col")
    row, col = lax.axis_index("row"), lax.axis_index("col")
    planes = n_row // 2
    plane = row // 2
    feats = tokens.shape[1]
    band = feats // n_col
    weight = qkv_weight.reshape(feats, -1).T
    columns = weight.shape[0]

    def flip_col(x, j):
        return lax.ppermute(x, "col", [(i, i ^ j) for i in range(n_col)])

    def flip_row(x, j):
        return lax.ppermute(x, "row", [(i, i ^ j) for i in range(n_row)])

    own = lax.dynamic_slice_in_dim(tokens, col * band, band, 1)
    held = []
    last = {0: own, 1: own}
    for s in range(1, planes):
        now = {}
        for parity in (0, 1):
            pairs, came = [], {}
            for p in range(parity, planes - 1, 2):
                if p - s + 1 >= 0:
                    pairs.append((p, p + 1))
                    came[p + 1] = p - s + 1
                if p + s < planes:
                    pairs.append((p + 1, p))
                    came[p] = p + s
            if pairs:
                sent = last[1 - parity]
                now[parity] = lax.ppermute(sent, "row", [(2 * a + c, 2 * b + c) for a, b in pairs for c in (0, 1)])
                held.append((now[parity], came))
        last = now

    w_band = [lax.dynamic_slice_in_dim(weight, (col ^ j) * band, band, 1) for j in range(n_col)]
    w_band = [w_band[0]] + [flip_col(w_band[j], j) for j in range(1, n_col)]

    def arrived(d):
        wanted = [next(i for i, (_, came) in enumerate(held) if came.get(p) == p ^ d) for p in range(planes)]
        value = held[wanted[0]][0]
        for i in sorted(set(wanted) - {wanted[0]}):
            mine = functools.reduce(jnp.logical_or, [plane == p for p in range(planes) if wanted[p] == i])
            value = jnp.where(mine, held[i][0], value)
        return value

    half = tokens.shape[0]
    parts = [None] * n_row
    here = products([weight], [tokens, flip_row(tokens, 1)], jnp.bfloat16)[0]
    parts[0] = here[:, :half]
    parts[1] = flip_row(here[:, half:], 1)

    bits = [1 << b for b in range(n_col.bit_length() - 1)]
    for d in range(1, planes):
        same = arrived(d)
        both = [same, flip_row(same, 1)]
        order = bits[d % len(bits) :] + bits[: d % len(bits)]
        out = [j for j in range(n_col) if j & order[0]]
        kept = [j for j in range(n_col) if not j & order[0]]
        sent = products([w_band[j] for j in out], both, jnp.bfloat16)
        mine = products([w_band[j] for j in kept], both, jnp.float32)
        for n, bit in enumerate(order):
            got = flip_col(sent, bit).astype(jnp.float32)
            mine = mine + got
            if n + 1 < len(order):
                nxt = order[n + 1]
                go = [i for i, j in enumerate(kept) if j & nxt]
                stay = [i for i, j in enumerate(kept) if not j & nxt]
                sent = jnp.stack([mine[i] for i in go]).astype(jnp.bfloat16)
                mine = jnp.stack([mine[i] for i in stay])
                kept = [kept[i] for i in stay]
        done = mine[0].astype(jnp.bfloat16)
        parts[2 * d] = flip_row(done[:, :half], 2 * d)
        parts[2 * d + 1] = flip_row(done[:, half:], 2 * d + 1)
    return join(parts, qkv_bias)


def solution(mesh):
    return jax.shard_map(
        shards,
        mesh=mesh,
        in_specs=(P("row", None), P(None, "col", "row", None), P("col")),
        out_specs=P("row", "col"),
        check_vma=False,
    )
```

time: 436 us -> 288 us (0.66)
  waiting for transfers between devices: 346 us -> 165 us
  Pallas kernels: 0 us -> 62.5 us
  matrix products: 27.7 us -> 0 us
  starting transfers between devices: 11.5 us -> 30.6 us
  local copies, waits for them, and re-layouts: 34.2 us -> 16.7 us
  between operations: 13.4 us -> 0.29 us
  other arithmetic: 2.64 us -> 8.37 us
    ppermute x0 -> x25, waiting for transfers between devices: none -> 165 us  [the longest x9 96.3 us: flip_col(): return lax.ppermute(x, 'col', [(i, i ^ j) for i in range(n_col)])]
    all_to_all x2 -> x0, waiting for transfers between devices: 151 us -> none  [the longest x1 128 us: shards(): lax.all_to_all(local_w, 'row', split_axis=0, concat_axis=1, tiled=True)]
    reduce_scatter x1 -> x0, waiting for transfers between devices: 113 us -> none  [shards(): lax.psum_scatter(jnp.dot(act_panel, w_tile, preferred_element_type=jnp.fl...]
    all_gather x1 -> x0, waiting for transfers between devices: 81.3 us -> none  [shards(): act_panel = lax.all_gather(slivers, 'col', axis=1, tiled=True)]
    pallas_call x0 -> x8, Pallas kernels: none -> 62.5 us  [the longest x7 59 us: products(): pl.pallas_call(functools.partial(product_kernel, len(ws), len(ts)), grid=...]
    ppermute x0 -> x25, starting transfers between devices: none -> 30.6 us  [the longest x9 12 us: flip_col(): return lax.ppermute(x, 'col', [(i, i ^ j) for i in range(n_col)])]
    dot_general x1 -> x0, matrix products: 27.7 us -> none  [shards(): jnp.dot(act_panel, w_tile, preferred_element_type=jnp.float32)]
    unnamed x4 -> x30, local copies, waits for them, and re-layouts: 20.5 us -> 4.25 us
  transfers between devices with their start and end apart: 4 -> 25, of which waited for: 4 -> 8; matrix products, arithmetic and copies ran while one was open for 5% -> 6% of each run, Pallas kernels for 0% -> 21%
where the time goes in v1:
time: 288 us; the launch traced here: 284 us
  waiting for transfers between devices  165 us (57%)
  Pallas kernels  62.5 us (22%)
  starting transfers between devices  30.6 us (11%)
  local copies, waits for them, and re-layouts  16.7 us (6%)
  other arithmetic  8.37 us (3%)
    ppermute x9, waiting for transfers between devices, flip_col(): return lax.ppermute(x, 'col', [(i, i ^ j) for i in range(n_col)])  96.3 us
    ppermute x5, waiting for transfers between devices, shards(): lax.ppermute(sent, 'row', [(2 * a + c, 2 * b + c) for a, b in pairs for c...  61.1 us
    pallas_call x7, Pallas kernels, products(): pl.pallas_call(functools.partial(product_kernel, len(ws), len(ts)), grid=...  59 us
    ppermute x9, starting transfers between devices, flip_col(): return lax.ppermute(x, 'col', [(i, i ^ j) for i in range(n_col)])  12 us
    ppermute x5, starting transfers between devices, shards(): lax.ppermute(sent, 'row', [(2 * a + c, 2 * b + c) for a, b in pairs for c...  9.5 us
    ppermute x11, starting transfers between devices, flip_row(): return lax.ppermute(x, 'row', [(i, i ^ j) for i in range(n_row)])  9.14 us
    ppermute x11, waiting for transfers between devices, flip_row(): return lax.ppermute(x, 'row', [(i, i ^ j) for i in range(n_row)])  7.69 us
    dynamic_slice x1, local copies, waits for them, and re-layouts, shards(): lax.dynamic_slice_in_dim(weight, (col ^ j) * band, band, 1)  7.14 us
  transfers between devices with their start and end apart: 25, of which 8 were waited for; matrix products, arithmetic and copies ran while one was open for 6% of the time, Pallas kernels for 21%

profile of v1, /device:TPU:0, one launch (start us, length us, event | category | flops | bytes accessed | tf_op | source)
XLA Modules:
  0.0 283.5 jit_solution(17555680224212276584)
XLA Ops:
  0.0 2.8 %constant_dynamic-slice_fusion = bf16[256,3584]{1,0:T(8,128)(2,1)} fusion(bf16[256,14336]{1,0:T(8,128)(2,1)} %refs_1_.1, s32[]{:T(128)S(6)} %select_n.30), kind=kLoop, calls=%fused_computation.21 | loop fusion | bytes 3670020 | tf_op jit(solution)/shard_map/dynamic_slice | solution.py:102
  2.8 3.0 %collective-permute-start.3 = (bf16[256,3584]{1,0:T(8,128)(2,1)}, bf16[256,3584]{1,0:T(8,128)(2,1)}, u32[]{:S(2)}, u32[]{:S(2)}) collective-permute-start(bf16[256,3584]{1,0:T(8,128)(2,1)} %constant_dynamic-slice_fusion), channel_id=1, source_target_pairs={{0,8},{4,12},{8,0},{12,4},{16,24},{20,28},{24,16},{28,20},{1,9},{5... | collective-permute-start | bytes 5505032 | tf_op jit(solution)/shard_map/ppermute | solution.py:118
  5.9 2.0 collective-permute-start.12
  7.8 7.1 %dynamic-slice_bitcast_fusion = (bf16[336,3584]{1,0:T(8,128)(2,1)}, bf16[336,3584]{1,0:T(8,128)(2,1)}, bf16[336,3584]{1,0:T(8,128)(2,1)}, bf16[336,3584]{1,0:T(8,128)(2,1)S(1)}) fusion(bf16[14336,1,1,336]{0,3,2,1:T(8,128)(2,1)} %param.4, s32[]{:T(128)S(6)} %select_n.33, s32[]{:T(128)S(6)} %select_n.31, s32[]{:T(128)S(6)} %select_n.30, s32[]{:T(128)S(6)} %select_n.32), kind=kLoop, calls=%fused_computation | loop fusion | bytes 19267600 | tf_op jit(solution)/shard_map/dynamic_slice | solution.py:122
  15.0 1.5 collective-permute-start.5
  16.5 29.7 %collective-permute-done.3.refs_2_ = bf16[256,3584]{1,0:T(8,128)(2,1)} collective-permute-done((bf16[256,3584]{1,0:T(8,128)(2,1)}, bf16[256,3584]{1,0:T(8,128)(2,1)}, u32[]{:S(2)}, u32[]{:S(2)}) %collective-permute-start.3) | collective-permute-done | bytes 1835040 | tf_op jit(solution)/shard_map/ppermute | solution.py:118
  46.2 1.9 collective-permute-start.11
  48.1 1.3 collective-permute-start.13
  49.4 0.1 collective-permute-start
  49.5 2.7 collective-permute-start.6
  52.2 68.2 %collective-permute-done.5.refs_0_.refs_1_ = bf16[336,3584]{1,0:T(8,128)(2,1)S(1)} collective-permute-done((bf16[336,3584]{1,0:T(8,128)(2,1)S(1)}, bf16[336,3584]{1,0:T(8,128)(2,1)S(1)}, u32[]{:S(2)}, u32[]{:S(2)}) %collective-permute-start.5) | collective-permute-done | bytes 2408480 | tf_op jit(solution)/shard_map/ppermute | solution.py:97
  120.3 0.0 collective-permute-start.4
  120.4 0.0 collective-permute-done.11
  120.4 1.3 collective-permute-start.19
  121.7 1.6 collective-permute-start.2
  123.2 1.7 broadcast_select_fusion.1.refs_2_
  124.9 0.0 collective-permute-done.6.refs_1_
  124.9 0.3 collective-permute-start.14
  125.2 0.0 collective-permute-done.4.refs_3_
  125.2 7.3 %shard_map.39 = bf16[2,336,512]{2,1,0:T(8,128)(2,1)} custom-call(bf16[336,3584]{1,0:T(8,128)(2,1)} %copy-done, bf16[336,3584]{1,0:T(8,128)(2,1)} %collective-permute-done.6.refs_1_, bf16[256,3584]{1,0:T(8,128)(2,1)} %collective-permute-done.3.refs_2_, bf16[256,3584]{1,0:T(8,128)(2,1)} %collective-permute-done.4.refs_3_), custom_call_target="tpu_custom_call" | custom-call | flops 2466250752 | bytes 9175040 | tf_op jit(solution)/shard_map/pallas_call | solution.py:43
  132.6 1.5 collective-permute-start.7
  134.1 31.4 %collective-permute-done.19 = bf16[256,3584]{1,0:T(8,128)(2,1)} collective-permute-done((bf16[256,3584]{1,0:T(8,128)(2,1)}, bf16[256,3584]{1,0:T(8,128)(2,1)}, u32[]{:S(2)}, u32[]{:S(2)}) %collective-permute-start.19) | collective-permute-done | bytes 1835040 | tf_op jit(solution)/shard_map/ppermute | solution.py:118
  165.5 1.7 broadcast_select_fusion.refs_2_
  167.2 0.1 collective-permute-start.20
  167.2 9.5 %collective-permute-done.2.refs_1_.refs_0_ = bf16[336,3584]{1,0:T(8,128)(2,1)} collective-permute-done((bf16[336,3584]{1,0:T(8,128)(2,1)}, bf16[336,3584]{1,0:T(8,128)(2,1)}, u32[]{:S(2)}, u32[]{:S(2)}) %collective-permute-start.2) | collective-permute-done | bytes 2408480 | tf_op jit(solution)/shard_map/ppermute | solution.py:97
  176.7 7.2 %shard_map.38 = f32[2,336,512]{2,1,0:T(8,128)} custom-call(bf16[336,3584]{1,0:T(8,128)(2,1)} %get-tuple-element.7.refs_0_, bf16[336,3584]{1,0:T(8,128)(2,1)} %collective-permute-done.2.refs_1_.refs_0_, bf16[256,3584]{1,0:T(8,128)(2,1)} %collective-permute-done.3.refs_2_, bf16[256,3584]{1,0:T(8,128)(2,1)} %collective-permute-done.4.refs_3_), custom_call_target="tpu_custom_call" | custom-call | flops 2466250752 | bytes 9175040 | tf_op jit(solution)/shard_map/pallas_call | solution.py:43
  184.0 1.6 convert_add_fusion.2
  185.5 0.0 copy-start.5
  185.6 1.0 copy-done.5
  186.6 1.5 collective-permute-start.8
  188.1 1.3 copy-done.4
  189.4 7.1 %shard_map.41 = bf16[2,336,512]{2,1,0:T(8,128)(2,1)} custom-call(bf16[336,3584]{1,0:T(8,128)(2,1)} %collective-permute-done.2.refs_1_.refs_0_, bf16[336,3584]{1,0:T(8,128)(2,1)} %collective-permute-done.6.refs_1_, bf16[256,3584]{1,0:T(8,128)(2,1)} %copy-done.2, bf16[256,3584]{1,0:T(8,128)(2,1)} %copy-done.4), custom_call_target="tpu_custom_call" | custom-call | flops 2466250752 | bytes 9175040 | tf_op jit(solution)/shard_map/pallas_call | solution.py:43
  196.5 0.5 collective-permute-start.15
  197.0 0.0 collective-permute-done.8
  197.0 0.1 fusion.3
  197.1 7.2 %shard_map.40 = f32[2,336,512]{2,1,0:T(8,128)} custom-call(bf16[336,3584]{1,0:T(8,128)(2,1)} %get-tuple-element.7.refs_0_, bf16[336,3584]{1,0:T(8,128)(2,1)} %copy-done, bf16[256,3584]{1,0:T(8,128)(2,1)} %copy-done.2, bf16[256,3584]{1,0:T(8,128)(2,1)} %copy-done.4), custom_call_target="tpu_custom_call" | custom-call | flops 2466250752 | bytes 9175040 | tf_op jit(solution)/shard_map/pallas_call | solution.py:43
  204.4 9.1 %collective-permute-done.15 = bf16[2,336,512]{2,1,0:T(8,128)(2,1)S(1)} collective-permute-done((bf16[2,336,512]{2,1,0:T(8,128)(2,1)}, bf16[2,336,512]{2,1,0:T(8,128)(2,1)S(1)}, u32[]{:S(2)}, u32[]{:S(2)}) %collective-permute-start.15) | collective-permute-done | bytes 688160 | tf_op jit(solution)/shard_map/ppermute | solution.py:97
  213.5 1.6 convert_add_fusion.1
  215.1 1.6 collective-permute-start.16
  216.7 4.1 %collective-permute-start.9 = (bf16[336,256]{1,0:T(8,128)(2,1)S(1)}, bf16[336,256]{1,0:T(8,128)(2,1)S(1)}, u32[]{:S(2)}, u32[]{:S(2)}) collective-permute-start(bf16[336,256]{1,0:T(8,128)(2,1)S(1)} %get-tuple-element.14), channel_id=1, source_target_pairs={{0,8},{4,12},{8,0},{12,4},{16,24},{20,28},{24,16},{28,20},{1,9},{5... | collective-permute-start | bytes 516104 | tf_op jit(solution)/shard_map/ppermute | solution.py:100
  220.8 0.0 collective-permute-start.10
  220.8 0.0 collective-permute-done.20.refs_3_
  220.8 1.3 copy-done.3
  222.1 7.0 %shard_map.43 = bf16[2,336,512]{2,1,0:T(8,128)(2,1)} custom-call(bf16[336,3584]{1,0:T(8,128)(2,1)} %copy-done, bf16[336,3584]{1,0:T(8,128)(2,1)} %collective-permute-done.6.refs_1_, bf16[256,3584]{1,0:T(8,128)(2,1)} %copy-done.1, bf16[256,3584]{1,0:T(8,128)(2,1)} %copy-done.3), custom_call_target="tpu_custom_call" | custom-call | flops 2466250752 | bytes 9175040 | tf_op jit(solution)/shard_map/pallas_call | solution.py:43
  229.0 0.5 collective-permute-start.21
  229.5 0.1 fusion.4
  229.7 0.4 collective-permute-start.17
  230.1 7.2 %shard_map.42 = f32[2,336,512]{2,1,0:T(8,128)} custom-call(bf16[336,3584]{1,0:T(8,128)(2,1)} %get-tuple-element.7.refs_0_, bf16[336,3584]{1,0:T(8,128)(2,1)} %collective-permute-done.2.refs_1_.refs_0_, bf16[256,3584]{1,0:T(8,128)(2,1)} %copy-done.1, bf16[256,3584]{1,0:T(8,128)(2,1)} %copy-done.3), custom_call_target="tpu_custom_call" | custom-call | flops 2466250752 | bytes 9175040 | tf_op jit(solution)/shard_map/pallas_call | solution.py:43
  237.3 9.5 %collective-permute-done.21 = bf16[2,336,512]{2,1,0:T(8,128)(2,1)S(1)} collective-permute-done((bf16[2,336,512]{2,1,0:T(8,128)(2,1)}, bf16[2,336,512]{2,1,0:T(8,128)(2,1)S(1)}, u32[]{:S(2)}, u32[]{:S(2)}) %collective-permute-start.21) | collective-permute-done | bytes 688160 | tf_op jit(solution)/shard_map/ppermute | solution.py:97
  246.8 0.5 collective-permute-start.18
  247.3 1.6 convert_add_fusion
  248.9 0.6 collective-permute-start.22
  249.5 16.0 %shard_map.37 = bf16[1,336,512]{2,1,0:T(8,128)(2,1)} custom-call(bf16[336,14336]{1,0:T(8,128)(2,1)} %bitcast.26, bf16[256,14336]{1,0:T(8,128)(2,1)} %refs_1_.1, bf16[256,14336]{1,0:T(8,128)(2,1)} %collective-permute-done.refs_2_), custom_call_target="tpu_custom_call" | custom-call | flops 4932501504 | bytes 24657920 | tf_op jit(solution)/shard_map/pallas_call | solution.py:43
  265.5 1.7 fusion.9
  267.2 0.0 collective-permute-done.22
  267.2 0.0 collective-permute-start.1
  267.2 0.1 fusion.5
  267.4 2.2 collective-permute-start.23
  269.6 1.5 collective-permute-start.24
  271.1 0.6 broadcast_in_dim.3.refs_8_
  271.8 4.8 %collective-permute-done.23.refs_6_ = bf16[336,256]{1,0:T(8,128)(2,1)S(1)} collective-permute-done((bf16[336,256]{1,0:T(8,128)(2,1)S(1)}, bf16[336,256]{1,0:T(8,128)(2,1)S(1)}, u32[]{:S(2)}, u32[]{:S(2)}) %collective-permute-start.23) | collective-permute-done | bytes 172064 | tf_op jit(solution)/shard_map/ppermute | solution.py:100
  276.5 2.9 %collective-permute-done.24.refs_7_ = bf16[336,256]{1,0:T(8,128)(2,1)S(1)} collective-permute-done((bf16[336,256]{1,0:T(8,128)(2,1)S(1)}, bf16[336,256]{1,0:T(8,128)(2,1)S(1)}, u32[]{:S(2)}, u32[]{:S(2)}) %collective-permute-start.24) | collective-permute-done | bytes 172064 | tf_op jit(solution)/shard_map/ppermute | solution.py:100
  279.5 0.6 copy-done.13
  280.1 3.5 %shard_map.44 = bf16[256,2688]{1,0:T(8,128)(2,1)} custom-call(bf16[336,256]{1,0:T(8,128)(2,1)} %get-tuple-element.16.refs_0_, bf16[336,256]{1,0:T(8,128)(2,1)} %copy-done.11, bf16[336,256]{1,0:T(8,128)(2,1)} %copy-done.7, bf16[336,256]{1,0:T(8,128)(2,1)} %copy-done.8, bf16[336,256]{1,0:T(8,128)(2,1)} %copy-done.9, bf16[336,256]{1,0:T(8,128)(2,1)} %copy-done.10, ...), custom_call_target="tpu_custom_call" | custom-call | flops 688128 | bytes 2752512 | tf_op jit(solution)/shard_map/pallas_call | solution.py:75
  (42 shorter events, 0.3 us)
Async XLA Ops:
  2.8 43.3 %collective-permute-start.3 = (bf16[256,3584]{1,0:T(8,128)(2,1)}, bf16[256,3584]{1,0:T(8,128)(2,1)}, u32[]{:S(2)}, u32[]{:S(2)}) collective-permute-start(bf16[256,3584]{1,0:T(8,128)(2,1)} %constant_dynamic-slice_fusion), channel_id=1, source_target_pairs={{0,8},{4,12},{8,0},{12,4},{16,24},{20,28},{24,16},{28,20},{1,9},{5... | collective-permute-start | bytes 5505032 | tf_op jit(solution)/shard_map/ppermute | solution.py:118
  5.9 42.3 %collective-permute-start.12 = (bf16[256,3584]{1,0:T(8,128)(2,1)}, bf16[256,3584]{1,0:T(8,128)(2,1)}, u32[]{:S(2)}, u32[]{:S(2)}) collective-permute-start(bf16[256,3584]{1,0:T(8,128)(2,1)} %constant_dynamic-slice_fusion), channel_id=1, source_target_pairs={{8,16},{12,20},{16,8},{20,12},{9,17},{13,21},{17,9},{21,13},{10,18... | collective-permute-start | bytes 5505032 | tf_op jit(solution)/shard_map/ppermute | solution.py:118
  15.0 105.4 %collective-permute-start.5 = (bf16[336,3584]{1,0:T(8,128)(2,1)S(1)}, bf16[336,3584]{1,0:T(8,128)(2,1)S(1)}, u32[]{:S(2)}, u32[]{:S(2)}) collective-permute-start(bf16[336,3584]{1,0:T(8,128)(2,1)S(1)} %get-tuple-element.8), channel_id=1, source_target_pairs={{0,2},{1,3},{2,0},{3,1},{4,6},{5,7},{6,4},{7,5},{8,10},{9,11},{10,... | collective-permute-start | bytes 7225352 | tf_op jit(solution)/shard_map/ppermute | solution.py:97
  46.2 74.2 %collective-permute-start.11 = (bf16[256,3584]{1,0:T(8,128)(2,1)}, bf16[256,3584]{1,0:T(8,128)(2,1)}, u32[]{:S(2)}, u32[]{:S(2)}) collective-permute-start(bf16[256,3584]{1,0:T(8,128)(2,1)} %collective-permute-done.3.refs_2_), channel_id=1, source_target_pairs={{8,16},{12,20},{16,8},{20,12},{9,17},{13,21},{17,9},{21,13},{10,18... | collective-permute-start | bytes 5505032 | tf_op jit(solution)/shard_map/ppermute | solution.py:118
  48.1 73.5 %collective-permute-start.13 = (bf16[256,3584]{1,0:T(8,128)(2,1)}, bf16[256,3584]{1,0:T(8,128)(2,1)}, u32[]{:S(2)}, u32[]{:S(2)}) collective-permute-start(bf16[256,3584]{1,0:T(8,128)(2,1)} %collective-permute-done.12), channel_id=1, source_target_pairs={{8,0},{12,4},{16,24},{20,28},{9,1},{13,5},{17,25},{21,29},{10,2},{... | collective-permute-start | bytes 5505032 | tf_op jit(solution)/shard_map/ppermute | solution.py:118
  49.4 199.5 %collective-permute-start = (bf16[256,14336]{1,0:T(8,128)(2,1)}, bf16[256,14336]{1,0:T(8,128)(2,1)}, u32[]{:S(2)}, u32[]{:S(2)}) collective-permute-start(bf16[256,14336]{1,0:T(8,128)(2,1)} %refs_1_.1), channel_id=1, source_target_pairs={{0,4},{4,0},{8,12},{12,8},{16,20},{20,16},{24,28},{28,24},{1,5},{5... | collective-permute-start | bytes 22020104 | tf_op jit(solution)/shard_map/ppermute | solution.py:100
  49.5 75.4 %collective-permute-start.6 = (bf16[336,3584]{1,0:T(8,128)(2,1)}, bf16[336,3584]{1,0:T(8,128)(2,1)}, u32[]{:S(2)}, u32[]{:S(2)}) collective-permute-start(bf16[336,3584]{1,0:T(8,128)(2,1)} %get-tuple-element.5), channel_id=1, source_target_pairs={{0,3},{1,2},{2,1},{3,0},{4,7},{5,6},{6,5},{7,4},{8,11},{9,10},{10,... | collective-permute-start | bytes 7225352 | tf_op jit(solution)/shard_map/ppermute | solution.py:97
  120.3 4.6 %copy-start = (bf16[336,3584]{1,0:T(8,128)(2,1)}, bf16[336,3584]{1,0:T(8,128)(2,1)S(1)}, u32[]{:S(2)}) copy-start(bf16[336,3584]{1,0:T(8,128)(2,1)S(1)} %collective-permute-done.5.refs_0_.refs_1_) | copy-start | bytes 7225348
  120.3 4.9 %collective-permute-start.4 = (bf16[256,3584]{1,0:T(8,128)(2,1)}, bf16[256,3584]{1,0:T(8,128)(2,1)}, u32[]{:S(2)}, u32[]{:S(2)}) collective-permute-start(bf16[256,3584]{1,0:T(8,128)(2,1)} %collective-permute-done.3.refs_2_), channel_id=1, source_target_pairs={{0,4},{4,0},{8,12},{12,8},{16,20},{20,16},{24,28},{28,24},{1,5},{5... | collective-permute-start | bytes 5505032 | tf_op jit(solution)/shard_map/ppermute | solution.py:100
  120.4 45.1 %collective-permute-start.19 = (bf16[256,3584]{1,0:T(8,128)(2,1)}, bf16[256,3584]{1,0:T(8,128)(2,1)}, u32[]{:S(2)}, u32[]{:S(2)}) collective-permute-start(bf16[256,3584]{1,0:T(8,128)(2,1)} %collective-permute-done.11), channel_id=1, source_target_pairs={{8,0},{12,4},{16,24},{20,28},{9,1},{13,5},{17,25},{21,29},{10,2},{... | collective-permute-start | bytes 5505032 | tf_op jit(solution)/shard_map/ppermute | solution.py:118
  121.7 55.1 %collective-permute-start.2 = (bf16[336,3584]{1,0:T(8,128)(2,1)}, bf16[336,3584]{1,0:T(8,128)(2,1)}, u32[]{:S(2)}, u32[]{:S(2)}) collective-permute-start(bf16[336,3584]{1,0:T(8,128)(2,1)} %get-tuple-element.6), channel_id=1, source_target_pairs={{0,1},{1,0},{2,3},{3,2},{4,5},{5,4},{6,7},{7,6},{8,9},{9,8},{10,11... | collective-permute-start | bytes 7225352 | tf_op jit(solution)/shard_map/ppermute | solution.py:97
  124.9 7.6 %copy-start.2 = (bf16[256,3584]{1,0:T(8,128)(2,1)}, bf16[256,3584]{1,0:T(8,128)(2,1)S(1)}, u32[]{:S(2)}) copy-start(bf16[256,3584]{1,0:T(8,128)(2,1)S(1)} %broadcast_select_fusion.1.refs_2_) | copy-start | bytes 5505028
  124.9 63.2 %collective-permute-start.14 = (bf16[256,3584]{1,0:T(8,128)(2,1)S(1)}, bf16[256,3584]{1,0:T(8,128)(2,1)S(1)}, u32[]{:S(2)}, u32[]{:S(2)}) collective-permute-start(bf16[256,3584]{1,0:T(8,128)(2,1)S(1)} %broadcast_select_fusion.1.refs_2_), channel_id=1, source_target_pairs={{0,4},{4,0},{8,12},{12,8},{16,20},{20,16},{24,28},{28,24},{1,5},{5... | collective-permute-start | bytes 5505032 | tf_op jit(solution)/shard_map/ppermute | solution.py:100
  132.6 51.4 %collective-permute-start.7 = (bf16[2,336,512]{2,1,0:T(8,128)(2,1)}, bf16[2,336,512]{2,1,0:T(8,128)(2,1)S(1)}, u32[]{:S(2)}, u32[]{:S(2)}) collective-permute-start(bf16[2,336,512]{2,1,0:T(8,128)(2,1)} %shard_map.39), channel_id=1, source_target_pairs={{0,2},{1,3},{2,0},{3,1},{4,6},{5,7},{6,4},{7,5},{8,10},{9,11},{10,... | collective-permute-start | bytes 2064392 | tf_op jit(solution)/shard_map/ppermute | solution.py:97
  167.2 16.8 %copy-start.1 = (bf16[256,3584]{1,0:T(8,128)(2,1)}, bf16[256,3584]{1,0:T(8,128)(2,1)S(1)}, u32[]{:S(2)}) copy-start(bf16[256,3584]{1,0:T(8,128)(2,1)S(1)} %broadcast_select_fusion.refs_2_) | copy-start | bytes 5505028
  167.2 53.6 %collective-permute-start.20 = (bf16[256,3584]{1,0:T(8,128)(2,1)S(1)}, bf16[256,3584]{1,0:T(8,128)(2,1)S(1)}, u32[]{:S(2)}, u32[]{:S(2)}) collective-permute-start(bf16[256,3584]{1,0:T(8,128)(2,1)S(1)} %broadcast_select_fusion.refs_2_), channel_id=1, source_target_pairs={{0,4},{4,0},{8,12},{12,8},{16,20},{20,16},{24,28},{28,24},{1,5},{5... | collective-permute-start | bytes 5505032 | tf_op jit(solution)/shard_map/ppermute | solution.py:100
  185.5 1.1 copy-start.5
  186.6 10.4 %collective-permute-start.8 = (bf16[1,336,512]{2,1,0:T(8,128)(2,1)S(1)}, bf16[1,336,512]{2,1,0:T(8,128)(2,1)S(1)}, u32[]{:S(2)}, u32[]{:S(2)}) collective-permute-start(bf16[1,336,512]{2,1,0:T(8,128)(2,1)S(1)} %slice.93), channel_id=1, source_target_pairs={{0,1},{1,0},{2,3},{3,2},{4,5},{5,4},{6,7},{7,6},{8,9},{9,8},{10,11... | collective-permute-start | bytes 1032200 | tf_op jit(solution)/shard_map/ppermute | solution.py:97
  188.1 1.3 copy-start.4
  189.4 7.6 %copy-start.6 = (f32[2,336,512]{2,1,0:T(8,128)S(1)}, f32[2,336,512]{2,1,0:T(8,128)}, u32[]{:S(2)}) copy-start(f32[2,336,512]{2,1,0:T(8,128)} %copy-done.5) | copy-start | bytes 4128772
  196.5 17.0 %collective-permute-start.15 = (bf16[2,336,512]{2,1,0:T(8,128)(2,1)}, bf16[2,336,512]{2,1,0:T(8,128)(2,1)S(1)}, u32[]{:S(2)}, u32[]{:S(2)}) collective-permute-start(bf16[2,336,512]{2,1,0:T(8,128)(2,1)} %shard_map.41), channel_id=1, source_target_pairs={{0,1},{1,0},{2,3},{3,2},{4,5},{5,4},{6,7},{7,6},{8,9},{9,8},{10,11... | collective-permute-start | bytes 2064392 | tf_op jit(solution)/shard_map/ppermute | solution.py:97
  215.1 14.5 %collective-permute-start.16 = (bf16[1,336,512]{2,1,0:T(8,128)(2,1)S(1)}, bf16[1,336,512]{2,1,0:T(8,128)(2,1)S(1)}, u32[]{:S(2)}, u32[]{:S(2)}) collective-permute-start(bf16[1,336,512]{2,1,0:T(8,128)(2,1)S(1)} %slice.92), channel_id=1, source_target_pairs={{0,2},{1,3},{2,0},{3,1},{4,6},{5,7},{6,4},{7,5},{8,10},{9,11},{10,... | collective-permute-start | bytes 1032200 | tf_op jit(solution)/shard_map/ppermute | solution.py:97
  216.7 50.7 %collective-permute-start.9 = (bf16[336,256]{1,0:T(8,128)(2,1)S(1)}, bf16[336,256]{1,0:T(8,128)(2,1)S(1)}, u32[]{:S(2)}, u32[]{:S(2)}) collective-permute-start(bf16[336,256]{1,0:T(8,128)(2,1)S(1)} %get-tuple-element.14), channel_id=1, source_target_pairs={{0,8},{4,12},{8,0},{12,4},{16,24},{20,28},{24,16},{28,20},{1,9},{5... | collective-permute-start | bytes 516104 | tf_op jit(solution)/shard_map/ppermute | solution.py:100
  220.8 48.8 %collective-permute-start.10 = (bf16[336,256]{1,0:T(8,128)(2,1)S(1)}, bf16[336,256]{1,0:T(8,128)(2,1)S(1)}, u32[]{:S(2)}, u32[]{:S(2)}) collective-permute-start(bf16[336,256]{1,0:T(8,128)(2,1)S(1)} %get-tuple-element.13), channel_id=1, source_target_pairs={{0,12},{4,8},{8,4},{12,0},{16,28},{20,24},{24,20},{28,16},{1,13},{... | collective-permute-start | bytes 516104 | tf_op jit(solution)/shard_map/ppermute | solution.py:100
  220.8 1.3 copy-start.3
  229.0 17.7 %collective-permute-start.21 = (bf16[2,336,512]{2,1,0:T(8,128)(2,1)}, bf16[2,336,512]{2,1,0:T(8,128)(2,1)S(1)}, u32[]{:S(2)}, u32[]{:S(2)}) collective-permute-start(bf16[2,336,512]{2,1,0:T(8,128)(2,1)} %shard_map.43), channel_id=1, source_target_pairs={{0,2},{1,3},{2,0},{3,1},{4,6},{5,7},{6,4},{7,5},{8,10},{9,11},{10,... | collective-permute-start | bytes 2064392 | tf_op jit(solution)/shard_map/ppermute | solution.py:97
  229.7 42.0 %collective-permute-start.17 = (bf16[336,256]{1,0:T(8,128)(2,1)S(1)}, bf16[336,256]{1,0:T(8,128)(2,1)S(1)}, u32[]{:S(2)}, u32[]{:S(2)}) collective-permute-start(bf16[336,256]{1,0:T(8,128)(2,1)S(1)} %get-tuple-element.12), channel_id=1, source_target_pairs={{0,16},{4,20},{8,24},{12,28},{16,0},{20,4},{24,8},{28,12},{1,17},{... | collective-permute-start | bytes 516104 | tf_op jit(solution)/shard_map/ppermute | solution.py:100
  246.8 24.9 %collective-permute-start.18 = (bf16[336,256]{1,0:T(8,128)(2,1)S(1)}, bf16[336,256]{1,0:T(8,128)(2,1)S(1)}, u32[]{:S(2)}, u32[]{:S(2)}) collective-permute-start(bf16[336,256]{1,0:T(8,128)(2,1)S(1)} %get-tuple-element.11), channel_id=1, source_target_pairs={{0,20},{4,16},{8,28},{12,24},{16,4},{20,0},{24,12},{28,8},{1,21},{... | collective-permute-start | bytes 516104 | tf_op jit(solution)/shard_map/ppermute | solution.py:100
  248.9 18.3 %collective-permute-start.22 = (bf16[1,336,512]{2,1,0:T(8,128)(2,1)S(1)}, bf16[1,336,512]{2,1,0:T(8,128)(2,1)S(1)}, u32[]{:S(2)}, u32[]{:S(2)}) collective-permute-start(bf16[1,336,512]{2,1,0:T(8,128)(2,1)S(1)} %slice.91), channel_id=1, source_target_pairs={{0,1},{1,0},{2,3},{3,2},{4,5},{5,4},{6,7},{7,6},{8,9},{9,8},{10,11... | collective-permute-start | bytes 1032200 | tf_op jit(solution)/shard_map/ppermute | solution.py:97
  265.5 5.6 %copy-start.14 = (f32[2688]{0:T(1024)S(1)}, f32[2688]{0:T(1024)}, u32[]{:S(2)}) copy-start(f32[2688]{0:T(1024)} %param.5) | copy-start | bytes 32260
  267.2 4.5 %collective-permute-start.1 = (bf16[336,256]{1,0:T(8,128)(2,1)S(1)}, bf16[336,256]{1,0:T(8,128)(2,1)S(1)}, u32[]{:S(2)}, u32[]{:S(2)}) collective-permute-start(bf16[336,256]{1,0:T(8,128)(2,1)S(1)} %get-tuple-element.15), channel_id=1, source_target_pairs={{0,4},{4,0},{8,12},{12,8},{16,20},{20,16},{24,28},{28,24},{1,5},{5... | collective-permute-start | bytes 516104 | tf_op jit(solution)/shard_map/ppermute | solution.py:100
  267.4 12.1 %copy-start.7 = (bf16[336,256]{1,0:T(8,128)(2,1)}, bf16[336,256]{1,0:T(8,128)(2,1)S(1)}, u32[]{:S(2)}) copy-start(bf16[336,256]{1,0:T(8,128)(2,1)S(1)} %collective-permute-done.9.refs_2_) | copy-start | bytes 516100
  267.4 9.1 %collective-permute-start.23 = (bf16[336,256]{1,0:T(8,128)(2,1)S(1)}, bf16[336,256]{1,0:T(8,128)(2,1)S(1)}, u32[]{:S(2)}, u32[]{:S(2)}) collective-permute-start(bf16[336,256]{1,0:T(8,128)(2,1)S(1)} %get-tuple-element.10), channel_id=1, source_target_pairs={{0,24},{4,28},{8,16},{12,20},{16,8},{20,12},{24,0},{28,4},{1,25},{... | collective-permute-start | bytes 516104 | tf_op jit(solution)/shard_map/ppermute | solution.py:100
  269.6 9.8 %copy-start.8 = (bf16[336,256]{1,0:T(8,128)(2,1)}, bf16[336,256]{1,0:T(8,128)(2,1)S(1)}, u32[]{:S(2)}) copy-start(bf16[336,256]{1,0:T(8,128)(2,1)S(1)} %collective-permute-done.10.refs_3_) | copy-start | bytes 516100
  269.6 9.8 %collective-permute-start.24 = (bf16[336,256]{1,0:T(8,128)(2,1)S(1)}, bf16[336,256]{1,0:T(8,128)(2,1)S(1)}, u32[]{:S(2)}, u32[]{:S(2)}) collective-permute-start(bf16[336,256]{1,0:T(8,128)(2,1)S(1)} %get-tuple-element.9), channel_id=1, source_target_pairs={{0,28},{4,24},{8,20},{12,16},{16,12},{20,8},{24,4},{28,0},{1,29},{... | collective-permute-start | bytes 516104 | tf_op jit(solution)/shard_map/ppermute | solution.py:100
  271.7 7.7 %copy-start.9 = (bf16[336,256]{1,0:T(8,128)(2,1)}, bf16[336,256]{1,0:T(8,128)(2,1)S(1)}, u32[]{:S(2)}) copy-start(bf16[336,256]{1,0:T(8,128)(2,1)S(1)} %collective-permute-done.17.refs_4_) | copy-start | bytes 516100
  271.7 7.7 %copy-start.10 = (bf16[336,256]{1,0:T(8,128)(2,1)}, bf16[336,256]{1,0:T(8,128)(2,1)S(1)}, u32[]{:S(2)}) copy-start(bf16[336,256]{1,0:T(8,128)(2,1)S(1)} %collective-permute-done.18.refs_5_) | copy-start | bytes 516100
  271.7 7.7 %copy-start.11 = (bf16[336,256]{1,0:T(8,128)(2,1)}, bf16[336,256]{1,0:T(8,128)(2,1)S(1)}, u32[]{:S(2)}) copy-start(bf16[336,256]{1,0:T(8,128)(2,1)S(1)} %collective-permute-done.1.refs_1_) | copy-start | bytes 516100
  276.5 2.9 %copy-start.12 = (bf16[336,256]{1,0:T(8,128)(2,1)}, bf16[336,256]{1,0:T(8,128)(2,1)S(1)}, u32[]{:S(2)}) copy-start(bf16[336,256]{1,0:T(8,128)(2,1)S(1)} %collective-permute-done.23.refs_6_) | copy-start | bytes 516100
  279.4 0.7 copy-start.13

commit v2 on v0

v2 whole, which is shorter than its diff:
```python
import functools

import jax
import jax.numpy as jnp
from jax import lax
from jax.experimental import pallas as pl
from jax.experimental.pallas import tpu as pltpu
from jax.sharding import PartitionSpec as P

ROOM = 14 * 1024 * 1024
SPACE = 0
GATE = 0
GATE2 = 0
IN_VMEM = pl.BlockSpec(memory_space=pltpu.VMEM)
IN_HBM = pl.BlockSpec(memory_space=pltpu.HBM)
ANYWHERE = pl.BlockSpec(memory_space=pl.ANY)
BOTH_LAST = (((1,), (1,)), ((), ()))


def divisor(size, most):
    return max(d for d in range(128, most + 1, 128) if size % d == 0)


def bands_kernel(pieces, band, x, *refs):
    outs, sems = refs[-1 - len(pieces) : -1], refs[-1]
    col = lax.axis_index("col")
    copies = []
    for i, (j, first, rows) in enumerate(pieces):
        start = pl.multiple_of((col ^ j) * band, 128)
        copies.append(pltpu.make_async_copy(x.at[pl.ds(first, rows), pl.ds(start, band)], outs[i], sems.at[i]))
    for copy in copies:
        copy.start()
    for copy in copies:
        copy.wait()


def bands(x, pieces, n_col, after):
    band = x.shape[1] // n_col
    return pl.pallas_call(
        functools.partial(bands_kernel, pieces, band),
        out_shape=[jax.ShapeDtypeStruct((rows, band), x.dtype) for _, _, rows in pieces],
        in_specs=[IN_HBM] + [ANYWHERE] * len(after),
        out_specs=[IN_VMEM] * len(pieces),
        scratch_shapes=[pltpu.SemaphoreType.DMA((len(pieces),))],
        compiler_params=pltpu.CompilerParams(vmem_limit_bytes=ROOM),
    )(pltpu.with_memory_space_constraint(x, pltpu.HBM), *after)


def choose_kernel(wanted, n, *refs):
    x_refs, outs, sem = refs[:n], refs[n:-1], refs[-1]
    plane = lax.axis_index("row") // 2
    for i, x in enumerate(x_refs):
        here = functools.reduce(jnp.logical_or, [plane == p for p, w in enumerate(wanted) if w == i])

        @pl.when(here)
        def _():
            first, copies = 0, []
            for k, out in enumerate(outs):
                width = out.shape[1]
                copies.append(pltpu.make_async_copy(x.at[:, pl.ds(first, width)], out, sem.at[k]))
                first += width
            for copy in copies:
                copy.start()
            for copy in copies:
                copy.wait()


def choose(xs, wanted, after, cuts):
    rows, width = xs[0].shape
    return pl.pallas_call(
        lambda *refs: choose_kernel(wanted, len(xs), *refs[: len(xs)], *refs[len(xs) + len(after) :]),
        out_shape=[jax.ShapeDtypeStruct((rows, width // cuts), xs[0].dtype)] * cuts,
        in_specs=[ANYWHERE] * (len(xs) + len(after)),
        out_specs=[IN_VMEM] * cuts,
        scratch_shapes=[pltpu.SemaphoreType.DMA((cuts,))],
        compiler_params=pltpu.CompilerParams(vmem_limit_bytes=ROOM),
    )(*xs, *after)


def pass_kernel(*refs):
    pass


def passed(xs, after, flops):
    return pl.pallas_call(
        pass_kernel,
        out_shape=[jax.ShapeDtypeStruct(x.shape, x.dtype) for x in xs],
        in_specs=[ANYWHERE] * (len(xs) + len(after)),
        out_specs=[ANYWHERE] * len(xs),
        input_output_aliases={i: i for i in range(len(xs))},
        compiler_params=pltpu.CompilerParams(vmem_limit_bytes=ROOM),
        cost_estimate=pl.CostEstimate(flops=flops, bytes_accessed=0, transcendentals=0),
    )(*xs, *after)


def gate_kernel(*refs):
    refs[-1][...] = jnp.zeros_like(refs[-1])


def gate(after, flops):
    return pl.pallas_call(
        gate_kernel,
        out_shape=jax.ShapeDtypeStruct((8, 128), jnp.float32),
        in_specs=[ANYWHERE] * len(after),
        out_specs=IN_VMEM,
        compiler_params=pltpu.CompilerParams(vmem_limit_bytes=ROOM),
        cost_estimate=pl.CostEstimate(flops=flops, bytes_accessed=0, transcendentals=0),
    )(*after)


def deep_kernel(w, t0, t1, out_ref, total):
    step = pl.program_id(0)

    @pl.when(step == 0)
    def _():
        total[...] = jnp.zeros_like(total)

    rows = t0.shape[0]
    for k, t in enumerate((t0, t1)):
        total[:, k * rows : (k + 1) * rows] += lax.dot_general(
            w[...], t[...], BOTH_LAST, preferred_element_type=jnp.float32
        )

    @pl.when(step == pl.num_programs(0) - 1)
    def _():
        out_ref[...] = total[...].astype(out_ref.dtype)


def deep_product(w, t0, t1):
    m, depth = w.shape
    rows = t0.shape[0]
    block = divisor(depth, 3584)
    return pl.pallas_call(
        deep_kernel,
        grid=(depth // block,),
        in_specs=[pl.BlockSpec((m, block), lambda i: (0, i))] + [pl.BlockSpec((rows, block), lambda i: (0, i))] * 2,
        out_specs=pl.BlockSpec((m, 2 * rows), lambda i: (0, 0)),
        out_shape=jax.ShapeDtypeStruct((m, 2 * rows), jnp.bfloat16),
        scratch_shapes=[pltpu.VMEM((m, 2 * rows), jnp.float32)],
        compiler_params=pltpu.CompilerParams(vmem_limit_bytes=ROOM),
        cost_estimate=pl.CostEstimate(
            flops=4 * m * rows * depth, bytes_accessed=2 * depth * (m + 2 * rows), transcendentals=0
        ),
    )(*[pltpu.with_memory_space_constraint(x, pltpu.HBM) for x in (w, t0)], t1)


def product_kernel(n_w, n_t, cuts, first, rows, *refs):
    out_ref = refs[-1]
    for i, w in enumerate(refs[:n_w]):
        for k in range(n_t):
            total, start = 0.0, 0
            for t in refs[n_w + k * cuts : n_w + (k + 1) * cuts]:
                stop = start + t.shape[1]
                total += lax.dot_general(
                    w[:, start:stop], t[first : first + rows, :], BOTH_LAST, preferred_element_type=jnp.float32
                )
                start = stop
            out_ref[i, :, k * rows : (k + 1) * rows] = total.astype(out_ref.dtype)


def products(ws, ts, first, rows, dtype, after):
    m = ws[0].shape[0]
    shape = (len(ws), m, rows * len(ts))
    flat = [piece for t in ts for piece in t]
    return pl.pallas_call(
        functools.partial(product_kernel, len(ws), len(ts), len(ts[0]), first, rows),
        in_specs=[IN_VMEM] * (len(ws) + len(flat)) + [ANYWHERE] * len(after),
        out_specs=IN_VMEM,
        out_shape=jax.ShapeDtypeStruct(shape, dtype),
        compiler_params=pltpu.CompilerParams(vmem_limit_bytes=ROOM),
        cost_estimate=pl.CostEstimate(
            flops=len(ws) * m * rows, bytes_accessed=len(ws) * m * rows, transcendentals=0
        ),
    )(*ws, *flat, *after)


def join_kernel(places, *refs):
    n = len(places)
    part_refs, bias_ref, out_ref, joined = refs[:n], refs[n], refs[n + 1], refs[n + 2]
    me = lax.axis_index("row")
    for (j, token), part in zip(places, part_refs):
        m, rows = part.shape
        joined[pl.ds(pl.multiple_of((me ^ j) * m, 8), m), token : token + rows] = part[...].astype(jnp.float32)
    block = divisor(out_ref.shape[1], 512)
    for i in range(out_ref.shape[1] // block):
        cols = slice(i * block, (i + 1) * block)
        out_ref[:, cols] = (joined[cols, :].T + bias_ref[:, cols]).astype(out_ref.dtype)


def join(parts, rows, bias):
    width = bias.shape[0]
    return pl.pallas_call(
        functools.partial(join_kernel, [(j, token) for j, token, _ in parts]),
        out_shape=jax.ShapeDtypeStruct((rows, width), jnp.bfloat16),
        in_specs=[IN_VMEM] * (len(parts) + 1),
        out_specs=IN_VMEM,
        scratch_shapes=[pltpu.VMEM((width, rows), jnp.float32)],
        compiler_params=pltpu.CompilerParams(vmem_limit_bytes=ROOM),
        cost_estimate=pl.CostEstimate(flops=width * rows, bytes_accessed=4 * width * rows, transcendentals=0),
    )(*[part for _, _, part in parts], bias[None, :])


def shards(tokens, qkv_weight, qkv_bias):
    n_row, n_col = lax.axis_size("row"), lax.axis_size("col")
    planes = n_row // 2
    half, feats = tokens.shape
    weight = qkv_weight.reshape(feats, -1).T
    columns = weight.shape[0]

    def flip_col(x, j):
        return lax.ppermute(x, "col", [(i, i ^ j) for i in range(n_col)])

    def flip_row(x, j):
        return lax.ppermute(x, "row", [(i, i ^ j) for i in range(n_row)])

    (own,) = bands(tokens, [(0, 0, half)], n_col, [])
    js = list(range(n_col))
    (far,) = bands(weight, [(n_col - 1, 0, columns)], n_col, [own])
    near = bands(weight, [(j, 0, columns) for j in js[:-1]], n_col, [far])
    w_band = [near[0]] + [flip_col(x, j) for j, x in zip(js[1:], list(near[1:]) + [far])]
    here = deep_product(weight, tokens, flip_row(tokens, 1))
    here_other = flip_row(here[:, half:], 1)
    parts = [(0, 0, here[:, :half]), (1, 0, here_other)]

    held = []
    last = {0: own, 1: own}
    second = []
    for s in range(1, planes):
        if s == 2:
            last = dict(enumerate(passed([last[0], last[1]], [here_other, near[0]], SPACE)))
            held = [(last[i], came) for i, (_, came) in enumerate(held)]
        now = {}
        for parity in (0, 1):
            pairs, came = [], {}
            for p in range(parity, planes - 1, 2):
                if p - s + 1 >= 0:
                    pairs.append((p, p + 1))
                    came[p + 1] = p - s + 1
                if p + s < planes:
                    pairs.append((p + 1, p))
                    came[p] = p + s
            if pairs:
                now[parity] = lax.ppermute(
                    last[1 - parity], "row", [(2 * a + c, 2 * b + c) for a, b in pairs for c in (0, 1)]
                )
                held.append((now[parity], came))
                if s == 2:
                    second.append(now[parity])
        last = now

    def arrived(d, after, cuts):
        wanted = [next(i for i, (_, came) in enumerate(held) if came.get(p) == p ^ d) for p in range(planes)]
        used = sorted(set(wanted))
        value = list(choose([held[i][0] for i in used], [used.index(i) for i in wanted], after, cuts))
        return [value, [flip_row(x, 1) for x in value]]

    bits = [1 << b for b in range(n_col.bit_length() - 1)]
    groups = [[(d, 0, half) for d in range(1, planes - 1)], [(planes - 1, at, half // 2) for at in (0, half // 2)]]
    moved = w_band[1:]
    blocks = [None] + [arrived(d, second + moved, 2) for d in range(1, planes - 1)]
    after = [gate(moved + blocks[1][0] + blocks[1][1], GATE)]
    n_slot = 0
    came_back = []
    for n_group, group in enumerate(groups):
        if n_group:
            blocks.append(arrived(planes - 1, after + came_back, 1))
            after = [gate(blocks[planes - 1][1] + after, GATE2)]
        work = []
        for d, token, rows in group:
            turned = n_slot % len(bits)
            n_slot += 1
            order = bits[turned:] + bits[:turned]
            out = [j for j in js if j & order[0]]
            kept = [j for j in js if not j & order[0]]
            sent = products([w_band[j] for j in out], blocks[d], token, rows, jnp.bfloat16, after)
            after = [sent]
            came_back.append(flip_col(sent, order[0]))
            work.append([d, token, rows, order, kept, came_back[-1]])
        for item in work:
            d, token, rows, order, kept, got = item
            mine = products([w_band[j] for j in kept], blocks[d], token, rows, jnp.float32, after)
            after = [mine]
            item.append(mine)
        for d, token, rows, order, kept, got, mine in work:
            for n, bit in enumerate(order):
                if n:
                    got = flip_col(sent, bit)
                mine = mine + got.astype(jnp.float32)
                if n + 1 < len(order):
                    nxt = order[n + 1]
                    go = [i for i, j in enumerate(kept) if j & nxt]
                    stay = [i for i, j in enumerate(kept) if not j & nxt]
                    sent = jnp.stack([mine[i] for i in go]).astype(jnp.bfloat16)
                    mine = jnp.stack([mine[i] for i in stay])
                    kept = [kept[i] for i in stay]
            done = mine[0].astype(jnp.bfloat16)
            parts.append((2 * d, token, flip_row(done[:, :rows], 2 * d)))
            parts.append((2 * d + 1, token, flip_row(done[:, rows:], 2 * d + 1)))
    return join(parts, half, qkv_bias)


def solution(mesh):
    return jax.shard_map(
        shards,
        mesh=mesh,
        in_specs=(P("row", None), P(None, "col", "row", None), P("col")),
        out_specs=P("row", "col"),
        check_vma=False,
    )
```

time: 436 us -> 203 us (0.47)
  waiting for transfers between devices: 346 us -> 123 us
  Pallas kernels: 0 us -> 39.4 us
  local copies, waits for them, and re-layouts: 34.2 us -> 0.24 us
  matrix products: 27.7 us -> 0 us
  starting transfers between devices: 11.5 us -> 36.5 us
  between operations: 13.4 us -> 0.35 us
    all_to_all x2 -> x0, waiting for transfers between devices: 151 us -> none  [the longest x1 128 us: shards(): lax.all_to_all(local_w, 'row', split_axis=0, concat_axis=1, tiled=True)]
    ppermute x0 -> x31, waiting for transfers between devices: none -> 123 us  [the longest x11 92.7 us: flip_col(): return lax.ppermute(x, 'col', [(i, i ^ j) for i in range(n_col)])]
    reduce_scatter x1 -> x0, waiting for transfers between devices: 113 us -> none  [shards(): lax.psum_scatter(jnp.dot(act_panel, w_tile, preferred_element_type=jnp.fl...]
    all_gather x1 -> x0, waiting for transfers between devices: 81.3 us -> none  [shards(): act_panel = lax.all_gather(slivers, 'col', axis=1, tiled=True)]
    pallas_call x0 -> x19, Pallas kernels: none -> 39.4 us  [the longest x8 21.2 us: products(): pl.pallas_call(functools.partial(product_kernel, len(ws), len(ts), len(ts...]
    ppermute x0 -> x31, starting transfers between devices: none -> 36.5 us  [the longest x15 14.9 us: flip_row(): return lax.ppermute(x, 'row', [(i, i ^ j) for i in range(n_row)])]
    dot_general x1 -> x0, matrix products: 27.7 us -> none  [shards(): jnp.dot(act_panel, w_tile, preferred_element_type=jnp.float32)]
    unnamed x4 -> x2, local copies, waits for them, and re-layouts: 20.5 us -> 0.01 us
  transfers between devices with their start and end apart: 4 -> 31, of which waited for: 4 -> 15; matrix products, arithmetic and copies ran while one was open for 5% -> 1% of each run, Pallas kernels for 0% -> 19%
where the time goes in v2:
time: 203 us; the launch traced here: 200 us
  waiting for transfers between devices  123 us (61%)
  Pallas kernels  39.4 us (19%)
  starting transfers between devices  36.5 us (18%)
    ppermute x11, waiting for transfers between devices, flip_col(): return lax.ppermute(x, 'col', [(i, i ^ j) for i in range(n_col)])  92.7 us
    ppermute x5, waiting for transfers between devices, shards(): lax.ppermute(last[1 - parity], 'row', [(2 * a + c, 2 * b + c) for a, b in...  21.3 us
    pallas_call x8, Pallas kernels, products(): pl.pallas_call(functools.partial(product_kernel, len(ws), len(ts), len(ts...  21.2 us
    ppermute x15, starting transfers between devices, flip_row(): return lax.ppermute(x, 'row', [(i, i ^ j) for i in range(n_row)])  14.9 us
    ppermute x11, starting transfers between devices, flip_col(): return lax.ppermute(x, 'col', [(i, i ^ j) for i in range(n_col)])  14.8 us
    pallas_call x1, Pallas kernels, deep_product(): pl.pallas_call(deep_kernel, grid=(depth // block,), in_specs=[pl.BlockSpe...  9.12 us
    ppermute x15, waiting for transfers between devices, flip_row(): return lax.ppermute(x, 'row', [(i, i ^ j) for i in range(n_row)])  8.57 us
    ppermute x5, starting transfers between devices, shards(): lax.ppermute(last[1 - parity], 'row', [(2 * a + c, 2 * b + c) for a, b in...  6.76 us
  transfers between devices with their start and end apart: 31, of which 15 were waited for; matrix products, arithmetic and copies ran while one was open for 1% of the time, Pallas kernels for 19%

profile of v2, /device:TPU:0, one launch (start us, length us, event | category | flops | bytes accessed | tf_op | source)
XLA Modules:
  0.0 199.9 jit_solution(8455153690323414478)
XLA Ops:
  0.0 0.5 collective-permute-start
  0.5 1.5 shard_map.38.refs_0_
  2.0 2.6 %collective-permute-start.3 = (bf16[256,3584]{1,0:T(8,128)(2,1)S(1)}, bf16[256,3584]{1,0:T(8,128)(2,1)S(1)}, u32[]{:S(2)}, u32[]{:S(2)}) collective-permute-start(bf16[256,3584]{1,0:T(8,128)(2,1)S(1)} %shard_map.38.refs_0_), channel_id=1, source_target_pairs={{0,8},{4,12},{8,0},{12,4},{16,24},{20,28},{24,16},{28,20},{1,9},{5... | collective-permute-start | bytes 5505032 | tf_op jit(solution)/shard_map/ppermute | solution.py:243
  4.6 0.8 collective-permute-start.4
  5.4 1.7 shard_map.39.refs_0_
  7.1 2.5 %collective-permute-start.8 = (bf16[336,3584]{1,0:T(8,128)(2,1)S(1)}, bf16[336,3584]{1,0:T(8,128)(2,1)S(1)}, u32[]{:S(2)}, u32[]{:S(2)}) collective-permute-start(bf16[336,3584]{1,0:T(8,128)(2,1)S(1)} %shard_map.39.refs_0_), channel_id=1, source_target_pairs={{0,3},{1,2},{2,1},{3,0},{4,7},{5,6},{6,5},{7,4},{8,11},{9,10},{10,... | collective-permute-start | bytes 7225352 | tf_op jit(solution)/shard_map/ppermute | solution.py:211
  9.6 3.2 %shard_map.40 = (bf16[336,3584]{1,0:T(8,128)(2,1)S(1)}, bf16[336,3584]{1,0:T(8,128)(2,1)S(1)}, bf16[336,3584]{1,0:T(8,128)(2,1)S(1)}) custom-call(bf16[336,14336]{1,0:T(8,128)(2,1)} %bitcast.12, bf16[336,3584]{1,0:T(8,128)(2,1)S(1)} %shard_map.39.refs_0_), custom_call_target="tpu_custom_call" | custom-call | tf_op jit(solution)/shard_map/pallas_call | solution.py:39
  12.8 0.6 collective-permute-start.2
  13.3 1.5 collective-permute-start.7
  14.8 9.1 %shard_map.37 = bf16[336,512]{1,0:T(8,128)(2,1)S(1)} custom-call(bf16[336,14336]{1,0:T(8,128)(2,1)} %bitcast.13, bf16[256,14336]{1,0:T(8,128)(2,1)} %x.1, bf16[256,14336]{1,0:T(8,128)(2,1)S(1)} %collective-permute-done.t1), custom_call_target="tpu_custom_call" | custom-call | flops 4932501504 | bytes 24313856 | tf_op jit(solution)/shard_map/pallas_call | solution.py:133
  24.0 21.3 %collective-permute-done.3.refs_0_ = bf16[256,3584]{1,0:T(8,128)(2,1)S(1)} collective-permute-done((bf16[256,3584]{1,0:T(8,128)(2,1)S(1)}, bf16[256,3584]{1,0:T(8,128)(2,1)S(1)}, u32[]{:S(2)}, u32[]{:S(2)}) %collective-permute-start.3) | collective-permute-done | bytes 1835040 | tf_op jit(solution)/shard_map/ppermute | solution.py:243
  45.3 1.4 collective-permute-done.1.refs_2_.refs_1_
  46.7 0.8 collective-permute-start.6
  47.5 1.3 collective-permute-start.5
  48.8 1.3 collective-permute-start.21
  50.1 64.0 %collective-permute-done.2.refs_4_.refs_5_.refs_1_.refs_0_ = bf16[336,3584]{1,0:T(8,128)(2,1)S(1)} collective-permute-done((bf16[336,3584]{1,0:T(8,128)(2,1)S(1)}, bf16[336,3584]{1,0:T(8,128)(2,1)S(1)}, u32[]{:S(2)}, u32[]{:S(2)}) %collective-permute-start.2) | collective-permute-done | bytes 2408480 | tf_op jit(solution)/shard_map/ppermute | solution.py:211
  114.1 0.1 collective-permute-done.7.refs_3_.refs_4_.refs_0_.refs_1_
  114.2 0.1 shard_map.42
  114.4 0.1 collective-permute-start.9
  114.4 0.5 collective-permute-start.10
  114.9 0.1 shard_map.43
  115.1 0.1 collective-permute-start.11
  115.2 0.4 collective-permute-start.12
  115.7 1.2 collective-permute-done.9.refs_5_.refs_4_
  116.9 1.3 collective-permute-done.10.refs_6_.refs_5_
  118.2 2.7 %shard_map.45.refs_6_ = bf16[2,336,512]{2,1,0:T(8,128)(2,1)S(1)} custom-call(bf16[336,3584]{1,0:T(8,128)(2,1)S(1)} %collective-permute-done.7.refs_3_.refs_4_.refs_0_.refs_1_, bf16[336,3584]{1,0:T(8,128)(2,1)S(1)} %collective-permute-done.8.refs_5_.refs_6_.refs_2_.refs_1_, bf16[256,1792]{1,0:T(8,128)(2,1)S(1)} %get-tuple-element.19.refs_3_.refs_2_, ...), custom_call_target="tpu_custom_call" | custom-call | flops 172032 | bytes 172032 | tf_op jit(solution)/shard_map/pallas_call | solution.py:165
  120.9 1.6 collective-permute-start.13
  122.5 2.7 %shard_map.46.refs_6_ = bf16[2,336,512]{2,1,0:T(8,128)(2,1)S(1)} custom-call(bf16[336,3584]{1,0:T(8,128)(2,1)S(1)} %collective-permute-done.2.refs_4_.refs_5_.refs_1_.refs_0_, bf16[336,3584]{1,0:T(8,128)(2,1)S(1)} %collective-permute-done.8.refs_5_.refs_6_.refs_2_.refs_1_, bf16[256,1792]{1,0:T(8,128)(2,1)S(1)} %get-tuple-element.21.refs_2_, ...), custom_call_target="tpu_custom_call" | custom-call | flops 172032 | bytes 172032 | tf_op jit(solution)/shard_map/pallas_call | solution.py:165
  125.1 1.5 collective-permute-start.17
  126.7 2.7 %shard_map.47.refs_6_ = f32[2,336,512]{2,1,0:T(8,128)S(1)} custom-call(bf16[336,3584]{1,0:T(8,128)(2,1)S(1)} %get-tuple-element.14.refs_3_.refs_0_, bf16[336,3584]{1,0:T(8,128)(2,1)S(1)} %collective-permute-done.2.refs_4_.refs_5_.refs_1_.refs_0_, bf16[256,1792]{1,0:T(8,128)(2,1)S(1)} %get-tuple-element.19.refs_3_.refs_2_, ...), custom_call_target="tpu_custom_call" | custom-call | flops 172032 | bytes 172032 | tf_op jit(solution)/shard_map/pallas_call | solution.py:165
  129.3 2.7 %shard_map.48.refs_2_.refs_1_ = f32[2,336,512]{2,1,0:T(8,128)S(1)} custom-call(bf16[336,3584]{1,0:T(8,128)(2,1)S(1)} %get-tuple-element.14.refs_3_.refs_0_, bf16[336,3584]{1,0:T(8,128)(2,1)S(1)} %collective-permute-done.7.refs_3_.refs_4_.refs_0_.refs_1_, bf16[256,1792]{1,0:T(8,128)(2,1)S(1)} %get-tuple-element.21.refs_2_, ...), custom_call_target="tpu_custom_call" | custom-call | flops 172032 | bytes 172032 | tf_op jit(solution)/shard_map/pallas_call | solution.py:165
  132.0 6.4 %collective-permute-done.13.refs_3_ = bf16[2,336,512]{2,1,0:T(8,128)(2,1)S(1)} collective-permute-done((bf16[2,336,512]{2,1,0:T(8,128)(2,1)S(1)}, bf16[2,336,512]{2,1,0:T(8,128)(2,1)S(1)}, u32[]{:S(2)}, u32[]{:S(2)}) %collective-permute-start.13) | collective-permute-done | bytes 688160 | tf_op jit(solution)/shard_map/ppermute | solution.py:211
  138.4 4.0 %collective-permute-done.17.refs_4_ = bf16[2,336,512]{2,1,0:T(8,128)(2,1)S(1)} collective-permute-done((bf16[2,336,512]{2,1,0:T(8,128)(2,1)S(1)}, bf16[2,336,512]{2,1,0:T(8,128)(2,1)S(1)}, u32[]{:S(2)}, u32[]{:S(2)}) %collective-permute-start.17) | collective-permute-done | bytes 688160 | tf_op jit(solution)/shard_map/ppermute | solution.py:211
  142.4 0.3 shard_map.49.refs_2_
  142.7 0.1 collective-permute-start.22
  142.8 0.2 convert_add_fusion.1
  143.1 1.5 collective-permute-start.14
  144.6 0.2 convert_add_fusion
  144.9 0.6 collective-permute-start.18
  145.5 8.1 %collective-permute-done.14 = bf16[1,336,512]{2,1,0:T(8,128)(2,1)S(1)} collective-permute-done((bf16[1,336,512]{2,1,0:T(8,128)(2,1)S(1)}, bf16[1,336,512]{2,1,0:T(8,128)(2,1)S(1)}, u32[]{:S(2)}, u32[]{:S(2)}) %collective-permute-start.14) | collective-permute-done | bytes 344096 | tf_op jit(solution)/shard_map/ppermute | solution.py:211
  153.6 0.1 fusion.2
  153.7 4.1 %collective-permute-start.15 = (bf16[336,256]{1,0:T(8,128)(2,1)S(1)}, bf16[336,256]{1,0:T(8,128)(2,1)S(1)}, u32[]{:S(2)}, u32[]{:S(2)}) collective-permute-start(bf16[336,256]{1,0:T(8,128)(2,1)S(1)} %get-tuple-element.26), channel_id=1, source_target_pairs={{0,8},{4,12},{8,0},{12,4},{16,24},{20,28},{24,16},{28,20},{1,9},{5... | collective-permute-start | bytes 516104 | tf_op jit(solution)/shard_map/ppermute | solution.py:214
  157.8 2.6 %shard_map.51.refs_4_ = bf16[2,336,256]{2,1,0:T(8,128)(2,1)S(1)} custom-call(bf16[336,3584]{1,0:T(8,128)(2,1)S(1)} %collective-permute-done.7.refs_3_.refs_4_.refs_0_.refs_1_, bf16[336,3584]{1,0:T(8,128)(2,1)S(1)} %collective-permute-done.8.refs_5_.refs_6_.refs_2_.refs_1_, bf16[256,3584]{1,0:T(8,128)(2,1)S(1)} %shard_map.49.refs_2_, ...), custom_call_target="tpu_custom_call" | custom-call | flops 86016 | bytes 86016 | tf_op jit(solution)/shard_map/pallas_call | solution.py:165
  160.5 0.6 collective-permute-start.23
  161.1 0.1 fusion.3
  161.2 2.6 %shard_map.52.refs_4_ = bf16[2,336,256]{2,1,0:T(8,128)(2,1)S(1)} custom-call(bf16[336,3584]{1,0:T(8,128)(2,1)S(1)} %collective-permute-done.2.refs_4_.refs_5_.refs_1_.refs_0_, bf16[336,3584]{1,0:T(8,128)(2,1)S(1)} %collective-permute-done.8.refs_5_.refs_6_.refs_2_.refs_1_, bf16[256,3584]{1,0:T(8,128)(2,1)S(1)} %shard_map.49.refs_2_, ...), custom_call_target="tpu_custom_call" | custom-call | flops 86016 | bytes 86016 | tf_op jit(solution)/shard_map/pallas_call | solution.py:165
  163.8 1.5 collective-permute-start.27
  165.4 2.6 %shard_map.53.refs_4_ = f32[2,336,256]{2,1,0:T(8,128)S(1)} custom-call(bf16[336,3584]{1,0:T(8,128)(2,1)S(1)} %get-tuple-element.14.refs_3_.refs_0_, bf16[336,3584]{1,0:T(8,128)(2,1)S(1)} %collective-permute-done.2.refs_4_.refs_5_.refs_1_.refs_0_, bf16[256,3584]{1,0:T(8,128)(2,1)S(1)} %shard_map.49.refs_2_, ...), custom_call_target="tpu_custom_call" | custom-call | flops 86016 | bytes 86016 | tf_op jit(solution)/shard_map/pallas_call | solution.py:165
  168.0 0.9 collective-permute-start.19
  168.9 2.6 %shard_map.54 = f32[2,336,256]{2,1,0:T(8,128)S(1)} custom-call(bf16[336,3584]{1,0:T(8,128)(2,1)S(1)} %get-tuple-element.14.refs_3_.refs_0_, bf16[336,3584]{1,0:T(8,128)(2,1)S(1)} %collective-permute-done.7.refs_3_.refs_4_.refs_0_.refs_1_, bf16[256,3584]{1,0:T(8,128)(2,1)S(1)} %shard_map.49.refs_2_, ...), custom_call_target="tpu_custom_call" | custom-call | flops 86016 | bytes 86016 | tf_op jit(solution)/shard_map/pallas_call | solution.py:165
  171.5 1.2 collective-permute-start.20
  172.8 1.0 collective-permute-done.27
  173.8 1.4 collective-permute-start.24
  175.3 5.0 %collective-permute-done.24 = bf16[1,336,256]{2,1,0:T(8,128)(2,1)S(1)} collective-permute-done((bf16[1,336,256]{2,1,0:T(8,128)(2,1)S(1)}, bf16[1,336,256]{2,1,0:T(8,128)(2,1)S(1)}, u32[]{:S(2)}, u32[]{:S(2)}) %collective-permute-start.24) | collective-permute-done | bytes 172064 | tf_op jit(solution)/shard_map/ppermute | solution.py:211
  180.3 1.5 collective-permute-start.28
  181.9 4.1 %collective-permute-done.28 = bf16[1,336,256]{2,1,0:T(8,128)(2,1)S(1)} collective-permute-done((bf16[1,336,256]{2,1,0:T(8,128)(2,1)S(1)}, bf16[1,336,256]{2,1,0:T(8,128)(2,1)S(1)}, u32[]{:S(2)}, u32[]{:S(2)}) %collective-permute-start.28) | collective-permute-done | bytes 172064 | tf_op jit(solution)/shard_map/ppermute | solution.py:211
  186.0 1.2 collective-permute-start.25
  187.3 0.5 collective-permute-start.26
  187.8 2.3 %collective-permute-start.29 = (bf16[336,128]{1,0:T(8,128)(2,1)S(1)}, bf16[336,128]{1,0:T(8,128)(2,1)S(1)}, u32[]{:S(2)}, u32[]{:S(2)}) collective-permute-start(bf16[336,128]{1,0:T(8,128)(2,1)S(1)} %get-tuple-element.30), channel_id=1, source_target_pairs={{0,24},{4,28},{8,16},{12,20},{16,8},{20,12},{24,0},{28,4},{1,25},{... | collective-permute-start | bytes 258056 | tf_op jit(solution)/shard_map/ppermute | solution.py:214
  190.0 3.2 %collective-permute-start.30 = (bf16[336,128]{1,0:T(8,128)(2,1)S(1)}, bf16[336,128]{1,0:T(8,128)(2,1)S(1)}, u32[]{:S(2)}, u32[]{:S(2)}) collective-permute-start(bf16[336,128]{1,0:T(8,128)(2,1)S(1)} %get-tuple-element.29), channel_id=1, source_target_pairs={{0,28},{4,24},{8,20},{12,16},{16,12},{20,8},{24,4},{28,0},{1,29},{... | collective-permute-start | bytes 258056 | tf_op jit(solution)/shard_map/ppermute | solution.py:214
  193.3 0.8 collective-permute-done.26.refs_7_
  194.0 1.7 collective-permute-done.29.refs_8_
  195.7 2.2 %collective-permute-done.30.refs_9_ = bf16[336,128]{1,0:T(8,128)(2,1)S(1)} collective-permute-done((bf16[336,128]{1,0:T(8,128)(2,1)S(1)}, bf16[336,128]{1,0:T(8,128)(2,1)S(1)}, u32[]{:S(2)}, u32[]{:S(2)}) %collective-permute-start.30) | collective-permute-done | bytes 86048 | tf_op jit(solution)/shard_map/ppermute | solution.py:214
  197.9 2.0 %shard_map.55 = bf16[256,2688]{1,0:T(8,128)(2,1)} custom-call(bf16[336,256]{1,0:T(8,128)(2,1)S(1)} %get-tuple-element.28.refs_0_, bf16[336,256]{1,0:T(8,128)(2,1)S(1)} %collective-permute-done.1.refs_2_.refs_1_, bf16[336,256]{1,0:T(8,128)(2,1)S(1)} %collective-permute-done.15.refs_2_, bf16[336,256]{1,0:T(8,128)(2,1)S(1)} %collective-permute-done.16.refs_3_, ...), custom_call_target="tpu_custom_call" | custom-call | flops 688128 | bytes 2752512 | tf_op jit(solution)/shard_map/pallas_call | solution.py:192
  (37 shorter events, 0.5 us)
Async XLA Ops:
  0.0 13.3 %collective-permute-start = (bf16[256,14336]{1,0:T(8,128)(2,1)}, bf16[256,14336]{1,0:T(8,128)(2,1)S(1)}, u32[]{:S(2)}, u32[]{:S(2)}) collective-permute-start(bf16[256,14336]{1,0:T(8,128)(2,1)} %x.1), channel_id=1, source_target_pairs={{0,4},{4,0},{8,12},{12,8},{16,20},{20,16},{24,28},{28,24},{1,5},{5... | collective-permute-start | bytes 22020104 | tf_op jit(solution)/shard_map/ppermute | solution.py:214
  2.0 43.3 %collective-permute-start.3 = (bf16[256,3584]{1,0:T(8,128)(2,1)S(1)}, bf16[256,3584]{1,0:T(8,128)(2,1)S(1)}, u32[]{:S(2)}, u32[]{:S(2)}) collective-permute-start(bf16[256,3584]{1,0:T(8,128)(2,1)S(1)} %shard_map.38.refs_0_), channel_id=1, source_target_pairs={{0,8},{4,12},{8,0},{12,4},{16,24},{20,28},{24,16},{28,20},{1,9},{5... | collective-permute-start | bytes 5505032 | tf_op jit(solution)/shard_map/ppermute | solution.py:243
  4.6 40.7 %collective-permute-start.4 = (bf16[256,3584]{1,0:T(8,128)(2,1)S(1)}, bf16[256,3584]{1,0:T(8,128)(2,1)S(1)}, u32[]{:S(2)}, u32[]{:S(2)}) collective-permute-start(bf16[256,3584]{1,0:T(8,128)(2,1)S(1)} %shard_map.38.refs_0_), channel_id=1, source_target_pairs={{8,16},{12,20},{16,8},{20,12},{9,17},{13,21},{17,9},{21,13},{10,18... | collective-permute-start | bytes 5505032 | tf_op jit(solution)/shard_map/ppermute | solution.py:243
  7.1 107.1 %collective-permute-start.8 = (bf16[336,3584]{1,0:T(8,128)(2,1)S(1)}, bf16[336,3584]{1,0:T(8,128)(2,1)S(1)}, u32[]{:S(2)}, u32[]{:S(2)}) collective-permute-start(bf16[336,3584]{1,0:T(8,128)(2,1)S(1)} %shard_map.39.refs_0_), channel_id=1, source_target_pairs={{0,3},{1,2},{2,1},{3,0},{4,7},{5,6},{6,5},{7,4},{8,11},{9,10},{10,... | collective-permute-start | bytes 7225352 | tf_op jit(solution)/shard_map/ppermute | solution.py:211
  12.8 101.3 %collective-permute-start.2 = (bf16[336,3584]{1,0:T(8,128)(2,1)S(1)}, bf16[336,3584]{1,0:T(8,128)(2,1)S(1)}, u32[]{:S(2)}, u32[]{:S(2)}) collective-permute-start(bf16[336,3584]{1,0:T(8,128)(2,1)S(1)} %get-tuple-element.15), channel_id=1, source_target_pairs={{0,2},{1,3},{2,0},{3,1},{4,6},{5,7},{6,4},{7,5},{8,10},{9,11},{10,... | collective-permute-start | bytes 7225352 | tf_op jit(solution)/shard_map/ppermute | solution.py:211
  13.3 100.9 %collective-permute-start.7 = (bf16[336,3584]{1,0:T(8,128)(2,1)S(1)}, bf16[336,3584]{1,0:T(8,128)(2,1)S(1)}, u32[]{:S(2)}, u32[]{:S(2)}) collective-permute-start(bf16[336,3584]{1,0:T(8,128)(2,1)S(1)} %get-tuple-element.18), channel_id=1, source_target_pairs={{0,1},{1,0},{2,3},{3,2},{4,5},{5,4},{6,7},{7,6},{8,9},{9,8},{10,11... | collective-permute-start | bytes 7225352 | tf_op jit(solution)/shard_map/ppermute | solution.py:211
  45.3 1.4 collective-permute-start.1
  46.7 2.1 %collective-permute-start.6 = (bf16[256,3584]{1,0:T(8,128)(2,1)S(1)}, bf16[256,3584]{1,0:T(8,128)(2,1)S(1)}, u32[]{:S(2)}, u32[]{:S(2)}) collective-permute-start(bf16[256,3584]{1,0:T(8,128)(2,1)S(1)} %get-tuple-element.16.refs_0_), channel_id=1, source_target_pairs={{8,16},{12,20},{16,8},{20,12},{9,17},{13,21},{17,9},{21,13},{10,18... | collective-permute-start | bytes 5505032 | tf_op jit(solution)/shard_map/ppermute | solution.py:243
  47.5 66.7 %collective-permute-start.5 = (bf16[256,3584]{1,0:T(8,128)(2,1)S(1)}, bf16[256,3584]{1,0:T(8,128)(2,1)S(1)}, u32[]{:S(2)}, u32[]{:S(2)}) collective-permute-start(bf16[256,3584]{1,0:T(8,128)(2,1)S(1)} %get-tuple-element.17.refs_0_), channel_id=1, source_target_pairs={{8,0},{12,4},{16,24},{20,28},{9,1},{13,5},{17,25},{21,29},{10,2},{... | collective-permute-start | bytes 5505032 | tf_op jit(solution)/shard_map/ppermute | solution.py:243
  48.8 93.6 %collective-permute-start.21 = (bf16[256,3584]{1,0:T(8,128)(2,1)S(1)}, bf16[256,3584]{1,0:T(8,128)(2,1)S(1)}, u32[]{:S(2)}, u32[]{:S(2)}) collective-permute-start(bf16[256,3584]{1,0:T(8,128)(2,1)S(1)} %collective-permute-done.6.refs_2_.refs_1_.refs_3_), channel_id=1, source_target_pairs={{8,0},{12,4},{16,24},{20,28},{9,1},{13,5},{17,25},{21,29},{10,2},{... | collective-permute-start | bytes 5505032 | tf_op jit(solution)/shard_map/ppermute | solution.py:243
  114.4 2.5 %collective-permute-start.9 = (bf16[256,1792]{1,0:T(8,128)(2,1)S(1)}, bf16[256,1792]{1,0:T(8,128)(2,1)S(1)}, u32[]{:S(2)}, u32[]{:S(2)}) collective-permute-start(bf16[256,1792]{1,0:T(8,128)(2,1)S(1)} %get-tuple-element.19.refs_3_.refs_2_), channel_id=1, source_target_pairs={{0,4},{4,0},{8,12},{12,8},{16,20},{20,16},{24,28},{28,24},{1,5},{5... | collective-permute-start | bytes 2752520 | tf_op jit(solution)/shard_map/ppermute | solution.py:214
  114.4 3.8 %collective-permute-start.10 = (bf16[256,1792]{1,0:T(8,128)(2,1)S(1)}, bf16[256,1792]{1,0:T(8,128)(2,1)S(1)}, u32[]{:S(2)}, u32[]{:S(2)}) collective-permute-start(bf16[256,1792]{1,0:T(8,128)(2,1)S(1)} %get-tuple-element.20.refs_4_.refs_3_), channel_id=1, source_target_pairs={{0,4},{4,0},{8,12},{12,8},{16,20},{20,16},{24,28},{28,24},{1,5},{5... | collective-permute-start | bytes 2752520 | tf_op jit(solution)/shard_map/ppermute | solution.py:214
  115.1 7.4 %collective-permute-start.11 = (bf16[256,1792]{1,0:T(8,128)(2,1)S(1)}, bf16[256,1792]{1,0:T(8,128)(2,1)S(1)}, u32[]{:S(2)}, u32[]{:S(2)}) collective-permute-start(bf16[256,1792]{1,0:T(8,128)(2,1)S(1)} %get-tuple-element.21.refs_2_), channel_id=1, source_target_pairs={{0,4},{4,0},{8,12},{12,8},{16,20},{20,16},{24,28},{28,24},{1,5},{5... | collective-permute-start | bytes 2752520 | tf_op jit(solution)/shard_map/ppermute | solution.py:214
  115.2 7.2 %collective-permute-start.12 = (bf16[256,1792]{1,0:T(8,128)(2,1)S(1)}, bf16[256,1792]{1,0:T(8,128)(2,1)S(1)}, u32[]{:S(2)}, u32[]{:S(2)}) collective-permute-start(bf16[256,1792]{1,0:T(8,128)(2,1)S(1)} %get-tuple-element.22.refs_3_), channel_id=1, source_target_pairs={{0,4},{4,0},{8,12},{12,8},{16,20},{20,16},{24,28},{28,24},{1,5},{5... | collective-permute-start | bytes 2752520 | tf_op jit(solution)/shard_map/ppermute | solution.py:214
  120.9 17.5 %collective-permute-start.13 = (bf16[2,336,512]{2,1,0:T(8,128)(2,1)S(1)}, bf16[2,336,512]{2,1,0:T(8,128)(2,1)S(1)}, u32[]{:S(2)}, u32[]{:S(2)}) collective-permute-start(bf16[2,336,512]{2,1,0:T(8,128)(2,1)S(1)} %shard_map.45.refs_6_), channel_id=1, source_target_pairs={{0,1},{1,0},{2,3},{3,2},{4,5},{5,4},{6,7},{7,6},{8,9},{9,8},{10,11... | collective-permute-start | bytes 2064392 | tf_op jit(solution)/shard_map/ppermute | solution.py:211
  125.1 17.3 %collective-permute-start.17 = (bf16[2,336,512]{2,1,0:T(8,128)(2,1)S(1)}, bf16[2,336,512]{2,1,0:T(8,128)(2,1)S(1)}, u32[]{:S(2)}, u32[]{:S(2)}) collective-permute-start(bf16[2,336,512]{2,1,0:T(8,128)(2,1)S(1)} %shard_map.46.refs_6_), channel_id=1, source_target_pairs={{0,2},{1,3},{2,0},{3,1},{4,6},{5,7},{6,4},{7,5},{8,10},{9,11},{10,... | collective-permute-start | bytes 2064392 | tf_op jit(solution)/shard_map/ppermute | solution.py:211
  142.7 15.1 %collective-permute-start.22 = (bf16[256,3584]{1,0:T(8,128)(2,1)S(1)}, bf16[256,3584]{1,0:T(8,128)(2,1)S(1)}, u32[]{:S(2)}, u32[]{:S(2)}) collective-permute-start(bf16[256,3584]{1,0:T(8,128)(2,1)S(1)} %shard_map.49.refs_2_), channel_id=1, source_target_pairs={{0,4},{4,0},{8,12},{12,8},{16,20},{20,16},{24,28},{28,24},{1,5},{5... | collective-permute-start | bytes 5505032 | tf_op jit(solution)/shard_map/ppermute | solution.py:214
  143.1 10.5 %collective-permute-start.14 = (bf16[1,336,512]{2,1,0:T(8,128)(2,1)S(1)}, bf16[1,336,512]{2,1,0:T(8,128)(2,1)S(1)}, u32[]{:S(2)}, u32[]{:S(2)}) collective-permute-start(bf16[1,336,512]{2,1,0:T(8,128)(2,1)S(1)} %slice.119), channel_id=1, source_target_pairs={{0,2},{1,3},{2,0},{3,1},{4,6},{5,7},{6,4},{7,5},{8,10},{9,11},{10,... | collective-permute-start | bytes 1032200 | tf_op jit(solution)/shard_map/ppermute | solution.py:211
  144.9 16.2 %collective-permute-start.18 = (bf16[1,336,512]{2,1,0:T(8,128)(2,1)S(1)}, bf16[1,336,512]{2,1,0:T(8,128)(2,1)S(1)}, u32[]{:S(2)}, u32[]{:S(2)}) collective-permute-start(bf16[1,336,512]{2,1,0:T(8,128)(2,1)S(1)} %slice.118), channel_id=1, source_target_pairs={{0,1},{1,0},{2,3},{3,2},{4,5},{5,4},{6,7},{7,6},{8,9},{9,8},{10,11... | collective-permute-start | bytes 1032200 | tf_op jit(solution)/shard_map/ppermute | solution.py:211
  153.7 33.5 %collective-permute-start.15 = (bf16[336,256]{1,0:T(8,128)(2,1)S(1)}, bf16[336,256]{1,0:T(8,128)(2,1)S(1)}, u32[]{:S(2)}, u32[]{:S(2)}) collective-permute-start(bf16[336,256]{1,0:T(8,128)(2,1)S(1)} %get-tuple-element.26), channel_id=1, source_target_pairs={{0,8},{4,12},{8,0},{12,4},{16,24},{20,28},{24,16},{28,20},{1,9},{5... | collective-permute-start | bytes 516104 | tf_op jit(solution)/shard_map/ppermute | solution.py:214
  157.8 29.9 %collective-permute-start.16 = (bf16[336,256]{1,0:T(8,128)(2,1)S(1)}, bf16[336,256]{1,0:T(8,128)(2,1)S(1)}, u32[]{:S(2)}, u32[]{:S(2)}) collective-permute-start(bf16[336,256]{1,0:T(8,128)(2,1)S(1)} %get-tuple-element.25), channel_id=1, source_target_pairs={{0,12},{4,8},{8,4},{12,0},{16,28},{20,24},{24,20},{28,16},{1,13},{... | collective-permute-start | bytes 516104 | tf_op jit(solution)/shard_map/ppermute | solution.py:214
  160.5 11.0 %collective-permute-start.23 = (bf16[2,336,256]{2,1,0:T(8,128)(2,1)S(1)}, bf16[2,336,256]{2,1,0:T(8,128)(2,1)S(1)}, u32[]{:S(2)}, u32[]{:S(2)}) collective-permute-start(bf16[2,336,256]{2,1,0:T(8,128)(2,1)S(1)} %shard_map.51.refs_4_), channel_id=1, source_target_pairs={{0,1},{1,0},{2,3},{3,2},{4,5},{5,4},{6,7},{7,6},{8,9},{9,8},{10,11... | collective-permute-start | bytes 1032200 | tf_op jit(solution)/shard_map/ppermute | solution.py:211
  163.8 10.0 %collective-permute-start.27 = (bf16[2,336,256]{2,1,0:T(8,128)(2,1)S(1)}, bf16[2,336,256]{2,1,0:T(8,128)(2,1)S(1)}, u32[]{:S(2)}, u32[]{:S(2)}) collective-permute-start(bf16[2,336,256]{2,1,0:T(8,128)(2,1)S(1)} %shard_map.52.refs_4_), channel_id=1, source_target_pairs={{0,2},{1,3},{2,0},{3,1},{4,6},{5,7},{6,4},{7,5},{8,10},{9,11},{10,... | collective-permute-start | bytes 1032200 | tf_op jit(solution)/shard_map/ppermute | solution.py:211
  168.0 22.0 %collective-permute-start.19 = (bf16[336,256]{1,0:T(8,128)(2,1)S(1)}, bf16[336,256]{1,0:T(8,128)(2,1)S(1)}, u32[]{:S(2)}, u32[]{:S(2)}) collective-permute-start(bf16[336,256]{1,0:T(8,128)(2,1)S(1)} %get-tuple-element.24), channel_id=1, source_target_pairs={{0,16},{4,20},{8,24},{12,28},{16,0},{20,4},{24,8},{28,12},{1,17},{... | collective-permute-start | bytes 516104 | tf_op jit(solution)/shard_map/ppermute | solution.py:214
  171.5 21.7 %collective-permute-start.20 = (bf16[336,256]{1,0:T(8,128)(2,1)S(1)}, bf16[336,256]{1,0:T(8,128)(2,1)S(1)}, u32[]{:S(2)}, u32[]{:S(2)}) collective-permute-start(bf16[336,256]{1,0:T(8,128)(2,1)S(1)} %get-tuple-element.23), channel_id=1, source_target_pairs={{0,20},{4,16},{8,28},{12,24},{16,4},{20,0},{24,12},{28,8},{1,21},{... | collective-permute-start | bytes 516104 | tf_op jit(solution)/shard_map/ppermute | solution.py:214
  172.8 20.5 %copy-start = (f32[2688]{0:T(1024)S(1)}, f32[2688]{0:T(1024)}, u32[]{:S(2)}) copy-start(f32[2688]{0:T(1024)} %param.5) | copy-start | bytes 32260
  173.8 6.5 %collective-permute-start.24 = (bf16[1,336,256]{2,1,0:T(8,128)(2,1)S(1)}, bf16[1,336,256]{2,1,0:T(8,128)(2,1)S(1)}, u32[]{:S(2)}, u32[]{:S(2)}) collective-permute-start(bf16[1,336,256]{2,1,0:T(8,128)(2,1)S(1)} %slice.121), channel_id=1, source_target_pairs={{0,2},{1,3},{2,0},{3,1},{4,6},{5,7},{6,4},{7,5},{8,10},{9,11},{10,... | collective-permute-start | bytes 516104 | tf_op jit(solution)/shard_map/ppermute | solution.py:211
  180.3 5.7 %collective-permute-start.28 = (bf16[1,336,256]{2,1,0:T(8,128)(2,1)S(1)}, bf16[1,336,256]{2,1,0:T(8,128)(2,1)S(1)}, u32[]{:S(2)}, u32[]{:S(2)}) collective-permute-start(bf16[1,336,256]{2,1,0:T(8,128)(2,1)S(1)} %slice.120), channel_id=1, source_target_pairs={{0,1},{1,0},{2,3},{3,2},{4,5},{5,4},{6,7},{7,6},{8,9},{9,8},{10,11... | collective-permute-start | bytes 516104 | tf_op jit(solution)/shard_map/ppermute | solution.py:211
  186.0 7.3 %collective-permute-start.25 = (bf16[336,128]{1,0:T(8,128)(2,1)S(1)}, bf16[336,128]{1,0:T(8,128)(2,1)S(1)}, u32[]{:S(2)}, u32[]{:S(2)}) collective-permute-start(bf16[336,128]{1,0:T(8,128)(2,1)S(1)} %get-tuple-element.32), channel_id=1, source_target_pairs={{0,24},{4,28},{8,16},{12,20},{16,8},{20,12},{24,0},{28,4},{1,25},{... | collective-permute-start | bytes 258056 | tf_op jit(solution)/shard_map/ppermute | solution.py:214
  187.3 6.8 %collective-permute-start.26 = (bf16[336,128]{1,0:T(8,128)(2,1)S(1)}, bf16[336,128]{1,0:T(8,128)(2,1)S(1)}, u32[]{:S(2)}, u32[]{:S(2)}) collective-permute-start(bf16[336,128]{1,0:T(8,128)(2,1)S(1)} %get-tuple-element.31), channel_id=1, source_target_pairs={{0,28},{4,24},{8,20},{12,16},{16,12},{20,8},{24,4},{28,0},{1,29},{... | collective-permute-start | bytes 258056 | tf_op jit(solution)/shard_map/ppermute | solution.py:214
  187.8 7.9 %collective-permute-start.29 = (bf16[336,128]{1,0:T(8,128)(2,1)S(1)}, bf16[336,128]{1,0:T(8,128)(2,1)S(1)}, u32[]{:S(2)}, u32[]{:S(2)}) collective-permute-start(bf16[336,128]{1,0:T(8,128)(2,1)S(1)} %get-tuple-element.30), channel_id=1, source_target_pairs={{0,24},{4,28},{8,16},{12,20},{16,8},{20,12},{24,0},{28,4},{1,25},{... | collective-permute-start | bytes 258056 | tf_op jit(solution)/shard_map/ppermute | solution.py:214
  190.0 7.8 %collective-permute-start.30 = (bf16[336,128]{1,0:T(8,128)(2,1)S(1)}, bf16[336,128]{1,0:T(8,128)(2,1)S(1)}, u32[]{:S(2)}, u32[]{:S(2)}) collective-permute-start(bf16[336,128]{1,0:T(8,128)(2,1)S(1)} %get-tuple-element.29), channel_id=1, source_target_pairs={{0,28},{4,24},{8,20},{12,16},{16,12},{20,8},{24,4},{28,0},{1,29},{... | collective-permute-start | bytes 258056 | tf_op jit(solution)/shard_map/ppermute | solution.py:214

commit v3 on v2

--- a/solution.py
+++ b/solution.py
@@ -9,8 +9,8 @@
 
 ROOM = 14 * 1024 * 1024
 SPACE = 0
-GATE = 0
-GATE2 = 0
+KEPT = 4_000_000_000
+BACKS = 9
 IN_VMEM = pl.BlockSpec(memory_space=pltpu.VMEM)
 IN_HBM = pl.BlockSpec(memory_space=pltpu.HBM)
 ANYWHERE = pl.BlockSpec(memory_space=pl.ANY)
@@ -21,29 +21,33 @@
     return max(d for d in range(128, most + 1, 128) if size % d == 0)
 
 
-def bands_kernel(pieces, band, x, *refs):
+def bands_kernel(pieces, n_col, n_x, *refs):
     outs, sems = refs[-1 - len(pieces) : -1], refs[-1]
     col = lax.axis_index("col")
     copies = []
-    for i, (j, first, rows) in enumerate(pieces):
+    for i, (which, j, first, rows) in enumerate(pieces):
+        band = refs[which].shape[1] // n_col
         start = pl.multiple_of((col ^ j) * band, 128)
-        copies.append(pltpu.make_async_copy(x.at[pl.ds(first, rows), pl.ds(start, band)], outs[i], sems.at[i]))
+        copies.append(
+            pltpu.make_async_copy(refs[which].at[pl.ds(first, rows), pl.ds(start, band)], outs[i], sems.at[i])
+        )
     for copy in copies:
         copy.start()
     for copy in copies:
         copy.wait()
 
 
-def bands(x, pieces, n_col, after):
-    band = x.shape[1] // n_col
-    return pl.pallas_call(
-        functools.partial(bands_kernel, pieces, band),
-        out_shape=[jax.ShapeDtypeStruct((rows, band), x.dtype) for _, _, rows in pieces],
-        in_specs=[IN_HBM] + [ANYWHERE] * len(after),
+def bands(xs, pieces, n_col, after):
+    return pl.pallas_call(
+        functools.partial(bands_kernel, pieces, n_col, len(xs)),
+        out_shape=[
+            jax.ShapeDtypeStruct((rows, xs[which].shape[1] // n_col), xs[which].dtype) for which, _, _, rows in pieces
+        ],
+        in_specs=[IN_HBM] * len(xs) + [ANYWHERE] * len(after),
         out_specs=[IN_VMEM] * len(pieces),
         scratch_shapes=[pltpu.SemaphoreType.DMA((len(pieces),))],
         compiler_params=pltpu.CompilerParams(vmem_limit_bytes=ROOM),
-    )(pltpu.with_memory_space_constraint(x, pltpu.HBM), *after)
+    )(*[pltpu.with_memory_space_constraint(x, pltpu.HBM) for x in xs], *after)
 
 
 def choose_kernel(wanted, n, *refs):
@@ -144,34 +148,60 @@
     )(*[pltpu.with_memory_space_constraint(x, pltpu.HBM) for x in (w, t0)], t1)
 
 
-def product_kernel(n_w, n_t, cuts, first, rows, *refs):
-    out_ref = refs[-1]
-    for i, w in enumerate(refs[:n_w]):
-        for k in range(n_t):
-            total, start = 0.0, 0
-            for t in refs[n_w + k * cuts : n_w + (k + 1) * cuts]:
-                stop = start + t.shape[1]
-                total += lax.dot_general(
-                    w[:, start:stop], t[first : first + rows, :], BOTH_LAST, preferred_element_type=jnp.float32
-                )
-                start = stop
-            out_ref[i, :, k * rows : (k + 1) * rows] = total.astype(out_ref.dtype)
-
-
-def products(ws, ts, first, rows, dtype, after):
-    m = ws[0].shape[0]
-    shape = (len(ws), m, rows * len(ts))
-    flat = [piece for t in ts for piece in t]
-    return pl.pallas_call(
-        functools.partial(product_kernel, len(ws), len(ts), len(ts[0]), first, rows),
-        in_specs=[IN_VMEM] * (len(ws) + len(flat)) + [ANYWHERE] * len(after),
-        out_specs=IN_VMEM,
-        out_shape=jax.ShapeDtypeStruct(shape, dtype),
-        compiler_params=pltpu.CompilerParams(vmem_limit_bytes=ROOM),
-        cost_estimate=pl.CostEstimate(
-            flops=len(ws) * m * rows, bytes_accessed=len(ws) * m * rows, transcendentals=0
-        ),
-    )(*ws, *flat, *after)
+def product_kernel(plan, n_in, *refs):
+    outs = refs[len(refs) - len(plan) :]
+    for out, (ws, ts) in zip(outs, plan):
+        for i, w in enumerate(ws):
+            for k, t in enumerate(ts):
+                rows = refs[t].shape[0]
+                out[i, :, k * rows : (k + 1) * rows] = lax.dot_general(
+                    refs[w][...], refs[t][...], BOTH_LAST, preferred_element_type=jnp.float32
+                ).astype(out.dtype)
+
+
+def products(jobs, dtype, after, flops=0):
+    arrays, plan, shapes = [], [], []
+    for ws, ts in jobs:
+        places = []
+        for group in (ws, ts):
+            place = []
+            for x in group:
+                known = [i for i, y in enumerate(arrays) if y is x]
+                if not known:
+                    arrays.append(x)
+                place.append(known[0] if known else len(arrays) - 1)
+            places.append(place)
+        plan.append(tuple(places))
+        shapes.append((len(ws), ws[0].shape[0], sum(t.shape[0] for t in ts)))
+    size = sum(a * b * c for a, b, c in shapes)
+    return pl.pallas_call(
+        functools.partial(product_kernel, plan, len(arrays)),
+        in_specs=[IN_VMEM] * len(arrays) + [ANYWHERE] * len(after),
+        out_specs=[IN_VMEM] * len(jobs),
+        out_shape=[jax.ShapeDtypeStruct(shape, dtype) for shape in shapes],
+        compiler_params=pltpu.CompilerParams(vmem_limit_bytes=ROOM),
+        cost_estimate=pl.CostEstimate(flops=flops + size, bytes_accessed=size, transcendentals=0),
+    )(*arrays, *after)
+
+
+def total_kernel(n_out, mine, got, *refs):
+    outs = refs[-n_out:]
+    rows = outs[0].shape[1]
+    for k, out in enumerate(outs):
+        part = slice(k * rows, (k + 1) * rows)
+        out[...] = (mine[0, :, part] + got[0, :, part].astype(jnp.float32)).astype(out.dtype)
+
+
+def totals(mine, got, rows, after):
+    _, m, width = mine.shape
+    return pl.pallas_call(
+        functools.partial(total_kernel, width // rows),
+        in_specs=[IN_VMEM] * 2 + [ANYWHERE] * len(after),
+        out_specs=[IN_VMEM] * (width // rows),
+        out_shape=[jax.ShapeDtypeStruct((m, rows), jnp.bfloat16)] * (width // rows),
+        compiler_params=pltpu.CompilerParams(vmem_limit_bytes=ROOM),
+        cost_estimate=pl.CostEstimate(flops=m * width, bytes_accessed=m * width, transcendentals=0),
+    )(mine, got, *after)
 
 
 def join_kernel(places, *refs):
@@ -213,10 +243,9 @@
     def flip_row(x, j):
         return lax.ppermute(x, "row", [(i, i ^ j) for i in range(n_row)])
 
-    (own,) = bands(tokens, [(0, 0, half)], n_col, [])
     js = list(range(n_col))
-    (far,) = bands(weight, [(n_col - 1, 0, columns)], n_col, [own])
-    near = bands(weight, [(j, 0, columns) for j in js[:-1]], n_col, [far])
+    own, far = bands([tokens, weight], [(0, 0, 0, half), (1, n_col - 1, 0, columns)], n_col, [])
+    near = bands([weight], [(0, j, 0, columns) for j in js[:-1]], n_col, [far])
     w_band = [near[0]] + [flip_col(x, j) for j, x in zip(js[1:], list(near[1:]) + [far])]
     here = deep_product(weight, tokens, flip_row(tokens, 1))
     here_other = flip_row(here[:, half:], 1)
@@ -248,54 +277,83 @@
                     second.append(now[parity])
         last = now
 
-    def arrived(d, after, cuts):
+    def arrived(d, after):
         wanted = [next(i for i, (_, came) in enumerate(held) if came.get(p) == p ^ d) for p in range(planes)]
         used = sorted(set(wanted))
-        value = list(choose([held[i][0] for i in used], [used.index(i) for i in wanted], after, cuts))
-        return [value, [flip_row(x, 1) for x in value]]
+        (value,) = choose([held[i][0] for i in used], [used.index(i) for i in wanted], after, 1)
+        return [value, flip_row(value, 1)]
+
+    def halve(kept, mine, sums, orders):
+        for bit in orders:
+            mine = mine + sums.astype(jnp.float32)
+            go = [i for i, j in enumerate(kept) if j & bit]
+            stay = [i for i, j in enumerate(kept) if not j & bit]
+            sent = jnp.stack([mine[i] for i in go]).astype(jnp.bfloat16)
+            mine = jnp.stack([mine[i] for i in stay])
+            kept = [kept[i] for i in stay]
+            sums = flip_col(sent, bit)
+        return mine, sums
 
     bits = [1 << b for b in range(n_col.bit_length() - 1)]
-    groups = [[(d, 0, half) for d in range(1, planes - 1)], [(planes - 1, at, half // 2) for at in (0, half // 2)]]
-    moved = w_band[1:]
-    blocks = [None] + [arrived(d, second + moved, 2) for d in range(1, planes - 1)]
-    after = [gate(moved + blocks[1][0] + blocks[1][1], GATE)]
-    n_slot = 0
-    came_back = []
-    for n_group, group in enumerate(groups):
-        if n_group:
-            blocks.append(arrived(planes - 1, after + came_back, 1))
-            after = [gate(blocks[planes - 1][1] + after, GATE2)]
-        work = []
-        for d, token, rows in group:
-            turned = n_slot % len(bits)
-            n_slot += 1
-            order = bits[turned:] + bits[:turned]
-            out = [j for j in js if j & order[0]]
-            kept = [j for j in js if not j & order[0]]
-            sent = products([w_band[j] for j in out], blocks[d], token, rows, jnp.bfloat16, after)
-            after = [sent]
-            came_back.append(flip_col(sent, order[0]))
-            work.append([d, token, rows, order, kept, came_back[-1]])
-        for item in work:
-            d, token, rows, order, kept, got = item
-            mine = products([w_band[j] for j in kept], blocks[d], token, rows, jnp.float32, after)
-            after = [mine]
-            item.append(mine)
-        for d, token, rows, order, kept, got, mine in work:
-            for n, bit in enumerate(order):
-                if n:
-                    got = flip_col(sent, bit)
-                mine = mine + got.astype(jnp.float32)
-                if n + 1 < len(order):
-                    nxt = order[n + 1]
-                    go = [i for i, j in enumerate(kept) if j & nxt]
-                    stay = [i for i, j in enumerate(kept) if not j & nxt]
-                    sent = jnp.stack([mine[i] for i in go]).astype(jnp.bfloat16)
-                    mine = jnp.stack([mine[i] for i in stay])
-                    kept = [kept[i] for i in stay]
-            done = mine[0].astype(jnp.bfloat16)
-            parts.append((2 * d, token, flip_row(done[:, :rows], 2 * d)))
-            parts.append((2 * d + 1, token, flip_row(done[:, rows:], 2 * d + 1)))
+    orders = [bits[i % len(bits) :] + bits[: i % len(bits)] for i in range(planes + 1)]
+    splits = [([j for j in js if j & o[0]], [j for j in js if not j & o[0]]) for o in orders]
+    last_j = n_col - 1
+
+    early = list(range(planes - 2, 0, -1))
+    blocks = {d: arrived(d, second + [w_band[last_j]]) for d in early}
+    firsts = products([([w_band[last_j]], blocks[d]) for d in early], jnp.bfloat16, [])
+    got_first = [flip_col(x, orders[i][0]) for i, x in enumerate(firsts)]
+    nexts = products(
+        [([w_band[j] for j in splits[i][0] if j != last_j], blocks[d]) for i, d in enumerate(early)],
+        jnp.bfloat16,
+        list(firsts[:1]),
+    )
+    got_next = [flip_col(x, orders[i][0]) for i, x in enumerate(nexts)]
+    mines = products(
+        [([w_band[j] for j in splits[i][1]], blocks[d]) for i, d in enumerate(early)],
+        jnp.float32,
+        list(nexts[:1]) + got_first,
+        KEPT,
+    )
+    def gather_sums(i, far, near):
+        came = {last_j: far[0]}
+        came.update(zip([j for j in splits[i][0] if j != last_j], near))
+        return jnp.stack([came[j | orders[i][0]] for j in splits[i][1]])
+
+    ended = []
+    for i, d in enumerate(early):
+        sums = gather_sums(i, got_first[i], got_next[i])
+        ended.append(totals(*halve(splits[i][1], mines[i], sums, orders[i][1:]), half, []))
+    swapped = [flip_row(other, 1) for _, other in ended[1:]]
+    both = arrived(planes - 1, [x for pair in ended for x in pair])
+    backs = []
+    for i, d in enumerate(early):
+        if i:
+            back = flip_row(jnp.stack([ended[i][0], swapped[i - 1]]), 2 * d)
+            backs.append(back)
+            parts.append((2 * d + 1, 0, back[1]))
+        else:
+            back = flip_row(jnp.stack(ended[i]), 2 * d)
+            hop = flip_row(jnp.concatenate([back[1], back[1][:, : half // 2]], axis=1), 1)
+            parts.append((2 * d + 1, 0, hop[:, :half]))
+        parts.append((2 * d, 0, back[0]))
+    sents = list(mines[:1])
+    late = []
+    for core in (0, 1):
+        i = len(early) + core
+        near_js = [j for j in splits[i][0] if j != last_j]
+        sents = products(
+            [([w_band[last_j]], [both[core]]), ([w_band[j] for j in near_js], [both[core]])], jnp.bfloat16, sents[:1]
+        )
+        late.append((i, core, [flip_col(x, orders[i][0]) for x in sents]))
+    late_mines = products(
+        [([w_band[j] for j in splits[i][1]], [both[core]]) for i, core, _ in late], jnp.float32, sents[:1]
+    )
+    for (i, core, got), mine in zip(late, late_mines):
+        (done,) = totals(
+            *halve(splits[i][1], mine, gather_sums(i, *got), orders[i][1:]), half, backs[: BACKS * core]
+        )
+        parts.append((2 * (planes - 1) + core, 0, flip_row(done, 2 * (planes - 1) + core)))
     return join(parts, half, qkv_bias)
 
 

time: 203 us -> 181 us (0.89)
  the two profiles are of different devices: /device:TPU:0 before, /device:TPU:17 now
where the time goes in v3:
time: 181 us; the launch traced here: 180 us
  waiting for transfers between devices  104 us (57%)
  starting transfers between devices  41.4 us (23%)
  Pallas kernels  33.4 us (18%)
    ppermute x5, waiting for transfers between devices, shards(): lax.ppermute(last[1 - parity], 'row', [(2 * a + c, 2 * b + c) for a, b in...  52.9 us
    ppermute x15, waiting for transfers between devices, flip_col(): return lax.ppermute(x, 'col', [(i, i ^ j) for i in range(n_col)])  29.1 us
    ppermute x11, waiting for transfers between devices, flip_row(): return lax.ppermute(x, 'row', [(i, i ^ j) for i in range(n_row)])  22.1 us
    ppermute x15, starting transfers between devices, flip_col(): return lax.ppermute(x, 'col', [(i, i ^ j) for i in range(n_col)])  17.3 us
    pallas_call x6, Pallas kernels, products(): pl.pallas_call(functools.partial(product_kernel, plan, len(arrays)), in_s...  16 us
    ppermute x11, starting transfers between devices, flip_row(): return lax.ppermute(x, 'row', [(i, i ^ j) for i in range(n_row)])  15.8 us
    pallas_call x1, Pallas kernels, deep_product(): pl.pallas_call(deep_kernel, grid=(depth // block,), in_specs=[pl.BlockSpe...  9.13 us
    ppermute x5, starting transfers between devices, shards(): lax.ppermute(last[1 - parity], 'row', [(2 * a + c, 2 * b + c) for a, b in...  8.3 us
  transfers between devices with their start and end apart: 31, of which 18 were waited for; matrix products, arithmetic and copies ran while one was open for 1% of the time, Pallas kernels for 17%

profile of v3, /device:TPU:17, one launch (start us, length us, event | category | flops | bytes accessed | tf_op | source)
XLA Modules:
  0.0 180.3 jit_solution(16730719775438363974)
XLA Ops:
  0.0 0.7 collective-permute-start
  0.7 2.2 %shard_map.38 = (bf16[256,3584]{1,0:T(8,128)(2,1)S(1)}, bf16[336,3584]{1,0:T(8,128)(2,1)S(1)}) custom-call(bf16[256,14336]{1,0:T(8,128)(2,1)} %refs_0_.1, bf16[336,14336]{1,0:T(8,128)(2,1)} %bitcast.18), custom_call_target="tpu_custom_call" | custom-call | tf_op jit(solution)/shard_map/pallas_call | solution.py:41
  2.9 1.4 collective-permute-start.3
  4.3 1.9 %collective-permute-start.4 = (bf16[256,3584]{1,0:T(8,128)(2,1)S(1)}, bf16[256,3584]{1,0:T(8,128)(2,1)S(1)}, u32[]{:S(2)}, u32[]{:S(2)}) collective-permute-start(bf16[256,3584]{1,0:T(8,128)(2,1)S(1)} %get-tuple-element.31), channel_id=1, source_target_pairs={{8,16},{12,20},{16,8},{20,12},{9,17},{13,21},{17,9},{21,13},{10,18... | collective-permute-start | bytes 5505032 | tf_op jit(solution)/shard_map/ppermute | solution.py:272
  6.2 2.2 %collective-permute-start.7 = (bf16[336,3584]{1,0:T(8,128)(2,1)S(1)}, bf16[336,3584]{1,0:T(8,128)(2,1)S(1)}, u32[]{:S(2)}, u32[]{:S(2)}) collective-permute-start(bf16[336,3584]{1,0:T(8,128)(2,1)S(1)} %get-tuple-element.28.refs_1_), channel_id=1, source_target_pairs={{0,3},{1,2},{2,1},{3,0},{4,7},{5,6},{6,5},{7,4},{8,11},{9,10},{10,... | collective-permute-start | bytes 7225352 | tf_op jit(solution)/shard_map/ppermute | solution.py:241
  8.4 3.7 %collective-permute-done.t1 = bf16[256,14336]{1,0:T(8,128)(2,1)S(1)} collective-permute-done((bf16[256,14336]{1,0:T(8,128)(2,1)}, bf16[256,14336]{1,0:T(8,128)(2,1)S(1)}, u32[]{:S(2)}, u32[]{:S(2)}) %collective-permute-start) | collective-permute-done | bytes 7340064 | tf_op jit(solution)/shard_map/ppermute | solution.py:244
  12.2 9.1 %shard_map.37 = bf16[336,512]{1,0:T(8,128)(2,1)S(1)} custom-call(bf16[336,14336]{1,0:T(8,128)(2,1)} %bitcast.19, bf16[256,14336]{1,0:T(8,128)(2,1)} %refs_0_.1, bf16[256,14336]{1,0:T(8,128)(2,1)S(1)} %collective-permute-done.t1), custom_call_target="tpu_custom_call" | custom-call | flops 4932501504 | bytes 24313856 | tf_op jit(solution)/shard_map/pallas_call | solution.py:137
  21.3 0.4 collective-permute-start.1
  21.8 3.2 %shard_map.39 = (bf16[336,3584]{1,0:T(8,128)(2,1)S(1)}, bf16[336,3584]{1,0:T(8,128)(2,1)S(1)}, bf16[336,3584]{1,0:T(8,128)(2,1)S(1)}) custom-call(bf16[336,14336]{1,0:T(8,128)(2,1)} %bitcast.20, bf16[336,3584]{1,0:T(8,128)(2,1)S(1)} %get-tuple-element.28.refs_1_), custom_call_target="tpu_custom_call" | custom-call | tf_op jit(solution)/shard_map/pallas_call | solution.py:41
  24.9 19.7 %collective-permute-done.3.refs_0_ = bf16[256,3584]{1,0:T(8,128)(2,1)S(1)} collective-permute-done((bf16[256,3584]{1,0:T(8,128)(2,1)S(1)}, bf16[256,3584]{1,0:T(8,128)(2,1)S(1)}, u32[]{:S(2)}, u32[]{:S(2)}) %collective-permute-start.3) | collective-permute-done | bytes 1835040 | tf_op jit(solution)/shard_map/ppermute | solution.py:272
  44.6 2.9 %collective-permute-done.4.refs_1_ = bf16[256,3584]{1,0:T(8,128)(2,1)S(1)} collective-permute-done((bf16[256,3584]{1,0:T(8,128)(2,1)S(1)}, bf16[256,3584]{1,0:T(8,128)(2,1)S(1)}, u32[]{:S(2)}, u32[]{:S(2)}) %collective-permute-start.4) | collective-permute-done | bytes 1835040 | tf_op jit(solution)/shard_map/ppermute | solution.py:272
  47.5 1.4 collective-permute-start.5
  48.9 2.2 %collective-permute-start.6 = (bf16[256,3584]{1,0:T(8,128)(2,1)S(1)}, bf16[256,3584]{1,0:T(8,128)(2,1)S(1)}, u32[]{:S(2)}, u32[]{:S(2)}) collective-permute-start(bf16[256,3584]{1,0:T(8,128)(2,1)S(1)} %get-tuple-element.33.refs_0_), channel_id=1, source_target_pairs={{8,16},{12,20},{16,8},{20,12},{9,17},{13,21},{17,9},{21,13},{10,18... | collective-permute-start | bytes 5505032 | tf_op jit(solution)/shard_map/ppermute | solution.py:272
  51.2 1.3 collective-permute-start.2
  52.5 1.2 collective-permute-start.9
  53.7 7.2 %collective-permute-done.7.refs_4_.refs_3_.refs_0_ = bf16[336,3584]{1,0:T(8,128)(2,1)S(1)} collective-permute-done((bf16[336,3584]{1,0:T(8,128)(2,1)S(1)}, bf16[336,3584]{1,0:T(8,128)(2,1)S(1)}, u32[]{:S(2)}, u32[]{:S(2)}) %collective-permute-start.7) | collective-permute-done | bytes 2408480 | tf_op jit(solution)/shard_map/ppermute | solution.py:241
  60.8 26.5 %collective-permute-done.5.refs_0_.refs_2_.refs_1_ = bf16[256,3584]{1,0:T(8,128)(2,1)S(1)} collective-permute-done((bf16[256,3584]{1,0:T(8,128)(2,1)S(1)}, bf16[256,3584]{1,0:T(8,128)(2,1)S(1)}, u32[]{:S(2)}, u32[]{:S(2)}) %collective-permute-start.5) | collective-permute-done | bytes 1835040 | tf_op jit(solution)/shard_map/ppermute | solution.py:272
  87.3 3.9 %collective-permute-done.6.refs_1_.refs_3_.refs_2_ = bf16[256,3584]{1,0:T(8,128)(2,1)S(1)} collective-permute-done((bf16[256,3584]{1,0:T(8,128)(2,1)S(1)}, bf16[256,3584]{1,0:T(8,128)(2,1)S(1)}, u32[]{:S(2)}, u32[]{:S(2)}) %collective-permute-start.6) | collective-permute-done | bytes 1835040 | tf_op jit(solution)/shard_map/ppermute | solution.py:272
  91.2 0.1 shard_map.41.refs_1_.refs_2_
  91.3 2.1 %collective-permute-start.8 = (bf16[256,3584]{1,0:T(8,128)(2,1)S(1)}, bf16[256,3584]{1,0:T(8,128)(2,1)S(1)}, u32[]{:S(2)}, u32[]{:S(2)}) collective-permute-start(bf16[256,3584]{1,0:T(8,128)(2,1)S(1)} %shard_map.41.refs_1_.refs_2_), channel_id=1, source_target_pairs={{0,4},{4,0},{8,12},{12,8},{16,20},{20,16},{24,28},{28,24},{1,5},{5... | collective-permute-start | bytes 5505032 | tf_op jit(solution)/shard_map/ppermute | solution.py:244
  93.4 0.1 shard_map.42.refs_3_.refs_4_.refs_5_
  93.6 0.1 collective-permute-start.10
  93.7 1.4 collective-permute-start.21
  95.1 1.8 collective-permute-done.8.refs_2_.refs_3_
  96.9 2.6 %collective-permute-done.10.refs_4_.refs_5_.refs_6_ = bf16[256,3584]{1,0:T(8,128)(2,1)S(1)} collective-permute-done((bf16[256,3584]{1,0:T(8,128)(2,1)S(1)}, bf16[256,3584]{1,0:T(8,128)(2,1)S(1)}, u32[]{:S(2)}, u32[]{:S(2)}) %collective-permute-start.10) | collective-permute-done | bytes 1835040 | tf_op jit(solution)/shard_map/ppermute | solution.py:244
  99.5 2.7 %shard_map.43 = (bf16[1,336,512]{2,1,0:T(8,128)(2,1)S(1)}, bf16[1,336,512]{2,1,0:T(8,128)(2,1)S(1)}) custom-call(bf16[336,3584]{1,0:T(8,128)(2,1)S(1)} %collective-permute-done.7.refs_4_.refs_3_.refs_0_, bf16[256,3584]{1,0:T(8,128)(2,1)S(1)} %shard_map.41.refs_1_.refs_2_, bf16[256,3584]{1,0:T(8,128)(2,1)S(1)} %collective-permute-done.8.refs_2_.refs_3_, ...), custom_call_target="tpu_custom_call" | custom-call | flops 344064 | bytes 344064 | tf_op jit(solution)/shard_map/pallas_call | solution.py:177
  102.2 1.3 collective-permute-start.11
  103.4 1.2 collective-permute-start.12
  104.7 8.3 %collective-permute-done.2.refs_3_.refs_1_.refs_2_ = bf16[336,3584]{1,0:T(8,128)(2,1)S(1)} collective-permute-done((bf16[336,3584]{1,0:T(8,128)(2,1)S(1)}, bf16[336,3584]{1,0:T(8,128)(2,1)S(1)}, u32[]{:S(2)}, u32[]{:S(2)}) %collective-permute-start.2) | collective-permute-done | bytes 2408480 | tf_op jit(solution)/shard_map/ppermute | solution.py:241
  113.0 2.7 %shard_map.44 = (bf16[1,336,512]{2,1,0:T(8,128)(2,1)S(1)}, bf16[1,336,512]{2,1,0:T(8,128)(2,1)S(1)}) custom-call(bf16[336,3584]{1,0:T(8,128)(2,1)S(1)} %collective-permute-done.9.refs_0_.refs_4_.refs_2_.refs_3_, bf16[256,3584]{1,0:T(8,128)(2,1)S(1)} %shard_map.41.refs_1_.refs_2_, bf16[256,3584]{1,0:T(8,128)(2,1)S(1)} %collective-permute-done.8.refs_2_.refs_3_, ...), custom_call_target="tpu_custom_call" | custom-call | flops 344064 | bytes 344064 | tf_op jit(solution)/shard_map/pallas_call | solution.py:177
  115.7 1.3 collective-permute-start.13
  117.0 1.2 collective-permute-start.17
  118.2 1.7 collective-permute-done.11.refs_8_
  119.9 0.5 collective-permute-done.12.refs_9_
  120.4 5.1 %shard_map.45 = (f32[2,336,512]{2,1,0:T(8,128)S(1)}, f32[2,336,512]{2,1,0:T(8,128)S(1)}) custom-call(bf16[336,3584]{1,0:T(8,128)(2,1)S(1)} %get-tuple-element.29.refs_3_.refs_0_, bf16[336,3584]{1,0:T(8,128)(2,1)S(1)} %collective-permute-done.2.refs_3_.refs_1_.refs_2_, bf16[256,3584]{1,0:T(8,128)(2,1)S(1)} %shard_map.41.refs_1_.refs_2_, ...), custom_call_target="tpu_custom_call" | custom-call | flops 4000688128 | bytes 688128 | tf_op jit(solution)/shard_map/pallas_call | solution.py:177
  125.5 1.7 collective-permute-done.13
  127.2 0.2 convert_add_fusion.1
  127.5 0.3 collective-permute-start.14
  127.8 0.2 convert_add_fusion
  128.1 1.3 collective-permute-start.18
  129.5 6.6 %collective-permute-done.14.got = bf16[1,336,512]{2,1,0:T(8,128)(2,1)S(1)} collective-permute-done((bf16[1,336,512]{2,1,0:T(8,128)(2,1)S(1)}, bf16[1,336,512]{2,1,0:T(8,128)(2,1)S(1)}, u32[]{:S(2)}, u32[]{:S(2)}) %collective-permute-start.14) | collective-permute-done | bytes 344096 | tf_op jit(solution)/shard_map/ppermute | solution.py:241
  136.1 0.2 collective-permute-done.18.got
  136.4 0.3 shard_map.48.refs_1_.refs_2_
  136.8 2.4 %collective-permute-start.22 = (bf16[256,3584]{1,0:T(8,128)(2,1)S(1)}, bf16[256,3584]{1,0:T(8,128)(2,1)S(1)}, u32[]{:S(2)}, u32[]{:S(2)}) collective-permute-start(bf16[256,3584]{1,0:T(8,128)(2,1)S(1)} %shard_map.48.refs_1_.refs_2_), channel_id=1, source_target_pairs={{0,4},{4,0},{8,12},{12,8},{16,20},{20,16},{24,28},{28,24},{1,5},{5... | collective-permute-start | bytes 5505032 | tf_op jit(solution)/shard_map/ppermute | solution.py:244
  139.2 1.4 shard_map.49
  140.6 1.3 collective-permute-start.24
  141.9 0.2 collective-permute-start.23
  142.3 0.5 collective-permute-done.19
  142.8 1.9 %collective-permute-start.20 = (bf16[2,336,256]{2,1,0:T(8,128)(2,1)S(1)}, bf16[2,336,256]{2,1,0:T(8,128)(2,1)S(1)}, u32[]{:S(2)}, u32[]{:S(2)}) collective-permute-start(bf16[2,336,256]{2,1,0:T(8,128)(2,1)S(1)} %pad_maximum_fusion.1), channel_id=1, source_target_pairs={{0,8},{4,12},{8,0},{12,4},{16,24},{20,28},{24,16},{28,20},{1,9},{5... | collective-permute-start | bytes 1032200 | tf_op jit(solution)/shard_map/ppermute | solution.py:244
  144.7 1.4 shard_map.50
  146.2 1.4 collective-permute-start.28
  147.5 2.7 %shard_map.51 = (f32[2,336,256]{2,1,0:T(8,128)S(1)}, f32[2,336,256]{2,1,0:T(8,128)S(1)}) custom-call(bf16[336,3584]{1,0:T(8,128)(2,1)S(1)} %get-tuple-element.29.refs_3_.refs_0_, bf16[336,3584]{1,0:T(8,128)(2,1)S(1)} %collective-permute-done.2.refs_3_.refs_1_.refs_2_, bf16[256,3584]{1,0:T(8,128)(2,1)S(1)} %shard_map.48.refs_1_.refs_2_, ...), custom_call_target="tpu_custom_call" | custom-call | flops 344064 | bytes 344064 | tf_op jit(solution)/shard_map/pallas_call | solution.py:177
  150.2 0.2 collective-permute-start.27
  150.4 0.1 convert_add_fusion.3
  150.6 1.4 collective-permute-start.25
  151.9 2.9 %collective-permute-done.27 = bf16[1,336,256]{2,1,0:T(8,128)(2,1)S(1)} collective-permute-done((bf16[1,336,256]{2,1,0:T(8,128)(2,1)S(1)}, bf16[1,336,256]{2,1,0:T(8,128)(2,1)S(1)}, u32[]{:S(2)}, u32[]{:S(2)}) %collective-permute-start.27) | collective-permute-done | bytes 172064 | tf_op jit(solution)/shard_map/ppermute | solution.py:241
  154.8 0.1 convert_add_fusion.2
  154.9 1.5 collective-permute-start.29
  156.5 4.4 %collective-permute-start.16 = (bf16[336,384]{1,0:T(8,128)(2,1)S(1)}, bf16[336,384]{1,0:T(8,128)(2,1)S(1)}, u32[]{:S(2)}, u32[]{:S(2)}) collective-permute-start(bf16[336,384]{1,0:T(8,128)(2,1)S(1)} %pad_maximum_fusion.2), channel_id=1, source_target_pairs={{0,4},{4,0},{8,12},{12,8},{16,20},{20,16},{24,28},{28,24},{1,5},{5... | collective-permute-start | bytes 774152 | tf_op jit(solution)/shard_map/ppermute | solution.py:244
  161.0 0.2 collective-permute-start.26
  161.3 3.5 %collective-permute-start.30 = (bf16[336,256]{1,0:T(8,128)(2,1)S(1)}, bf16[336,256]{1,0:T(8,128)(2,1)S(1)}, u32[]{:S(2)}, u32[]{:S(2)}) collective-permute-start(bf16[336,256]{1,0:T(8,128)(2,1)S(1)} %shard_map.53), channel_id=1, source_target_pairs={{0,28},{4,24},{8,20},{12,16},{16,12},{20,8},{24,4},{28,0},{1,29},{... | collective-permute-start | bytes 516104 | tf_op jit(solution)/shard_map/ppermute | solution.py:244
  164.8 9.6 %collective-permute-done.26.refs_6_ = bf16[336,256]{1,0:T(8,128)(2,1)S(1)} collective-permute-done((bf16[336,256]{1,0:T(8,128)(2,1)S(1)}, bf16[336,256]{1,0:T(8,128)(2,1)S(1)}, u32[]{:S(2)}, u32[]{:S(2)}) %collective-permute-start.26) | collective-permute-done | bytes 172064 | tf_op jit(solution)/shard_map/ppermute | solution.py:244
  174.5 3.8 %collective-permute-done.30.refs_7_ = bf16[336,256]{1,0:T(8,128)(2,1)S(1)} collective-permute-done((bf16[336,256]{1,0:T(8,128)(2,1)S(1)}, bf16[336,256]{1,0:T(8,128)(2,1)S(1)}, u32[]{:S(2)}, u32[]{:S(2)}) %collective-permute-start.30) | collective-permute-done | bytes 172064 | tf_op jit(solution)/shard_map/ppermute | solution.py:244
  178.3 2.0 %shard_map.54 = bf16[256,2688]{1,0:T(8,128)(2,1)} custom-call(bf16[336,256]{1,0:T(8,128)(2,1)S(1)} %get-tuple-element.56.refs_0_, bf16[336,256]{1,0:T(8,128)(2,1)S(1)} %collective-permute-done.1.refs_2_.refs_1_, bf16[336,256]{1,0:T(8,128)(2,1)S(1)} %slice.75.refs_2_, bf16[336,256]{1,0:T(8,128)(2,1)S(1)} %get-tuple-element.53.refs_3_, ...), custom_call_target="tpu_custom_call" | custom-call | flops 688128 | bytes 2752512 | tf_op jit(solution)/shard_map/pallas_call | solution.py:222
  (39 shorter events, 0.9 us)
Async XLA Ops:
  0.0 12.2 %collective-permute-start = (bf16[256,14336]{1,0:T(8,128)(2,1)}, bf16[256,14336]{1,0:T(8,128)(2,1)S(1)}, u32[]{:S(2)}, u32[]{:S(2)}) collective-permute-start(bf16[256,14336]{1,0:T(8,128)(2,1)} %refs_0_.1), channel_id=1, source_target_pairs={{0,4},{4,0},{8,12},{12,8},{16,20},{20,16},{24,28},{28,24},{1,5},{5... | collective-permute-start | bytes 22020104 | tf_op jit(solution)/shard_map/ppermute | solution.py:244
  2.9 41.7 %collective-permute-start.3 = (bf16[256,3584]{1,0:T(8,128)(2,1)S(1)}, bf16[256,3584]{1,0:T(8,128)(2,1)S(1)}, u32[]{:S(2)}, u32[]{:S(2)}) collective-permute-start(bf16[256,3584]{1,0:T(8,128)(2,1)S(1)} %get-tuple-element.31), channel_id=1, source_target_pairs={{0,8},{4,12},{8,0},{12,4},{16,24},{20,28},{24,16},{28,20},{1,9},{5... | collective-permute-start | bytes 5505032 | tf_op jit(solution)/shard_map/ppermute | solution.py:272
  4.3 43.2 %collective-permute-start.4 = (bf16[256,3584]{1,0:T(8,128)(2,1)S(1)}, bf16[256,3584]{1,0:T(8,128)(2,1)S(1)}, u32[]{:S(2)}, u32[]{:S(2)}) collective-permute-start(bf16[256,3584]{1,0:T(8,128)(2,1)S(1)} %get-tuple-element.31), channel_id=1, source_target_pairs={{8,16},{12,20},{16,8},{20,12},{9,17},{13,21},{17,9},{21,13},{10,18... | collective-permute-start | bytes 5505032 | tf_op jit(solution)/shard_map/ppermute | solution.py:272
  6.2 54.6 %collective-permute-start.7 = (bf16[336,3584]{1,0:T(8,128)(2,1)S(1)}, bf16[336,3584]{1,0:T(8,128)(2,1)S(1)}, u32[]{:S(2)}, u32[]{:S(2)}) collective-permute-start(bf16[336,3584]{1,0:T(8,128)(2,1)S(1)} %get-tuple-element.28.refs_1_), channel_id=1, source_target_pairs={{0,3},{1,2},{2,1},{3,0},{4,7},{5,6},{6,5},{7,4},{8,11},{9,10},{10,... | collective-permute-start | bytes 7225352 | tf_op jit(solution)/shard_map/ppermute | solution.py:241
  21.3 26.2 %collective-permute-start.1 = (bf16[336,256]{1,0:T(8,128)(2,1)S(1)}, bf16[336,256]{1,0:T(8,128)(2,1)S(1)}, u32[]{:S(2)}, u32[]{:S(2)}) collective-permute-start(bf16[336,256]{1,0:T(8,128)(2,1)S(1)} %get-tuple-element.55), channel_id=1, source_target_pairs={{0,4},{4,0},{8,12},{12,8},{16,20},{20,16},{24,28},{28,24},{1,5},{5... | collective-permute-start | bytes 516104 | tf_op jit(solution)/shard_map/ppermute | solution.py:244
  47.5 39.8 %collective-permute-start.5 = (bf16[256,3584]{1,0:T(8,128)(2,1)S(1)}, bf16[256,3584]{1,0:T(8,128)(2,1)S(1)}, u32[]{:S(2)}, u32[]{:S(2)}) collective-permute-start(bf16[256,3584]{1,0:T(8,128)(2,1)S(1)} %get-tuple-element.32.refs_0_), channel_id=1, source_target_pairs={{8,0},{12,4},{16,24},{20,28},{9,1},{13,5},{17,25},{21,29},{10,2},{... | collective-permute-start | bytes 5505032 | tf_op jit(solution)/shard_map/ppermute | solution.py:272
  48.9 42.3 %collective-permute-start.6 = (bf16[256,3584]{1,0:T(8,128)(2,1)S(1)}, bf16[256,3584]{1,0:T(8,128)(2,1)S(1)}, u32[]{:S(2)}, u32[]{:S(2)}) collective-permute-start(bf16[256,3584]{1,0:T(8,128)(2,1)S(1)} %get-tuple-element.33.refs_0_), channel_id=1, source_target_pairs={{8,16},{12,20},{16,8},{20,12},{9,17},{13,21},{17,9},{21,13},{10,18... | collective-permute-start | bytes 5505032 | tf_op jit(solution)/shard_map/ppermute | solution.py:272
  51.2 61.9 %collective-permute-start.2 = (bf16[336,3584]{1,0:T(8,128)(2,1)S(1)}, bf16[336,3584]{1,0:T(8,128)(2,1)S(1)}, u32[]{:S(2)}, u32[]{:S(2)}) collective-permute-start(bf16[336,3584]{1,0:T(8,128)(2,1)S(1)} %get-tuple-element.30), channel_id=1, source_target_pairs={{0,2},{1,3},{2,0},{3,1},{4,6},{5,7},{6,4},{7,5},{8,10},{9,11},{10,... | collective-permute-start | bytes 7225352 | tf_op jit(solution)/shard_map/ppermute | solution.py:241
  52.5 60.6 %collective-permute-start.9 = (bf16[336,3584]{1,0:T(8,128)(2,1)S(1)}, bf16[336,3584]{1,0:T(8,128)(2,1)S(1)}, u32[]{:S(2)}, u32[]{:S(2)}) collective-permute-start(bf16[336,3584]{1,0:T(8,128)(2,1)S(1)} %get-tuple-element.34), channel_id=1, source_target_pairs={{0,1},{1,0},{2,3},{3,2},{4,5},{5,4},{6,7},{7,6},{8,9},{9,8},{10,11... | collective-permute-start | bytes 7225352 | tf_op jit(solution)/shard_map/ppermute | solution.py:241
  91.3 5.5 %collective-permute-start.8 = (bf16[256,3584]{1,0:T(8,128)(2,1)S(1)}, bf16[256,3584]{1,0:T(8,128)(2,1)S(1)}, u32[]{:S(2)}, u32[]{:S(2)}) collective-permute-start(bf16[256,3584]{1,0:T(8,128)(2,1)S(1)} %shard_map.41.refs_1_.refs_2_), channel_id=1, source_target_pairs={{0,4},{4,0},{8,12},{12,8},{16,20},{20,16},{24,28},{28,24},{1,5},{5... | collective-permute-start | bytes 5505032 | tf_op jit(solution)/shard_map/ppermute | solution.py:244
  93.6 5.9 %collective-permute-start.10 = (bf16[256,3584]{1,0:T(8,128)(2,1)S(1)}, bf16[256,3584]{1,0:T(8,128)(2,1)S(1)}, u32[]{:S(2)}, u32[]{:S(2)}) collective-permute-start(bf16[256,3584]{1,0:T(8,128)(2,1)S(1)} %shard_map.42.refs_3_.refs_4_.refs_5_), channel_id=1, source_target_pairs={{0,4},{4,0},{8,12},{12,8},{16,20},{20,16},{24,28},{28,24},{1,5},{5... | collective-permute-start | bytes 5505032 | tf_op jit(solution)/shard_map/ppermute | solution.py:244
  93.7 42.7 %collective-permute-start.21 = (bf16[256,3584]{1,0:T(8,128)(2,1)S(1)}, bf16[256,3584]{1,0:T(8,128)(2,1)S(1)}, u32[]{:S(2)}, u32[]{:S(2)}) collective-permute-start(bf16[256,3584]{1,0:T(8,128)(2,1)S(1)} %collective-permute-done.6.refs_1_.refs_3_.refs_2_), channel_id=1, source_target_pairs={{8,0},{12,4},{16,24},{20,28},{9,1},{13,5},{17,25},{21,29},{10,2},{... | collective-permute-start | bytes 5505032 | tf_op jit(solution)/shard_map/ppermute | solution.py:272
  102.2 17.7 %collective-permute-start.11 = (bf16[1,336,512]{2,1,0:T(8,128)(2,1)S(1)}, bf16[1,336,512]{2,1,0:T(8,128)(2,1)S(1)}, u32[]{:S(2)}, u32[]{:S(2)}) collective-permute-start(bf16[1,336,512]{2,1,0:T(8,128)(2,1)S(1)} %get-tuple-element.35.refs_6_), channel_id=1, source_target_pairs={{0,1},{1,0},{2,3},{3,2},{4,5},{5,4},{6,7},{7,6},{8,9},{9,8},{10,11... | collective-permute-start | bytes 1032200 | tf_op jit(solution)/shard_map/ppermute | solution.py:241
  103.4 17.0 %collective-permute-start.12 = (bf16[1,336,512]{2,1,0:T(8,128)(2,1)S(1)}, bf16[1,336,512]{2,1,0:T(8,128)(2,1)S(1)}, u32[]{:S(2)}, u32[]{:S(2)}) collective-permute-start(bf16[1,336,512]{2,1,0:T(8,128)(2,1)S(1)} %get-tuple-element.37), channel_id=1, source_target_pairs={{0,2},{1,3},{2,0},{3,1},{4,6},{5,7},{6,4},{7,5},{8,10},{9,11},{10,... | collective-permute-start | bytes 1032200 | tf_op jit(solution)/shard_map/ppermute | solution.py:241
  115.7 11.6 %collective-permute-start.13 = (bf16[1,336,512]{2,1,0:T(8,128)(2,1)S(1)}, bf16[1,336,512]{2,1,0:T(8,128)(2,1)S(1)}, u32[]{:S(2)}, u32[]{:S(2)}) collective-permute-start(bf16[1,336,512]{2,1,0:T(8,128)(2,1)S(1)} %get-tuple-element.36.refs_7_), channel_id=1, source_target_pairs={{0,1},{1,0},{2,3},{3,2},{4,5},{5,4},{6,7},{7,6},{8,9},{9,8},{10,11... | collective-permute-start | bytes 1032200 | tf_op jit(solution)/shard_map/ppermute | solution.py:241
  117.0 10.9 %collective-permute-start.17 = (bf16[1,336,512]{2,1,0:T(8,128)(2,1)S(1)}, bf16[1,336,512]{2,1,0:T(8,128)(2,1)S(1)}, u32[]{:S(2)}, u32[]{:S(2)}) collective-permute-start(bf16[1,336,512]{2,1,0:T(8,128)(2,1)S(1)} %get-tuple-element.42), channel_id=1, source_target_pairs={{0,2},{1,3},{2,0},{3,1},{4,6},{5,7},{6,4},{7,5},{8,10},{9,11},{10,... | collective-permute-start | bytes 1032200 | tf_op jit(solution)/shard_map/ppermute | solution.py:241
  127.5 8.5 %collective-permute-start.14 = (bf16[1,336,512]{2,1,0:T(8,128)(2,1)S(1)}, bf16[1,336,512]{2,1,0:T(8,128)(2,1)S(1)}, u32[]{:S(2)}, u32[]{:S(2)}) collective-permute-start(bf16[1,336,512]{2,1,0:T(8,128)(2,1)S(1)} %slice.94), channel_id=1, source_target_pairs={{0,2},{1,3},{2,0},{3,1},{4,6},{5,7},{6,4},{7,5},{8,10},{9,11},{10,... | collective-permute-start | bytes 1032200 | tf_op jit(solution)/shard_map/ppermute | solution.py:241
  128.1 8.2 %collective-permute-start.18 = (bf16[1,336,512]{2,1,0:T(8,128)(2,1)S(1)}, bf16[1,336,512]{2,1,0:T(8,128)(2,1)S(1)}, u32[]{:S(2)}, u32[]{:S(2)}) collective-permute-start(bf16[1,336,512]{2,1,0:T(8,128)(2,1)S(1)} %slice.93), channel_id=1, source_target_pairs={{0,1},{1,0},{2,3},{3,2},{4,5},{5,4},{6,7},{7,6},{8,9},{9,8},{10,11... | collective-permute-start | bytes 1032200 | tf_op jit(solution)/shard_map/ppermute | solution.py:241
  136.8 7.9 %collective-permute-start.22 = (bf16[256,3584]{1,0:T(8,128)(2,1)S(1)}, bf16[256,3584]{1,0:T(8,128)(2,1)S(1)}, u32[]{:S(2)}, u32[]{:S(2)}) collective-permute-start(bf16[256,3584]{1,0:T(8,128)(2,1)S(1)} %shard_map.48.refs_1_.refs_2_), channel_id=1, source_target_pairs={{0,4},{4,0},{8,12},{12,8},{16,20},{20,16},{24,28},{28,24},{1,5},{5... | collective-permute-start | bytes 5505032 | tf_op jit(solution)/shard_map/ppermute | solution.py:244
  139.1 3.7 %collective-permute-start.19 = (bf16[336,256]{1,0:T(8,128)(2,1)S(1)}, bf16[336,256]{1,0:T(8,128)(2,1)S(1)}, u32[]{:S(2)}, u32[]{:S(2)}) collective-permute-start(bf16[336,256]{1,0:T(8,128)(2,1)S(1)} %get-tuple-element.44.refs_5_), channel_id=1, source_target_pairs={{0,4},{4,0},{8,12},{12,8},{16,20},{20,16},{24,28},{28,24},{1,5},{5... | collective-permute-start | bytes 516104 | tf_op jit(solution)/shard_map/ppermute | solution.py:244
  140.6 9.6 %collective-permute-start.24 = (bf16[1,336,256]{2,1,0:T(8,128)(2,1)S(1)}, bf16[1,336,256]{2,1,0:T(8,128)(2,1)S(1)}, u32[]{:S(2)}, u32[]{:S(2)}) collective-permute-start(bf16[1,336,256]{2,1,0:T(8,128)(2,1)S(1)} %get-tuple-element.45.refs_3_), channel_id=1, source_target_pairs={{0,1},{1,0},{2,3},{3,2},{4,5},{5,4},{6,7},{7,6},{8,9},{9,8},{10,11... | collective-permute-start | bytes 516104 | tf_op jit(solution)/shard_map/ppermute | solution.py:241
  141.9 8.5 %collective-permute-start.23 = (bf16[1,336,256]{2,1,0:T(8,128)(2,1)S(1)}, bf16[1,336,256]{2,1,0:T(8,128)(2,1)S(1)}, u32[]{:S(2)}, u32[]{:S(2)}) collective-permute-start(bf16[1,336,256]{2,1,0:T(8,128)(2,1)S(1)} %get-tuple-element.48), channel_id=1, source_target_pairs={{0,1},{1,0},{2,3},{3,2},{4,5},{5,4},{6,7},{7,6},{8,9},{9,8},{10,11... | collective-permute-start | bytes 516104 | tf_op jit(solution)/shard_map/ppermute | solution.py:241
  142.2 14.2 %collective-permute-start.15 = (bf16[2,336,256]{2,1,0:T(8,128)(2,1)S(1)}, bf16[2,336,256]{2,1,0:T(8,128)(2,1)S(1)}, u32[]{:S(2)}, u32[]{:S(2)}) collective-permute-start(bf16[2,336,256]{2,1,0:T(8,128)(2,1)S(1)} %pad_maximum_fusion), channel_id=1, source_target_pairs={{0,16},{4,20},{8,24},{12,28},{16,0},{20,4},{24,8},{28,12},{1,17},{... | collective-permute-start | bytes 1032200 | tf_op jit(solution)/shard_map/ppermute | solution.py:244
  142.8 18.4 %collective-permute-start.20 = (bf16[2,336,256]{2,1,0:T(8,128)(2,1)S(1)}, bf16[2,336,256]{2,1,0:T(8,128)(2,1)S(1)}, u32[]{:S(2)}, u32[]{:S(2)}) collective-permute-start(bf16[2,336,256]{2,1,0:T(8,128)(2,1)S(1)} %pad_maximum_fusion.1), channel_id=1, source_target_pairs={{0,8},{4,12},{8,0},{12,4},{16,24},{20,28},{24,16},{28,20},{1,9},{5... | collective-permute-start | bytes 1032200 | tf_op jit(solution)/shard_map/ppermute | solution.py:244
  146.2 5.8 %collective-permute-start.28 = (bf16[1,336,256]{2,1,0:T(8,128)(2,1)S(1)}, bf16[1,336,256]{2,1,0:T(8,128)(2,1)S(1)}, u32[]{:S(2)}, u32[]{:S(2)}) collective-permute-start(bf16[1,336,256]{2,1,0:T(8,128)(2,1)S(1)} %get-tuple-element.46.refs_5_), channel_id=1, source_target_pairs={{0,2},{1,3},{2,0},{3,1},{4,6},{5,7},{6,4},{7,5},{8,10},{9,11},{10,... | collective-permute-start | bytes 516104 | tf_op jit(solution)/shard_map/ppermute | solution.py:241
  150.2 4.6 %collective-permute-start.27 = (bf16[1,336,256]{2,1,0:T(8,128)(2,1)S(1)}, bf16[1,336,256]{2,1,0:T(8,128)(2,1)S(1)}, u32[]{:S(2)}, u32[]{:S(2)}) collective-permute-start(bf16[1,336,256]{2,1,0:T(8,128)(2,1)S(1)} %get-tuple-element.50), channel_id=1, source_target_pairs={{0,2},{1,3},{2,0},{3,1},{4,6},{5,7},{6,4},{7,5},{8,10},{9,11},{10,... | collective-permute-start | bytes 516104 | tf_op jit(solution)/shard_map/ppermute | solution.py:241
  150.5 10.4 %copy-start = (f32[2688]{0:T(1024)S(1)}, f32[2688]{0:T(1024)}, u32[]{:S(2)}) copy-start(f32[2688]{0:T(1024)} %param.5) | copy-start | bytes 32260
  150.6 10.4 %collective-permute-start.25 = (bf16[1,336,256]{2,1,0:T(8,128)(2,1)S(1)}, bf16[1,336,256]{2,1,0:T(8,128)(2,1)S(1)}, u32[]{:S(2)}, u32[]{:S(2)}) collective-permute-start(bf16[1,336,256]{2,1,0:T(8,128)(2,1)S(1)} %slice.96), channel_id=1, source_target_pairs={{0,2},{1,3},{2,0},{3,1},{4,6},{5,7},{6,4},{7,5},{8,10},{9,11},{10,... | collective-permute-start | bytes 516104 | tf_op jit(solution)/shard_map/ppermute | solution.py:241
  154.9 6.3 %collective-permute-start.29 = (bf16[1,336,256]{2,1,0:T(8,128)(2,1)S(1)}, bf16[1,336,256]{2,1,0:T(8,128)(2,1)S(1)}, u32[]{:S(2)}, u32[]{:S(2)}) collective-permute-start(bf16[1,336,256]{2,1,0:T(8,128)(2,1)S(1)} %slice.95), channel_id=1, source_target_pairs={{0,1},{1,0},{2,3},{3,2},{4,5},{5,4},{6,7},{7,6},{8,9},{9,8},{10,11... | collective-permute-start | bytes 516104 | tf_op jit(solution)/shard_map/ppermute | solution.py:241
  156.5 8.3 %collective-permute-start.16 = (bf16[336,384]{1,0:T(8,128)(2,1)S(1)}, bf16[336,384]{1,0:T(8,128)(2,1)S(1)}, u32[]{:S(2)}, u32[]{:S(2)}) collective-permute-start(bf16[336,384]{1,0:T(8,128)(2,1)S(1)} %pad_maximum_fusion.2), channel_id=1, source_target_pairs={{0,4},{4,0},{8,12},{12,8},{16,20},{20,16},{24,28},{28,24},{1,5},{5... | collective-permute-start | bytes 774152 | tf_op jit(solution)/shard_map/ppermute | solution.py:244
  161.0 13.4 %collective-permute-start.26 = (bf16[336,256]{1,0:T(8,128)(2,1)S(1)}, bf16[336,256]{1,0:T(8,128)(2,1)S(1)}, u32[]{:S(2)}, u32[]{:S(2)}) collective-permute-start(bf16[336,256]{1,0:T(8,128)(2,1)S(1)} %shard_map.52), channel_id=1, source_target_pairs={{0,24},{4,28},{8,16},{12,20},{16,8},{20,12},{24,0},{28,4},{1,25},{... | collective-permute-start | bytes 516104 | tf_op jit(solution)/shard_map/ppermute | solution.py:244
  161.3 17.0 %collective-permute-start.30 = (bf16[336,256]{1,0:T(8,128)(2,1)S(1)}, bf16[336,256]{1,0:T(8,128)(2,1)S(1)}, u32[]{:S(2)}, u32[]{:S(2)}) collective-permute-start(bf16[336,256]{1,0:T(8,128)(2,1)S(1)} %shard_map.53), channel_id=1, source_target_pairs={{0,28},{4,24},{8,20},{12,16},{16,12},{20,8},{24,4},{28,0},{1,29},{... | collective-permute-start | bytes 516104 | tf_op jit(solution)/shard_map/ppermute | solution.py:244

commit v4 on v3

--- a/solution.py
+++ b/solution.py
@@ -8,9 +8,8 @@
 from jax.sharding import PartitionSpec as P
 
 ROOM = 14 * 1024 * 1024
-SPACE = 0
 KEPT = 4_000_000_000
-BACKS = 9
+BACKS = 0
 IN_VMEM = pl.BlockSpec(memory_space=pltpu.VMEM)
 IN_HBM = pl.BlockSpec(memory_space=pltpu.HBM)
 ANYWHERE = pl.BlockSpec(memory_space=pl.ANY)
@@ -85,7 +84,7 @@
     pass
 
 
-def passed(xs, after, flops):
+def passed(xs, after):
     return pl.pallas_call(
         pass_kernel,
         out_shape=[jax.ShapeDtypeStruct(x.shape, x.dtype) for x in xs],
@@ -93,7 +92,6 @@
         out_specs=[ANYWHERE] * len(xs),
         input_output_aliases={i: i for i in range(len(xs))},
         compiler_params=pltpu.CompilerParams(vmem_limit_bytes=ROOM),
-        cost_estimate=pl.CostEstimate(flops=flops, bytes_accessed=0, transcendentals=0),
     )(*xs, *after)
 
 
@@ -208,9 +206,12 @@
     n = len(places)
     part_refs, bias_ref, out_ref, joined = refs[:n], refs[n], refs[n + 1], refs[n + 2]
     me = lax.axis_index("row")
-    for (j, token), part in zip(places, part_refs):
-        m, rows = part.shape
-        joined[pl.ds(pl.multiple_of((me ^ j) * m, 8), m), token : token + rows] = part[...].astype(jnp.float32)
+    plane, core = me // 2, me % 2
+    for (came, other), part in zip(places, part_refs):
+        m = part.shape[0]
+        source = functools.reduce(lambda x, p: jnp.where(plane == p, came[p], x), range(1, len(came)), came[0])
+        start = pl.multiple_of((2 * source + (core ^ other)) * m, 8)
+        joined[pl.ds(start, m), :] = part[...].astype(jnp.float32)
     block = divisor(out_ref.shape[1], 512)
     for i in range(out_ref.shape[1] // block):
         cols = slice(i * block, (i + 1) * block)
@@ -220,7 +221,7 @@
 def join(parts, rows, bias):
     width = bias.shape[0]
     return pl.pallas_call(
-        functools.partial(join_kernel, [(j, token) for j, token, _ in parts]),
+        functools.partial(join_kernel, [(came, other) for came, other, _ in parts]),
         out_shape=jax.ShapeDtypeStruct((rows, width), jnp.bfloat16),
         in_specs=[IN_VMEM] * (len(parts) + 1),
         out_specs=IN_VMEM,
@@ -230,33 +231,13 @@
     )(*[part for _, _, part in parts], bias[None, :])
 
 
-def shards(tokens, qkv_weight, qkv_bias):
-    n_row, n_col = lax.axis_size("row"), lax.axis_size("col")
-    planes = n_row // 2
-    half, feats = tokens.shape
-    weight = qkv_weight.reshape(feats, -1).T
-    columns = weight.shape[0]
-
-    def flip_col(x, j):
-        return lax.ppermute(x, "col", [(i, i ^ j) for i in range(n_col)])
-
-    def flip_row(x, j):
-        return lax.ppermute(x, "row", [(i, i ^ j) for i in range(n_row)])
-
-    js = list(range(n_col))
-    own, far = bands([tokens, weight], [(0, 0, 0, half), (1, n_col - 1, 0, columns)], n_col, [])
-    near = bands([weight], [(0, j, 0, columns) for j in js[:-1]], n_col, [far])
-    w_band = [near[0]] + [flip_col(x, j) for j, x in zip(js[1:], list(near[1:]) + [far])]
-    here = deep_product(weight, tokens, flip_row(tokens, 1))
-    here_other = flip_row(here[:, half:], 1)
-    parts = [(0, 0, here[:, :half]), (1, 0, here_other)]
-
+def chain(own, planes, send, after):
     held = []
     last = {0: own, 1: own}
     second = []
     for s in range(1, planes):
         if s == 2:
-            last = dict(enumerate(passed([last[0], last[1]], [here_other, near[0]], SPACE)))
+            last = dict(enumerate(passed([last[0], last[1]], after)))
             held = [(last[i], came) for i, (_, came) in enumerate(held)]
         now = {}
         for parity in (0, 1):
@@ -269,18 +250,72 @@
                     pairs.append((p + 1, p))
                     came[p] = p + s
             if pairs:
-                now[parity] = lax.ppermute(
-                    last[1 - parity], "row", [(2 * a + c, 2 * b + c) for a, b in pairs for c in (0, 1)]
-                )
+                now[parity] = send(last[1 - parity], pairs)
                 held.append((now[parity], came))
                 if s == 2:
                     second.append(now[parity])
         last = now
-
-    def arrived(d, after):
+    slots = []
+    for d in range(planes - 2, 0, -1) if planes > 2 else ():
+        slots.append(d)
+    found = []
+    for d in slots + [planes - 1]:
         wanted = [next(i for i, (_, came) in enumerate(held) if came.get(p) == p ^ d) for p in range(planes)]
         used = sorted(set(wanted))
-        (value,) = choose([held[i][0] for i in used], [used.index(i) for i in wanted], after, 1)
+        found.append(([held[i][0] for i in used], [used.index(i) for i in wanted], [p ^ d for p in range(planes)]))
+    return found, second
+
+
+def line_of_four(own, send, after):
+    ends = [0, 1, 1, 0]
+    swap = [(0, 1), (1, 0), (2, 3), (3, 2)]
+    cross = send(own, [(0, 3), (3, 0)])
+    (out,) = choose([cross, own], ends, after, 1)
+    near = send(out, swap)
+    inner = send(out, [(1, 2), (2, 1)])
+    (out,) = choose([own, inner], ends, [near], 1)
+    final = send(out, swap)
+    slots = [
+        ([cross, inner], ends, [3, 2, 1, 0]),
+        ([near], [0, 0, 0, 0], [1, 3, 0, 2]),
+        ([final], [0, 0, 0, 0], [2, 0, 3, 1]),
+    ]
+    return slots, [near, inner]
+
+
+def shards(tokens, qkv_weight, qkv_bias):
+    n_row, n_col = lax.axis_size("row"), lax.axis_size("col")
+    planes = n_row // 2
+    half, feats = tokens.shape
+    weight = qkv_weight.reshape(feats, -1).T
+    columns = weight.shape[0]
+
+    def flip_col(x, j):
+        return lax.ppermute(x, "col", [(i, i ^ j) for i in range(n_col)])
+
+    def flip_row(x, j):
+        return lax.ppermute(x, "row", [(i, i ^ j) for i in range(n_row)])
+
+    js = list(range(n_col))
+    own, far = bands([tokens, weight], [(0, 0, 0, half), (1, n_col - 1, 0, columns)], n_col, [])
+    near = bands([weight], [(0, j, 0, columns) for j in js[:-1]], n_col, [far])
+    w_band = [near[0]] + [flip_col(x, j) for j, x in zip(js[1:], list(near[1:]) + [far])]
+    here = deep_product(weight, tokens, flip_row(tokens, 1))
+    here_other = flip_row(here[:, half:], 1)
+    everyone = list(range(planes))
+    parts = [(everyone, 0, here[:, :half]), (everyone, 1, here_other)]
+
+    def send(x, pairs):
+        return lax.ppermute(x, "row", [(2 * a + c, 2 * b + c) for a, b in pairs for c in (0, 1)])
+
+    if planes == 4:
+        slots, second = line_of_four(own, send, [here_other, near[0]])
+    else:
+        slots, second = chain(own, planes, send, [here_other, near[0]])
+
+    def arrived(slot, after):
+        arrays, wanted, _ = slot
+        (value,) = choose(arrays, wanted, after, 1)
         return [value, flip_row(value, 1)]
 
     def halve(kept, mine, sums, orders):
@@ -299,8 +334,8 @@
     splits = [([j for j in js if j & o[0]], [j for j in js if not j & o[0]]) for o in orders]
     last_j = n_col - 1
 
-    early = list(range(planes - 2, 0, -1))
-    blocks = {d: arrived(d, second + [w_band[last_j]]) for d in early}
+    early = list(range(planes - 2))
+    blocks = {d: arrived(slots[d], second + [w_band[last_j]]) for d in early}
     firsts = products([([w_band[last_j]], blocks[d]) for d in early], jnp.bfloat16, [])
     got_first = [flip_col(x, orders[i][0]) for i, x in enumerate(firsts)]
     nexts = products(
@@ -325,18 +360,20 @@
         sums = gather_sums(i, got_first[i], got_next[i])
         ended.append(totals(*halve(splits[i][1], mines[i], sums, orders[i][1:]), half, []))
     swapped = [flip_row(other, 1) for _, other in ended[1:]]
-    both = arrived(planes - 1, [x for pair in ended for x in pair])
+    both = arrived(slots[-1], [x for pair in ended for x in pair])
     backs = []
-    for i, d in enumerate(early):
+    for i, slot in enumerate(slots[:-1]):
+        home = [(p, c) for p, c in enumerate(slot[2])]
+        source = [slot[2].index(c) for c in everyone]
         if i:
-            back = flip_row(jnp.stack([ended[i][0], swapped[i - 1]]), 2 * d)
+            back = send(jnp.stack([ended[i][0], swapped[i - 1]]), home)
             backs.append(back)
-            parts.append((2 * d + 1, 0, back[1]))
+            parts.append((source, 1, back[1]))
         else:
-            back = flip_row(jnp.stack(ended[i]), 2 * d)
+            back = send(jnp.stack(ended[i]), home)
             hop = flip_row(jnp.concatenate([back[1], back[1][:, : half // 2]], axis=1), 1)
-            parts.append((2 * d + 1, 0, hop[:, :half]))
-        parts.append((2 * d, 0, back[0]))
+            parts.append((source, 1, hop[:, :half]))
+        parts.append((source, 0, back[0]))
     sents = list(mines[:1])
     late = []
     for core in (0, 1):
@@ -353,7 +390,9 @@
         (done,) = totals(
             *halve(splits[i][1], mine, gather_sums(i, *got), orders[i][1:]), half, backs[: BACKS * core]
         )
-        parts.append((2 * (planes - 1) + core, 0, flip_row(done, 2 * (planes - 1) + core)))
+        home = [(2 * p + c, 2 * q + (c ^ core)) for p, q in enumerate(slots[-1][2]) for c in (0, 1)]
+        source = [slots[-1][2].index(q) for q in everyone]
+        parts.append((source, core, lax.ppermute(done, "row", home)))
     return join(parts, half, qkv_bias)
 
 

time: 181 us -> 178 us (0.983)
  the two profiles are of different devices: /device:TPU:17 before, /device:TPU:0 now
where the time goes in v4:
time: 178 us; the launch traced here: 177 us
  waiting for transfers between devices  105 us (59%)
  starting transfers between devices  37.7 us (21%)
  Pallas kernels  33.5 us (19%)
    ppermute x6, waiting for transfers between devices, send(): lax.ppermute(x, 'row', [(2 * a + c, 2 * b + c) for a, b in pairs for c in...  53.3 us
    ppermute x15, waiting for transfers between devices, flip_col(): return lax.ppermute(x, 'col', [(i, i ^ j) for i in range(n_col)])  43 us
    ppermute x15, starting transfers between devices, flip_col(): return lax.ppermute(x, 'col', [(i, i ^ j) for i in range(n_col)])  20.5 us
    pallas_call x6, Pallas kernels, products(): pl.pallas_call(functools.partial(product_kernel, plan, len(arrays)), in_s...  16 us
    ppermute x6, starting transfers between devices, send(): lax.ppermute(x, 'row', [(2 * a + c, 2 * b + c) for a, b in pairs for c in...  12.3 us
    pallas_call x1, Pallas kernels, deep_product(): pl.pallas_call(deep_kernel, grid=(depth // block,), in_specs=[pl.BlockSpe...  9.13 us
    ppermute x2, waiting for transfers between devices, shards(): parts.append((source, core, lax.ppermute(done, 'row', home)))  7.11 us
    pallas_call x2, Pallas kernels, bands(): pl.pallas_call(functools.partial(bands_kernel, pieces, n_col, len(xs)), o...  5.41 us
  transfers between devices with their start and end apart: 30, of which 19 were waited for; matrix products, arithmetic and copies ran while one was open for 1% of the time, Pallas kernels for 18%

profile of v4, /device:TPU:0, one launch (start us, length us, event | category | flops | bytes accessed | tf_op | source)
XLA Modules:
  0.0 177.4 jit_solution(4778608980595839403)
XLA Ops:
  0.0 0.5 collective-permute-start
  0.5 2.2 %shard_map.38 = (bf16[256,3584]{1,0:T(8,128)(2,1)S(1)}, bf16[336,3584]{1,0:T(8,128)(2,1)S(1)}) custom-call(bf16[256,14336]{1,0:T(8,128)(2,1)} %refs_0_.1, bf16[336,14336]{1,0:T(8,128)(2,1)} %bitcast.18), custom_call_target="tpu_custom_call" | custom-call | tf_op jit(solution)/shard_map/pallas_call | solution.py:40
  2.7 6.5 %collective-permute-start.3 = (bf16[256,3584]{1,0:T(8,128)(2,1)S(1)}, bf16[256,3584]{1,0:T(8,128)(2,1)S(1)}, u32[]{:S(2)}, u32[]{:S(2)}) collective-permute-start(bf16[256,3584]{1,0:T(8,128)(2,1)S(1)} %get-tuple-element.29.refs_1_.refs_0_), channel_id=1, source_target_pairs={{0,24},{4,28},{24,0},{28,4},{1,25},{5,29},{25,1},{29,5},{2,26},{6,... | collective-permute-start | bytes 5505032 | tf_op jit(solution)/shard_map/ppermute | solution.py:309
  9.2 2.5 %collective-permute-start.6 = (bf16[336,3584]{1,0:T(8,128)(2,1)S(1)}, bf16[336,3584]{1,0:T(8,128)(2,1)S(1)}, u32[]{:S(2)}, u32[]{:S(2)}) collective-permute-start(bf16[336,3584]{1,0:T(8,128)(2,1)S(1)} %get-tuple-element.26.refs_1_), channel_id=1, source_target_pairs={{0,3},{1,2},{2,1},{3,0},{4,7},{5,6},{6,5},{7,4},{8,11},{9,10},{10,... | collective-permute-start | bytes 7225352 | tf_op jit(solution)/shard_map/ppermute | solution.py:294
  11.7 0.2 collective-permute-done.t1
  11.9 9.1 %shard_map.37 = bf16[336,512]{1,0:T(8,128)(2,1)S(1)} custom-call(bf16[336,14336]{1,0:T(8,128)(2,1)} %bitcast.19, bf16[256,14336]{1,0:T(8,128)(2,1)} %refs_0_.1, bf16[256,14336]{1,0:T(8,128)(2,1)S(1)} %collective-permute-done.t1), custom_call_target="tpu_custom_call" | custom-call | flops 4932501504 | bytes 24313856 | tf_op jit(solution)/shard_map/pallas_call | solution.py:135
  21.1 0.4 collective-permute-start.1
  21.6 3.2 %shard_map.39 = (bf16[336,3584]{1,0:T(8,128)(2,1)S(1)}, bf16[336,3584]{1,0:T(8,128)(2,1)S(1)}, bf16[336,3584]{1,0:T(8,128)(2,1)S(1)}) custom-call(bf16[336,14336]{1,0:T(8,128)(2,1)} %bitcast.20, bf16[336,3584]{1,0:T(8,128)(2,1)S(1)} %get-tuple-element.26.refs_1_), custom_call_target="tpu_custom_call" | custom-call | tf_op jit(solution)/shard_map/pallas_call | solution.py:40
  24.7 25.2 %collective-permute-done.3.refs_0_ = bf16[256,3584]{1,0:T(8,128)(2,1)S(1)} collective-permute-done((bf16[256,3584]{1,0:T(8,128)(2,1)S(1)}, bf16[256,3584]{1,0:T(8,128)(2,1)S(1)}, u32[]{:S(2)}, u32[]{:S(2)}) %collective-permute-start.3) | collective-permute-done | bytes 1835040 | tf_op jit(solution)/shard_map/ppermute | solution.py:309
  49.9 0.1 shard_map.40
  50.1 0.8 collective-permute-start.4
  50.9 1.6 collective-permute-start.2
  52.5 1.5 collective-permute-start.8
  54.0 11.4 %collective-permute-done.6.refs_4_.refs_3_.refs_0_ = bf16[336,3584]{1,0:T(8,128)(2,1)S(1)} collective-permute-done((bf16[336,3584]{1,0:T(8,128)(2,1)S(1)}, bf16[336,3584]{1,0:T(8,128)(2,1)S(1)}, u32[]{:S(2)}, u32[]{:S(2)}) %collective-permute-start.6) | collective-permute-done | bytes 2408480 | tf_op jit(solution)/shard_map/ppermute | solution.py:294
  65.4 26.6 %collective-permute-done.5.refs_2_.refs_0_.refs_1_ = bf16[256,3584]{1,0:T(8,128)(2,1)S(1)} collective-permute-done((bf16[256,3584]{1,0:T(8,128)(2,1)S(1)}, bf16[256,3584]{1,0:T(8,128)(2,1)S(1)}, u32[]{:S(2)}, u32[]{:S(2)}) %collective-permute-start.5) | collective-permute-done | bytes 1835040 | tf_op jit(solution)/shard_map/ppermute | solution.py:309
  92.0 0.1 shard_map.42.refs_3_.refs_4_.refs_5_
  92.2 0.2 shard_map.41.refs_1_.refs_2_
  92.3 0.5 collective-permute-start.7
  92.9 0.1 shard_map.48
  93.0 4.4 %collective-permute-start.20 = (bf16[256,3584]{1,0:T(8,128)(2,1)S(1)}, bf16[256,3584]{1,0:T(8,128)(2,1)S(1)}, u32[]{:S(2)}, u32[]{:S(2)}) collective-permute-start(bf16[256,3584]{1,0:T(8,128)(2,1)S(1)} %shard_map.48), channel_id=1, source_target_pairs={{0,8},{4,12},{8,0},{12,4},{16,24},{20,28},{24,16},{28,20},{1,9},{5... | collective-permute-start | bytes 5505032 | tf_op jit(solution)/shard_map/ppermute | solution.py:309
  97.4 1.2 collective-permute-done.7.refs_2_.refs_3_
  98.6 2.7 %shard_map.43 = (bf16[1,336,512]{2,1,0:T(8,128)(2,1)S(1)}, bf16[1,336,512]{2,1,0:T(8,128)(2,1)S(1)}) custom-call(bf16[336,3584]{1,0:T(8,128)(2,1)S(1)} %collective-permute-done.6.refs_4_.refs_3_.refs_0_, bf16[256,3584]{1,0:T(8,128)(2,1)S(1)} %shard_map.41.refs_1_.refs_2_, bf16[256,3584]{1,0:T(8,128)(2,1)S(1)} %collective-permute-done.7.refs_2_.refs_3_, ...), custom_call_target="tpu_custom_call" | custom-call | flops 344064 | bytes 344064 | tf_op jit(solution)/shard_map/pallas_call | solution.py:175
  101.3 1.5 collective-permute-start.11
  102.7 1.5 collective-permute-start.10
  104.2 12.1 %collective-permute-done.2.refs_3_.refs_1_.refs_2_ = bf16[336,3584]{1,0:T(8,128)(2,1)S(1)} collective-permute-done((bf16[336,3584]{1,0:T(8,128)(2,1)S(1)}, bf16[336,3584]{1,0:T(8,128)(2,1)S(1)}, u32[]{:S(2)}, u32[]{:S(2)}) %collective-permute-start.2) | collective-permute-done | bytes 2408480 | tf_op jit(solution)/shard_map/ppermute | solution.py:294
  116.3 0.7 collective-permute-done.8.refs_0_.refs_4_.refs_2_.refs_3_
  117.0 2.7 %shard_map.44 = (bf16[1,336,512]{2,1,0:T(8,128)(2,1)S(1)}, bf16[1,336,512]{2,1,0:T(8,128)(2,1)S(1)}) custom-call(bf16[336,3584]{1,0:T(8,128)(2,1)S(1)} %collective-permute-done.8.refs_0_.refs_4_.refs_2_.refs_3_, bf16[256,3584]{1,0:T(8,128)(2,1)S(1)} %shard_map.41.refs_1_.refs_2_, bf16[256,3584]{1,0:T(8,128)(2,1)S(1)} %collective-permute-done.7.refs_2_.refs_3_, ...), custom_call_target="tpu_custom_call" | custom-call | flops 344064 | bytes 344064 | tf_op jit(solution)/shard_map/pallas_call | solution.py:175
  119.7 0.9 collective-permute-start.16
  120.6 1.5 collective-permute-start.12
  122.1 1.6 collective-permute-done.11.refs_9_
  123.7 0.7 collective-permute-done.10.refs_8_
  124.4 5.1 %shard_map.45 = (f32[2,336,512]{2,1,0:T(8,128)S(1)}, f32[2,336,512]{2,1,0:T(8,128)S(1)}) custom-call(bf16[336,3584]{1,0:T(8,128)(2,1)S(1)} %get-tuple-element.27.refs_3_.refs_0_, bf16[336,3584]{1,0:T(8,128)(2,1)S(1)} %collective-permute-done.2.refs_3_.refs_1_.refs_2_, bf16[256,3584]{1,0:T(8,128)(2,1)S(1)} %shard_map.41.refs_1_.refs_2_, ...), custom_call_target="tpu_custom_call" | custom-call | flops 4000688128 | bytes 688128 | tf_op jit(solution)/shard_map/pallas_call | solution.py:175
  129.6 1.4 collective-permute-done.16
  131.0 0.2 convert_add_fusion
  131.3 1.6 collective-permute-start.17
  132.8 0.2 convert_add_fusion.1
  133.1 1.6 collective-permute-start.13
  134.8 6.5 %collective-permute-done.17.got = bf16[1,336,512]{2,1,0:T(8,128)(2,1)S(1)} collective-permute-done((bf16[1,336,512]{2,1,0:T(8,128)(2,1)S(1)}, bf16[1,336,512]{2,1,0:T(8,128)(2,1)S(1)}, u32[]{:S(2)}, u32[]{:S(2)}) %collective-permute-start.17) | collective-permute-done | bytes 344096 | tf_op jit(solution)/shard_map/ppermute | solution.py:294
  141.4 1.5 collective-permute-done.13.got
  142.9 0.2 shard_map.49.refs_1_.refs_2_
  143.2 0.5 collective-permute-start.18
  143.7 1.4 shard_map.50
  145.1 0.6 collective-permute-start.22
  145.7 1.5 collective-permute-start.23
  147.3 0.3 collective-permute-start.14
  147.6 0.2 collective-permute-start.19
  147.9 1.4 shard_map.51
  149.4 1.6 collective-permute-start.27
  150.9 2.7 %shard_map.52 = (f32[2,336,256]{2,1,0:T(8,128)S(1)}, f32[2,336,256]{2,1,0:T(8,128)S(1)}) custom-call(bf16[336,3584]{1,0:T(8,128)(2,1)S(1)} %get-tuple-element.27.refs_3_.refs_0_, bf16[336,3584]{1,0:T(8,128)(2,1)S(1)} %collective-permute-done.2.refs_3_.refs_1_.refs_2_, bf16[256,3584]{1,0:T(8,128)(2,1)S(1)} %shard_map.49.refs_1_.refs_2_, ...), custom_call_target="tpu_custom_call" | custom-call | flops 344064 | bytes 344064 | tf_op jit(solution)/shard_map/pallas_call | solution.py:175
  153.6 0.6 collective-permute-start.26
  154.2 1.0 collective-permute-done.23
  155.2 0.1 convert_add_fusion.3
  155.4 1.6 collective-permute-start.24
  157.0 4.0 %collective-permute-done.26 = bf16[1,336,256]{2,1,0:T(8,128)(2,1)S(1)} collective-permute-done((bf16[1,336,256]{2,1,0:T(8,128)(2,1)S(1)}, bf16[1,336,256]{2,1,0:T(8,128)(2,1)S(1)}, u32[]{:S(2)}, u32[]{:S(2)}) %collective-permute-start.26) | collective-permute-done | bytes 172064 | tf_op jit(solution)/shard_map/ppermute | solution.py:294
  161.0 0.1 convert_add_fusion.2
  161.1 0.6 collective-permute-start.28
  161.8 0.1 collective-permute-start.15
  161.9 1.2 collective-permute-done.24.got
  163.2 2.7 %collective-permute-start.25 = (bf16[336,256]{1,0:T(8,128)(2,1)S(1)}, bf16[336,256]{1,0:T(8,128)(2,1)S(1)}, u32[]{:S(2)}, u32[]{:S(2)}) collective-permute-start(bf16[336,256]{1,0:T(8,128)(2,1)S(1)} %shard_map.53), channel_id=1, source_target_pairs={{0,16},{4,20},{8,0},{12,4},{16,24},{20,28},{24,8},{28,12},{1,17},{... | collective-permute-start | bytes 516104 | tf_op jit(solution)/shard_map/ppermute | solution.py:395
  165.9 0.7 collective-permute-done.28.got
  166.7 1.5 collective-permute-done.19
  168.3 3.6 %collective-permute-done.25.refs_6_ = bf16[336,256]{1,0:T(8,128)(2,1)S(1)} collective-permute-done((bf16[336,256]{1,0:T(8,128)(2,1)S(1)}, bf16[336,256]{1,0:T(8,128)(2,1)S(1)}, u32[]{:S(2)}, u32[]{:S(2)}) %collective-permute-start.25) | collective-permute-done | bytes 172064 | tf_op jit(solution)/shard_map/ppermute | solution.py:395
  171.9 3.5 %collective-permute-done.29.refs_7_ = bf16[336,256]{1,0:T(8,128)(2,1)S(1)} collective-permute-done((bf16[336,256]{1,0:T(8,128)(2,1)S(1)}, bf16[336,256]{1,0:T(8,128)(2,1)S(1)}, u32[]{:S(2)}, u32[]{:S(2)}) %collective-permute-start.29) | collective-permute-done | bytes 172064 | tf_op jit(solution)/shard_map/ppermute | solution.py:395
  175.4 2.1 %shard_map.55 = bf16[256,2688]{1,0:T(8,128)(2,1)} custom-call(bf16[336,256]{1,0:T(8,128)(2,1)S(1)} %get-tuple-element.52.refs_0_, bf16[336,256]{1,0:T(8,128)(2,1)S(1)} %collective-permute-done.1.refs_2_.refs_1_, bf16[336,256]{1,0:T(8,128)(2,1)S(1)} %slice.75.refs_2_, bf16[336,256]{1,0:T(8,128)(2,1)S(1)} %get-tuple-element.49.refs_3_, ...), custom_call_target="tpu_custom_call" | custom-call | flops 688128 | bytes 2752512 | tf_op jit(solution)/shard_map/pallas_call | solution.py:223
  (38 shorter events, 1.0 us)
Async XLA Ops:
  0.0 11.9 %collective-permute-start = (bf16[256,14336]{1,0:T(8,128)(2,1)}, bf16[256,14336]{1,0:T(8,128)(2,1)S(1)}, u32[]{:S(2)}, u32[]{:S(2)}) collective-permute-start(bf16[256,14336]{1,0:T(8,128)(2,1)} %refs_0_.1), channel_id=1, source_target_pairs={{0,4},{4,0},{8,12},{12,8},{16,20},{20,16},{24,28},{28,24},{1,5},{5... | collective-permute-start | bytes 22020104 | tf_op jit(solution)/shard_map/ppermute | solution.py:297
  2.7 47.2 %collective-permute-start.3 = (bf16[256,3584]{1,0:T(8,128)(2,1)S(1)}, bf16[256,3584]{1,0:T(8,128)(2,1)S(1)}, u32[]{:S(2)}, u32[]{:S(2)}) collective-permute-start(bf16[256,3584]{1,0:T(8,128)(2,1)S(1)} %get-tuple-element.29.refs_1_.refs_0_), channel_id=1, source_target_pairs={{0,24},{4,28},{24,0},{28,4},{1,25},{5,29},{25,1},{29,5},{2,26},{6,... | collective-permute-start | bytes 5505032 | tf_op jit(solution)/shard_map/ppermute | solution.py:309
  9.2 56.1 %collective-permute-start.6 = (bf16[336,3584]{1,0:T(8,128)(2,1)S(1)}, bf16[336,3584]{1,0:T(8,128)(2,1)S(1)}, u32[]{:S(2)}, u32[]{:S(2)}) collective-permute-start(bf16[336,3584]{1,0:T(8,128)(2,1)S(1)} %get-tuple-element.26.refs_1_), channel_id=1, source_target_pairs={{0,3},{1,2},{2,1},{3,0},{4,7},{5,6},{6,5},{7,4},{8,11},{9,10},{10,... | collective-permute-start | bytes 7225352 | tf_op jit(solution)/shard_map/ppermute | solution.py:294
  21.1 28.8 %collective-permute-start.1 = (bf16[336,256]{1,0:T(8,128)(2,1)S(1)}, bf16[336,256]{1,0:T(8,128)(2,1)S(1)}, u32[]{:S(2)}, u32[]{:S(2)}) collective-permute-start(bf16[336,256]{1,0:T(8,128)(2,1)S(1)} %get-tuple-element.51), channel_id=1, source_target_pairs={{0,4},{4,0},{8,12},{12,8},{16,20},{20,16},{24,28},{28,24},{1,5},{5... | collective-permute-start | bytes 516104 | tf_op jit(solution)/shard_map/ppermute | solution.py:297
  50.0 41.9 %collective-permute-start.5 = (bf16[256,3584]{1,0:T(8,128)(2,1)S(1)}, bf16[256,3584]{1,0:T(8,128)(2,1)S(1)}, u32[]{:S(2)}, u32[]{:S(2)}) collective-permute-start(bf16[256,3584]{1,0:T(8,128)(2,1)S(1)} %shard_map.40), channel_id=1, source_target_pairs={{0,8},{4,12},{8,0},{12,4},{16,24},{20,28},{24,16},{28,20},{1,9},{5... | collective-permute-start | bytes 5505032 | tf_op jit(solution)/shard_map/ppermute | solution.py:309
  50.1 41.8 %collective-permute-start.4 = (bf16[256,3584]{1,0:T(8,128)(2,1)S(1)}, bf16[256,3584]{1,0:T(8,128)(2,1)S(1)}, u32[]{:S(2)}, u32[]{:S(2)}) collective-permute-start(bf16[256,3584]{1,0:T(8,128)(2,1)S(1)} %shard_map.40), channel_id=1, source_target_pairs={{8,16},{12,20},{16,8},{20,12},{9,17},{13,21},{17,9},{21,13},{10,18... | collective-permute-start | bytes 5505032 | tf_op jit(solution)/shard_map/ppermute | solution.py:309
  50.9 65.4 %collective-permute-start.2 = (bf16[336,3584]{1,0:T(8,128)(2,1)S(1)}, bf16[336,3584]{1,0:T(8,128)(2,1)S(1)}, u32[]{:S(2)}, u32[]{:S(2)}) collective-permute-start(bf16[336,3584]{1,0:T(8,128)(2,1)S(1)} %get-tuple-element.28), channel_id=1, source_target_pairs={{0,2},{1,3},{2,0},{3,1},{4,6},{5,7},{6,4},{7,5},{8,10},{9,11},{10,... | collective-permute-start | bytes 7225352 | tf_op jit(solution)/shard_map/ppermute | solution.py:294
  52.5 64.5 %collective-permute-start.8 = (bf16[336,3584]{1,0:T(8,128)(2,1)S(1)}, bf16[336,3584]{1,0:T(8,128)(2,1)S(1)}, u32[]{:S(2)}, u32[]{:S(2)}) collective-permute-start(bf16[336,3584]{1,0:T(8,128)(2,1)S(1)} %get-tuple-element.30), channel_id=1, source_target_pairs={{0,1},{1,0},{2,3},{3,2},{4,5},{5,4},{6,7},{7,6},{8,9},{9,8},{10,11... | collective-permute-start | bytes 7225352 | tf_op jit(solution)/shard_map/ppermute | solution.py:294
  92.1 5.3 %collective-permute-start.9 = (bf16[256,3584]{1,0:T(8,128)(2,1)S(1)}, bf16[256,3584]{1,0:T(8,128)(2,1)S(1)}, u32[]{:S(2)}, u32[]{:S(2)}) collective-permute-start(bf16[256,3584]{1,0:T(8,128)(2,1)S(1)} %shard_map.42.refs_3_.refs_4_.refs_5_), channel_id=1, source_target_pairs={{0,4},{4,0},{8,12},{12,8},{16,20},{20,16},{24,28},{28,24},{1,5},{5... | collective-permute-start | bytes 5505032 | tf_op jit(solution)/shard_map/ppermute | solution.py:297
  92.3 6.2 %collective-permute-start.7 = (bf16[256,3584]{1,0:T(8,128)(2,1)S(1)}, bf16[256,3584]{1,0:T(8,128)(2,1)S(1)}, u32[]{:S(2)}, u32[]{:S(2)}) collective-permute-start(bf16[256,3584]{1,0:T(8,128)(2,1)S(1)} %shard_map.41.refs_1_.refs_2_), channel_id=1, source_target_pairs={{0,4},{4,0},{8,12},{12,8},{16,20},{20,16},{24,28},{28,24},{1,5},{5... | collective-permute-start | bytes 5505032 | tf_op jit(solution)/shard_map/ppermute | solution.py:297
  93.0 49.9 %collective-permute-start.20 = (bf16[256,3584]{1,0:T(8,128)(2,1)S(1)}, bf16[256,3584]{1,0:T(8,128)(2,1)S(1)}, u32[]{:S(2)}, u32[]{:S(2)}) collective-permute-start(bf16[256,3584]{1,0:T(8,128)(2,1)S(1)} %shard_map.48), channel_id=1, source_target_pairs={{0,8},{4,12},{8,0},{12,4},{16,24},{20,28},{24,16},{28,20},{1,9},{5... | collective-permute-start | bytes 5505032 | tf_op jit(solution)/shard_map/ppermute | solution.py:309
  101.3 22.4 %collective-permute-start.11 = (bf16[1,336,512]{2,1,0:T(8,128)(2,1)S(1)}, bf16[1,336,512]{2,1,0:T(8,128)(2,1)S(1)}, u32[]{:S(2)}, u32[]{:S(2)}) collective-permute-start(bf16[1,336,512]{2,1,0:T(8,128)(2,1)S(1)} %get-tuple-element.33), channel_id=1, source_target_pairs={{0,2},{1,3},{2,0},{3,1},{4,6},{5,7},{6,4},{7,5},{8,10},{9,11},{10,... | collective-permute-start | bytes 1032200 | tf_op jit(solution)/shard_map/ppermute | solution.py:294
  102.7 21.7 %collective-permute-start.10 = (bf16[1,336,512]{2,1,0:T(8,128)(2,1)S(1)}, bf16[1,336,512]{2,1,0:T(8,128)(2,1)S(1)}, u32[]{:S(2)}, u32[]{:S(2)}) collective-permute-start(bf16[1,336,512]{2,1,0:T(8,128)(2,1)S(1)} %get-tuple-element.31.refs_6_), channel_id=1, source_target_pairs={{0,1},{1,0},{2,3},{3,2},{4,5},{5,4},{6,7},{7,6},{8,9},{9,8},{10,11... | collective-permute-start | bytes 1032200 | tf_op jit(solution)/shard_map/ppermute | solution.py:294
  119.7 11.3 %collective-permute-start.16 = (bf16[1,336,512]{2,1,0:T(8,128)(2,1)S(1)}, bf16[1,336,512]{2,1,0:T(8,128)(2,1)S(1)}, u32[]{:S(2)}, u32[]{:S(2)}) collective-permute-start(bf16[1,336,512]{2,1,0:T(8,128)(2,1)S(1)} %get-tuple-element.38), channel_id=1, source_target_pairs={{0,2},{1,3},{2,0},{3,1},{4,6},{5,7},{6,4},{7,5},{8,10},{9,11},{10,... | collective-permute-start | bytes 1032200 | tf_op jit(solution)/shard_map/ppermute | solution.py:294
  120.6 12.2 %collective-permute-start.12 = (bf16[1,336,512]{2,1,0:T(8,128)(2,1)S(1)}, bf16[1,336,512]{2,1,0:T(8,128)(2,1)S(1)}, u32[]{:S(2)}, u32[]{:S(2)}) collective-permute-start(bf16[1,336,512]{2,1,0:T(8,128)(2,1)S(1)} %get-tuple-element.32.refs_7_), channel_id=1, source_target_pairs={{0,1},{1,0},{2,3},{3,2},{4,5},{5,4},{6,7},{7,6},{8,9},{9,8},{10,11... | collective-permute-start | bytes 1032200 | tf_op jit(solution)/shard_map/ppermute | solution.py:294
  131.3 10.0 %collective-permute-start.17 = (bf16[1,336,512]{2,1,0:T(8,128)(2,1)S(1)}, bf16[1,336,512]{2,1,0:T(8,128)(2,1)S(1)}, u32[]{:S(2)}, u32[]{:S(2)}) collective-permute-start(bf16[1,336,512]{2,1,0:T(8,128)(2,1)S(1)} %slice.93), channel_id=1, source_target_pairs={{0,1},{1,0},{2,3},{3,2},{4,5},{5,4},{6,7},{7,6},{8,9},{9,8},{10,11... | collective-permute-start | bytes 1032200 | tf_op jit(solution)/shard_map/ppermute | solution.py:294
  133.1 9.8 %collective-permute-start.13 = (bf16[1,336,512]{2,1,0:T(8,128)(2,1)S(1)}, bf16[1,336,512]{2,1,0:T(8,128)(2,1)S(1)}, u32[]{:S(2)}, u32[]{:S(2)}) collective-permute-start(bf16[1,336,512]{2,1,0:T(8,128)(2,1)S(1)} %slice.94), channel_id=1, source_target_pairs={{0,2},{1,3},{2,0},{3,1},{4,6},{5,7},{6,4},{7,5},{8,10},{9,11},{10,... | collective-permute-start | bytes 1032200 | tf_op jit(solution)/shard_map/ppermute | solution.py:294
  143.1 4.8 %collective-permute-start.21 = (bf16[256,3584]{1,0:T(8,128)(2,1)S(1)}, bf16[256,3584]{1,0:T(8,128)(2,1)S(1)}, u32[]{:S(2)}, u32[]{:S(2)}) collective-permute-start(bf16[256,3584]{1,0:T(8,128)(2,1)S(1)} %shard_map.49.refs_1_.refs_2_), channel_id=1, source_target_pairs={{0,4},{4,0},{8,12},{12,8},{16,20},{20,16},{24,28},{28,24},{1,5},{5... | collective-permute-start | bytes 5505032 | tf_op jit(solution)/shard_map/ppermute | solution.py:297
  143.2 4.4 %collective-permute-start.18 = (bf16[336,256]{1,0:T(8,128)(2,1)S(1)}, bf16[336,256]{1,0:T(8,128)(2,1)S(1)}, u32[]{:S(2)}, u32[]{:S(2)}) collective-permute-start(bf16[336,256]{1,0:T(8,128)(2,1)S(1)} %get-tuple-element.40.refs_4_), channel_id=1, source_target_pairs={{0,4},{4,0},{8,12},{12,8},{16,20},{20,16},{24,28},{28,24},{1,5},{5... | collective-permute-start | bytes 516104 | tf_op jit(solution)/shard_map/ppermute | solution.py:297
  145.1 8.5 %collective-permute-start.22 = (bf16[1,336,256]{2,1,0:T(8,128)(2,1)S(1)}, bf16[1,336,256]{2,1,0:T(8,128)(2,1)S(1)}, u32[]{:S(2)}, u32[]{:S(2)}) collective-permute-start(bf16[1,336,256]{2,1,0:T(8,128)(2,1)S(1)} %get-tuple-element.44), channel_id=1, source_target_pairs={{0,1},{1,0},{2,3},{3,2},{4,5},{5,4},{6,7},{7,6},{8,9},{9,8},{10,11... | collective-permute-start | bytes 516104 | tf_op jit(solution)/shard_map/ppermute | solution.py:294
  145.7 9.5 %collective-permute-start.23 = (bf16[1,336,256]{2,1,0:T(8,128)(2,1)S(1)}, bf16[1,336,256]{2,1,0:T(8,128)(2,1)S(1)}, u32[]{:S(2)}, u32[]{:S(2)}) collective-permute-start(bf16[1,336,256]{2,1,0:T(8,128)(2,1)S(1)} %get-tuple-element.41.refs_3_), channel_id=1, source_target_pairs={{0,1},{1,0},{2,3},{3,2},{4,5},{5,4},{6,7},{7,6},{8,9},{9,8},{10,11... | collective-permute-start | bytes 516104 | tf_op jit(solution)/shard_map/ppermute | solution.py:294
  147.3 14.5 %collective-permute-start.14 = (bf16[2,336,256]{2,1,0:T(8,128)(2,1)S(1)}, bf16[2,336,256]{2,1,0:T(8,128)(2,1)S(1)}, u32[]{:S(2)}, u32[]{:S(2)}) collective-permute-start(bf16[2,336,256]{2,1,0:T(8,128)(2,1)S(1)} %pad_maximum_fusion), channel_id=1, source_target_pairs={{0,24},{4,28},{8,16},{12,20},{16,8},{20,12},{24,0},{28,4},{1,25},{... | collective-permute-start | bytes 1032200 | tf_op jit(solution)/shard_map/ppermute | solution.py:309
  147.6 20.6 %collective-permute-start.19 = (bf16[2,336,256]{2,1,0:T(8,128)(2,1)S(1)}, bf16[2,336,256]{2,1,0:T(8,128)(2,1)S(1)}, u32[]{:S(2)}, u32[]{:S(2)}) collective-permute-start(bf16[2,336,256]{2,1,0:T(8,128)(2,1)S(1)} %pad_maximum_fusion.1), channel_id=1, source_target_pairs={{0,8},{4,12},{8,24},{12,28},{16,0},{20,4},{24,16},{28,20},{1,9},{5... | collective-permute-start | bytes 1032200 | tf_op jit(solution)/shard_map/ppermute | solution.py:309
  149.4 11.7 %collective-permute-start.27 = (bf16[1,336,256]{2,1,0:T(8,128)(2,1)S(1)}, bf16[1,336,256]{2,1,0:T(8,128)(2,1)S(1)}, u32[]{:S(2)}, u32[]{:S(2)}) collective-permute-start(bf16[1,336,256]{2,1,0:T(8,128)(2,1)S(1)} %get-tuple-element.42.refs_5_), channel_id=1, source_target_pairs={{0,2},{1,3},{2,0},{3,1},{4,6},{5,7},{6,4},{7,5},{8,10},{9,11},{10,... | collective-permute-start | bytes 516104 | tf_op jit(solution)/shard_map/ppermute | solution.py:294
  153.6 7.4 %collective-permute-start.26 = (bf16[1,336,256]{2,1,0:T(8,128)(2,1)S(1)}, bf16[1,336,256]{2,1,0:T(8,128)(2,1)S(1)}, u32[]{:S(2)}, u32[]{:S(2)}) collective-permute-start(bf16[1,336,256]{2,1,0:T(8,128)(2,1)S(1)} %get-tuple-element.46), channel_id=1, source_target_pairs={{0,2},{1,3},{2,0},{3,1},{4,6},{5,7},{6,4},{7,5},{8,10},{9,11},{10,... | collective-permute-start | bytes 516104 | tf_op jit(solution)/shard_map/ppermute | solution.py:294
  155.3 6.6 %copy-start = (f32[2688]{0:T(1024)S(1)}, f32[2688]{0:T(1024)}, u32[]{:S(2)}) copy-start(f32[2688]{0:T(1024)} %param.5) | copy-start | bytes 32260
  155.4 7.7 %collective-permute-start.24 = (bf16[1,336,256]{2,1,0:T(8,128)(2,1)S(1)}, bf16[1,336,256]{2,1,0:T(8,128)(2,1)S(1)}, u32[]{:S(2)}, u32[]{:S(2)}) collective-permute-start(bf16[1,336,256]{2,1,0:T(8,128)(2,1)S(1)} %slice.96), channel_id=1, source_target_pairs={{0,2},{1,3},{2,0},{3,1},{4,6},{5,7},{6,4},{7,5},{8,10},{9,11},{10,... | collective-permute-start | bytes 516104 | tf_op jit(solution)/shard_map/ppermute | solution.py:294
  161.1 5.5 %collective-permute-start.28 = (bf16[1,336,256]{2,1,0:T(8,128)(2,1)S(1)}, bf16[1,336,256]{2,1,0:T(8,128)(2,1)S(1)}, u32[]{:S(2)}, u32[]{:S(2)}) collective-permute-start(bf16[1,336,256]{2,1,0:T(8,128)(2,1)S(1)} %slice.95), channel_id=1, source_target_pairs={{0,1},{1,0},{2,3},{3,2},{4,5},{5,4},{6,7},{7,6},{8,9},{9,8},{10,11... | collective-permute-start | bytes 516104 | tf_op jit(solution)/shard_map/ppermute | solution.py:294
  161.8 6.4 %collective-permute-start.15 = (bf16[336,384]{1,0:T(8,128)(2,1)S(1)}, bf16[336,384]{1,0:T(8,128)(2,1)S(1)}, u32[]{:S(2)}, u32[]{:S(2)}) collective-permute-start(bf16[336,384]{1,0:T(8,128)(2,1)S(1)} %pad_maximum_fusion.2), channel_id=1, source_target_pairs={{0,4},{4,0},{8,12},{12,8},{16,20},{20,16},{24,28},{28,24},{1,5},{5... | collective-permute-start | bytes 774152 | tf_op jit(solution)/shard_map/ppermute | solution.py:297
  163.2 8.7 %collective-permute-start.25 = (bf16[336,256]{1,0:T(8,128)(2,1)S(1)}, bf16[336,256]{1,0:T(8,128)(2,1)S(1)}, u32[]{:S(2)}, u32[]{:S(2)}) collective-permute-start(bf16[336,256]{1,0:T(8,128)(2,1)S(1)} %shard_map.53), channel_id=1, source_target_pairs={{0,16},{4,20},{8,0},{12,4},{16,24},{20,28},{24,8},{28,12},{1,17},{... | collective-permute-start | bytes 516104 | tf_op jit(solution)/shard_map/ppermute | solution.py:395
  166.6 8.7 %collective-permute-start.29 = (bf16[336,256]{1,0:T(8,128)(2,1)S(1)}, bf16[336,256]{1,0:T(8,128)(2,1)S(1)}, u32[]{:S(2)}, u32[]{:S(2)}) collective-permute-start(bf16[336,256]{1,0:T(8,128)(2,1)S(1)} %shard_map.54), channel_id=1, source_target_pairs={{0,20},{4,16},{8,4},{12,0},{16,28},{20,24},{24,12},{28,8},{1,21},{... | collective-permute-start | bytes 516104 | tf_op jit(solution)/shard_map/ppermute | solution.py:395

commit v5 on v4

--- a/solution.py
+++ b/solution.py
@@ -8,7 +8,7 @@
 from jax.sharding import PartitionSpec as P
 
 ROOM = 14 * 1024 * 1024
-KEPT = 4_000_000_000
+KEPT = 0
 BACKS = 0
 IN_VMEM = pl.BlockSpec(memory_space=pltpu.VMEM)
 IN_HBM = pl.BlockSpec(memory_space=pltpu.HBM)
@@ -182,24 +182,46 @@
     )(*arrays, *after)
 
 
-def total_kernel(n_out, mine, got, *refs):
+def add_kernel(n, *refs):
+    out = refs[-1]
+    for i in range(n):
+        out[i : i + 1] = (refs[i][...] + refs[n + i][...].astype(jnp.float32)).astype(out.dtype)
+
+
+def added(mine, came, dtype):
+    shape = (len(mine), *mine[0].shape[1:])
+    size = shape[0] * shape[1] * shape[2]
+    return pl.pallas_call(
+        functools.partial(add_kernel, len(mine)),
+        in_specs=[IN_VMEM] * (2 * len(mine)),
+        out_specs=IN_VMEM,
+        out_shape=jax.ShapeDtypeStruct(shape, dtype),
+        compiler_params=pltpu.CompilerParams(vmem_limit_bytes=ROOM),
+        cost_estimate=pl.CostEstimate(flops=size, bytes_accessed=size, transcendentals=0),
+    )(*mine, *came)
+
+
+def total_kernel(n_out, n_terms, *refs):
     outs = refs[-n_out:]
     rows = outs[0].shape[1]
     for k, out in enumerate(outs):
         part = slice(k * rows, (k + 1) * rows)
-        out[...] = (mine[0, :, part] + got[0, :, part].astype(jnp.float32)).astype(out.dtype)
-
-
-def totals(mine, got, rows, after):
-    _, m, width = mine.shape
-    return pl.pallas_call(
-        functools.partial(total_kernel, width // rows),
-        in_specs=[IN_VMEM] * 2 + [ANYWHERE] * len(after),
+        total = refs[0][0, :, part]
+        for term in refs[1:n_terms]:
+            total = total + term[0, :, part].astype(jnp.float32)
+        out[...] = total.astype(out.dtype)
+
+
+def totals(terms, rows, after):
+    _, m, width = terms[0].shape
+    return pl.pallas_call(
+        functools.partial(total_kernel, width // rows, len(terms)),
+        in_specs=[IN_VMEM] * len(terms) + [ANYWHERE] * len(after),
         out_specs=[IN_VMEM] * (width // rows),
         out_shape=[jax.ShapeDtypeStruct((m, rows), jnp.bfloat16)] * (width // rows),
         compiler_params=pltpu.CompilerParams(vmem_limit_bytes=ROOM),
         cost_estimate=pl.CostEstimate(flops=m * width, bytes_accessed=m * width, transcendentals=0),
-    )(mine, got, *after)
+    )(*terms, *after)
 
 
 def join_kernel(places, *refs):
@@ -318,16 +340,20 @@
         (value,) = choose(arrays, wanted, after, 1)
         return [value, flip_row(value, 1)]
 
-    def halve(kept, mine, sums, orders):
-        for bit in orders:
-            mine = mine + sums.astype(jnp.float32)
+    def apart(x):
+        return [x] if x.shape[0] == 1 else [x[i : i + 1] for i in range(x.shape[0])]
+
+    def halve(kept, mine, came, orders):
+        for n, bit in enumerate(orders):
             go = [i for i, j in enumerate(kept) if j & bit]
             stay = [i for i, j in enumerate(kept) if not j & bit]
-            sent = jnp.stack([mine[i] for i in go]).astype(jnp.bfloat16)
-            mine = jnp.stack([mine[i] for i in stay])
+            got = flip_col(added([mine[i] for i in go], [came[i] for i in go], jnp.bfloat16), bit)
             kept = [kept[i] for i in stay]
-            sums = flip_col(sent, bit)
-        return mine, sums
+            if n + 1 == len(orders):
+                return [mine[stay[0]], came[stay[0]], got]
+            mine = [added([mine[i]], [came[i]], jnp.float32) for i in stay]
+            came = apart(got)
+        return [mine[0], came[0]]
 
     bits = [1 << b for b in range(n_col.bit_length() - 1)]
     orders = [bits[i % len(bits) :] + bits[: i % len(bits)] for i in range(planes + 1)]
@@ -344,21 +370,26 @@
         list(firsts[:1]),
     )
     got_next = [flip_col(x, orders[i][0]) for i, x in enumerate(nexts)]
-    mines = products(
-        [([w_band[j] for j in splits[i][1]], blocks[d]) for i, d in enumerate(early)],
-        jnp.float32,
-        list(nexts[:1]) + got_first,
-        KEPT,
-    )
+    passing = [[j for j in splits[i][1] if len(orders[i]) > 1 and j & orders[i][1]] for i in early]
+    staying = [[j for j in splits[i][1] if j not in passing[i]] for i in early]
+    mine_of, first_mine = {}, list(nexts[:1])
+    for which, flops in ((passing, KEPT), (staying, 0)):
+        mines = products(
+            [([w_band[j]], blocks[d]) for i, d in enumerate(early) for j in which[i]], jnp.float32, first_mine, flops
+        )
+        first_mine = list(mines[:1])
+        mine_of.update(zip([(i, j) for i in early for j in which[i]], mines))
+
     def gather_sums(i, far, near):
-        came = {last_j: far[0]}
-        came.update(zip([j for j in splits[i][0] if j != last_j], near))
-        return jnp.stack([came[j | orders[i][0]] for j in splits[i][1]])
-
+        came = {last_j: far}
+        came.update(zip([j for j in splits[i][0] if j != last_j], apart(near)))
+        return [came[j | orders[i][0]] for j in splits[i][1]]
+
+    n_kept = n_col // 2
     ended = []
     for i, d in enumerate(early):
         sums = gather_sums(i, got_first[i], got_next[i])
-        ended.append(totals(*halve(splits[i][1], mines[i], sums, orders[i][1:]), half, []))
+        ended.append(totals(halve(splits[i][1], [mine_of[i, j] for j in splits[i][1]], sums, orders[i][1:]), half, []))
     swapped = [flip_row(other, 1) for _, other in ended[1:]]
     both = arrived(slots[-1], [x for pair in ended for x in pair])
     backs = []
@@ -374,7 +405,7 @@
             hop = flip_row(jnp.concatenate([back[1], back[1][:, : half // 2]], axis=1), 1)
             parts.append((source, 1, hop[:, :half]))
         parts.append((source, 0, back[0]))
-    sents = list(mines[:1])
+    sents = first_mine
     late = []
     for core in (0, 1):
         i = len(early) + core
@@ -384,12 +415,11 @@
         )
         late.append((i, core, [flip_col(x, orders[i][0]) for x in sents]))
     late_mines = products(
-        [([w_band[j] for j in splits[i][1]], [both[core]]) for i, core, _ in late], jnp.float32, sents[:1]
+        [([w_band[j]], [both[core]]) for i, core, _ in late for j in splits[i][1]], jnp.float32, list(sents[:1])
     )
-    for (i, core, got), mine in zip(late, late_mines):
-        (done,) = totals(
-            *halve(splits[i][1], mine, gather_sums(i, *got), orders[i][1:]), half, backs[: BACKS * core]
-        )
+    for i, core, got in late:
+        mine = late_mines[core * n_kept : (core + 1) * n_kept]
+        (done,) = totals(halve(splits[i][1], mine, gather_sums(i, *got), orders[i][1:]), half, [])
         home = [(2 * p + c, 2 * q + (c ^ core)) for p, q in enumerate(slots[-1][2]) for c in (0, 1)]
         source = [slots[-1][2].index(q) for q in everyone]
         parts.append((source, core, lax.ppermute(done, "row", home)))

time: 178 us -> 174 us (0.978)
  waiting for transfers between devices: 105 us -> 98.7 us
  starting transfers between devices: 37.7 us -> 40.5 us
    ppermute x6, waiting for transfers between devices: 53.3 us -> 60.7 us  [send(): lax.ppermute(x, 'row', [(2 * a + c, 2 * b + c) for a, b in pairs for c in...]
    ppermute x2, waiting for transfers between devices: 7.11 us -> 0.01 us  [shards(): parts.append((source, core, lax.ppermute(done, 'row', home)))]
    ppermute x15, waiting for transfers between devices: 43 us -> 36.6 us  [flip_col(): return lax.ppermute(x, 'col', [(i, i ^ j) for i in range(n_col)])]
    ppermute x6, starting transfers between devices: 12.3 us -> 14.3 us  [send(): lax.ppermute(x, 'row', [(2 * a + c, 2 * b + c) for a, b in pairs for c in...]
    pallas_call x6 -> x7, Pallas kernels: 16 us -> 16.2 us  [products(): pl.pallas_call(functools.partial(product_kernel, plan, len(arrays)), in_s...]
  transfers between devices with their start and end apart: 30 -> 30, of which waited for: 19 -> 11; matrix products, arithmetic and copies ran while one was open for 1% -> 0% of each run, Pallas kernels for 18% -> 18%
where the time goes in v5:
time: 174 us
  waiting for transfers between devices  98.7 us (57%)
  starting transfers between devices  40.5 us (23%)
  Pallas kernels  34.2 us (20%)
    ppermute x6, waiting for transfers between devices, send(): lax.ppermute(x, 'row', [(2 * a + c, 2 * b + c) for a, b in pairs for c in...  60.7 us
    ppermute x15, waiting for transfers between devices, flip_col(): return lax.ppermute(x, 'col', [(i, i ^ j) for i in range(n_col)])  36.6 us
    ppermute x15, starting transfers between devices, flip_col(): return lax.ppermute(x, 'col', [(i, i ^ j) for i in range(n_col)])  20.1 us
    pallas_call x7, Pallas kernels, products(): pl.pallas_call(functools.partial(product_kernel, plan, len(arrays)), in_s...  16.2 us
    ppermute x6, starting transfers between devices, send(): lax.ppermute(x, 'row', [(2 * a + c, 2 * b + c) for a, b in pairs for c in...  14.3 us
    pallas_call x1, Pallas kernels, deep_product(): pl.pallas_call(deep_kernel, grid=(depth // block,), in_specs=[pl.BlockSpe...  9.13 us
    pallas_call x2, Pallas kernels, bands(): pl.pallas_call(functools.partial(bands_kernel, pieces, n_col, len(xs)), o...  5.41 us
    ppermute x2, starting transfers between devices, shards(): parts.append((source, core, lax.ppermute(done, 'row', home)))  4.24 us
  transfers between devices with their start and end apart: 30, of which 11 were waited for; matrix products, arithmetic and copies ran while one was open for 0% of the time, Pallas kernels for 18%

profile of v5, /device:TPU:0, one launch (start us, length us, event | category | flops | bytes accessed | tf_op | source)
XLA Modules:
  0.0 174.1 jit_solution(11347944263116057085)
XLA Ops:
  0.0 0.5 collective-permute-start
  0.5 2.2 %shard_map.38 = (bf16[256,3584]{1,0:T(8,128)(2,1)S(1)}, bf16[336,3584]{1,0:T(8,128)(2,1)S(1)}) custom-call(bf16[256,14336]{1,0:T(8,128)(2,1)} %refs_0_.1, bf16[336,14336]{1,0:T(8,128)(2,1)} %bitcast.18), custom_call_target="tpu_custom_call" | custom-call | tf_op jit(solution)/shard_map/pallas_call | solution.py:40
  2.7 6.5 %collective-permute-start.2 = (bf16[256,3584]{1,0:T(8,128)(2,1)S(1)}, bf16[256,3584]{1,0:T(8,128)(2,1)S(1)}, u32[]{:S(2)}, u32[]{:S(2)}) collective-permute-start(bf16[256,3584]{1,0:T(8,128)(2,1)S(1)} %get-tuple-element.32.refs_1_.refs_0_), channel_id=1, source_target_pairs={{0,24},{4,28},{24,0},{28,4},{1,25},{5,29},{25,1},{29,5},{2,26},{6,... | collective-permute-start | bytes 5505032 | tf_op jit(solution)/shard_map/ppermute | solution.py:331
  9.2 2.5 %collective-permute-start.5 = (bf16[336,3584]{1,0:T(8,128)(2,1)S(1)}, bf16[336,3584]{1,0:T(8,128)(2,1)S(1)}, u32[]{:S(2)}, u32[]{:S(2)}) collective-permute-start(bf16[336,3584]{1,0:T(8,128)(2,1)S(1)} %get-tuple-element.30.refs_1_), channel_id=1, source_target_pairs={{0,3},{1,2},{2,1},{3,0},{4,7},{5,6},{6,5},{7,4},{8,11},{9,10},{10,... | collective-permute-start | bytes 7225352 | tf_op jit(solution)/shard_map/ppermute | solution.py:316
  11.7 0.2 collective-permute-done.t1
  11.9 9.1 %shard_map.37 = bf16[336,512]{1,0:T(8,128)(2,1)S(1)} custom-call(bf16[336,14336]{1,0:T(8,128)(2,1)} %bitcast.19, bf16[256,14336]{1,0:T(8,128)(2,1)} %refs_0_.1, bf16[256,14336]{1,0:T(8,128)(2,1)S(1)} %collective-permute-done.t1), custom_call_target="tpu_custom_call" | custom-call | flops 4932501504 | bytes 24313856 | tf_op jit(solution)/shard_map/pallas_call | solution.py:135
  21.1 0.4 collective-permute-start.1
  21.6 3.2 %shard_map.39 = (bf16[336,3584]{1,0:T(8,128)(2,1)S(1)}, bf16[336,3584]{1,0:T(8,128)(2,1)S(1)}, bf16[336,3584]{1,0:T(8,128)(2,1)S(1)}) custom-call(bf16[336,14336]{1,0:T(8,128)(2,1)} %bitcast.20, bf16[336,3584]{1,0:T(8,128)(2,1)S(1)} %get-tuple-element.30.refs_1_), custom_call_target="tpu_custom_call" | custom-call | tf_op jit(solution)/shard_map/pallas_call | solution.py:40
  24.7 25.2 %collective-permute-done.2.refs_0_ = bf16[256,3584]{1,0:T(8,128)(2,1)S(1)} collective-permute-done((bf16[256,3584]{1,0:T(8,128)(2,1)S(1)}, bf16[256,3584]{1,0:T(8,128)(2,1)S(1)}, u32[]{:S(2)}, u32[]{:S(2)}) %collective-permute-start.2) | collective-permute-done | bytes 1835040 | tf_op jit(solution)/shard_map/ppermute | solution.py:331
  49.9 0.1 shard_map.40
  50.0 0.1 collective-permute-start.4
  50.1 0.8 collective-permute-start.3
  50.9 1.6 collective-permute-start.8
  52.5 1.5 collective-permute-start.9
  54.0 11.4 %collective-permute-done.5.refs_4_.refs_3_.refs_0_ = bf16[336,3584]{1,0:T(8,128)(2,1)S(1)} collective-permute-done((bf16[336,3584]{1,0:T(8,128)(2,1)S(1)}, bf16[336,3584]{1,0:T(8,128)(2,1)S(1)}, u32[]{:S(2)}, u32[]{:S(2)}) %collective-permute-start.5) | collective-permute-done | bytes 2408480 | tf_op jit(solution)/shard_map/ppermute | solution.py:316
  65.4 26.6 %collective-permute-done.4.refs_2_.refs_0_.refs_1_ = bf16[256,3584]{1,0:T(8,128)(2,1)S(1)} collective-permute-done((bf16[256,3584]{1,0:T(8,128)(2,1)S(1)}, bf16[256,3584]{1,0:T(8,128)(2,1)S(1)}, u32[]{:S(2)}, u32[]{:S(2)}) %collective-permute-start.4) | collective-permute-done | bytes 1835040 | tf_op jit(solution)/shard_map/ppermute | solution.py:331
  92.0 0.1 shard_map.42.refs_3_.refs_4_
  92.1 0.1 collective-permute-start.7
  92.2 0.2 shard_map.41.refs_1_
  92.3 0.5 collective-permute-start.6
  92.9 0.1 shard_map.51
  93.0 4.4 %collective-permute-start.20 = (bf16[256,3584]{1,0:T(8,128)(2,1)S(1)}, bf16[256,3584]{1,0:T(8,128)(2,1)S(1)}, u32[]{:S(2)}, u32[]{:S(2)}) collective-permute-start(bf16[256,3584]{1,0:T(8,128)(2,1)S(1)} %shard_map.51), channel_id=1, source_target_pairs={{0,8},{4,12},{8,0},{12,4},{16,24},{20,28},{24,16},{28,20},{1,9},{5... | collective-permute-start | bytes 5505032 | tf_op jit(solution)/shard_map/ppermute | solution.py:331
  97.4 1.2 collective-permute-done.6.refs_2_
  98.6 2.7 %shard_map.43 = (bf16[1,336,512]{2,1,0:T(8,128)(2,1)S(1)}, bf16[1,336,512]{2,1,0:T(8,128)(2,1)S(1)}) custom-call(bf16[336,3584]{1,0:T(8,128)(2,1)S(1)} %collective-permute-done.5.refs_4_.refs_3_.refs_0_, bf16[256,3584]{1,0:T(8,128)(2,1)S(1)} %shard_map.41.refs_1_, bf16[256,3584]{1,0:T(8,128)(2,1)S(1)} %collective-permute-done.6.refs_2_, ...), custom_call_target="tpu_custom_call" | custom-call | flops 344064 | bytes 344064 | tf_op jit(solution)/shard_map/pallas_call | solution.py:175
  101.3 1.4 collective-permute-start.11
  102.7 1.5 collective-permute-start.16
  104.2 12.1 %collective-permute-done.8.refs_3_.refs_0_.refs_2_ = bf16[336,3584]{1,0:T(8,128)(2,1)S(1)} collective-permute-done((bf16[336,3584]{1,0:T(8,128)(2,1)S(1)}, bf16[336,3584]{1,0:T(8,128)(2,1)S(1)}, u32[]{:S(2)}, u32[]{:S(2)}) %collective-permute-start.8) | collective-permute-done | bytes 2408480 | tf_op jit(solution)/shard_map/ppermute | solution.py:316
  116.3 0.7 collective-permute-done.9.refs_0_.refs_3_.refs_2_.refs_4_
  117.0 2.7 %shard_map.44 = (bf16[1,336,512]{2,1,0:T(8,128)(2,1)S(1)}, bf16[1,336,512]{2,1,0:T(8,128)(2,1)S(1)}) custom-call(bf16[336,3584]{1,0:T(8,128)(2,1)S(1)} %collective-permute-done.9.refs_0_.refs_3_.refs_2_.refs_4_, bf16[256,3584]{1,0:T(8,128)(2,1)S(1)} %shard_map.41.refs_1_, bf16[256,3584]{1,0:T(8,128)(2,1)S(1)} %collective-permute-done.6.refs_2_, ...), custom_call_target="tpu_custom_call" | custom-call | flops 344064 | bytes 344064 | tf_op jit(solution)/shard_map/pallas_call | solution.py:175
  119.7 0.9 collective-permute-start.15
  120.6 1.5 collective-permute-start.10
  122.1 2.7 %shard_map.45 = (f32[1,336,512]{2,1,0:T(8,128)S(1)}, f32[1,336,512]{2,1,0:T(8,128)S(1)}) custom-call(bf16[336,3584]{1,0:T(8,128)(2,1)S(1)} %collective-permute-done.8.refs_3_.refs_0_.refs_2_, bf16[256,3584]{1,0:T(8,128)(2,1)S(1)} %shard_map.41.refs_1_, bf16[256,3584]{1,0:T(8,128)(2,1)S(1)} %collective-permute-done.6.refs_2_, ...), custom_call_target="tpu_custom_call" | custom-call | flops 344064 | bytes 344064 | tf_op jit(solution)/shard_map/pallas_call | solution.py:175
  124.8 0.1 shard_map.47
  124.8 1.3 collective-permute-start.12
  126.1 0.1 shard_map.49
  126.2 0.6 collective-permute-start.17
  126.8 2.7 %shard_map.46 = (f32[1,336,512]{2,1,0:T(8,128)S(1)}, f32[1,336,512]{2,1,0:T(8,128)S(1)}) custom-call(bf16[336,3584]{1,0:T(8,128)(2,1)S(1)} %get-tuple-element.31.refs_3_.refs_0_, bf16[256,3584]{1,0:T(8,128)(2,1)S(1)} %shard_map.41.refs_1_, bf16[256,3584]{1,0:T(8,128)(2,1)S(1)} %collective-permute-done.6.refs_2_, ...), custom_call_target="tpu_custom_call" | custom-call | flops 344064 | bytes 344064 | tf_op jit(solution)/shard_map/pallas_call | solution.py:175
  129.5 2.3 %collective-permute-done.10.refs_1_ = bf16[1,336,512]{2,1,0:T(8,128)(2,1)S(1)} collective-permute-done((bf16[1,336,512]{2,1,0:T(8,128)(2,1)S(1)}, bf16[1,336,512]{2,1,0:T(8,128)(2,1)S(1)}, u32[]{:S(2)}, u32[]{:S(2)}) %collective-permute-start.10) | collective-permute-done | bytes 344096 | tf_op jit(solution)/shard_map/ppermute | solution.py:316
  131.8 6.6 %collective-permute-done.12.refs_2_ = bf16[1,336,512]{2,1,0:T(8,128)(2,1)S(1)} collective-permute-done((bf16[1,336,512]{2,1,0:T(8,128)(2,1)S(1)}, bf16[1,336,512]{2,1,0:T(8,128)(2,1)S(1)}, u32[]{:S(2)}, u32[]{:S(2)}) %collective-permute-start.12) | collective-permute-done | bytes 344096 | tf_op jit(solution)/shard_map/ppermute | solution.py:316
  138.4 0.1 shard_map.48
  138.5 0.1 shard_map.50
  138.6 0.3 shard_map.52.refs_1_
  138.9 0.1 collective-permute-start.21
  139.1 1.7 collective-permute-start.13
  140.8 0.2 collective-permute-start.18
  141.0 1.4 shard_map.53
  142.4 1.6 collective-permute-start.23
  144.0 1.4 shard_map.54
  145.4 1.6 collective-permute-start.27
  147.0 0.5 collective-permute-start.22
  147.6 0.9 collective-permute-start.19
  148.5 2.7 %shard_map.55 = (f32[1,336,256]{2,1,0:T(8,128)S(1)}, f32[1,336,256]{2,1,0:T(8,128)S(1)}, f32[1,336,256]{2,1,0:T(8,128)S(1)}, f32[1,336,256]{2,1,0:T(8,128)S(1)}) custom-call(bf16[336,3584]{1,0:T(8,128)(2,1)S(1)} %get-tuple-element.31.refs_3_.refs_0_, bf16[256,3584]{1,0:T(8,128)(2,1)S(1)} %shard_map.52.refs_1_, ...), custom_call_target="tpu_custom_call" | custom-call | flops 344064 | bytes 344064 | tf_op jit(solution)/shard_map/pallas_call | solution.py:175
  151.1 0.0 copy-start
  151.2 0.6 collective-permute-start.24
  151.8 1.5 collective-permute-start.26
  153.4 1.6 collective-permute-start.28
  155.0 0.1 collective-permute-start.14
  155.1 3.5 %collective-permute-done.24.refs_2_ = bf16[1,336,256]{2,1,0:T(8,128)(2,1)S(1)} collective-permute-done((bf16[1,336,256]{2,1,0:T(8,128)(2,1)S(1)}, bf16[1,336,256]{2,1,0:T(8,128)(2,1)S(1)}, u32[]{:S(2)}, u32[]{:S(2)}) %collective-permute-start.24) | collective-permute-done | bytes 172064 | tf_op jit(solution)/shard_map/ppermute | solution.py:316
  158.6 0.1 shard_map.57
  158.7 2.4 %collective-permute-start.25 = (bf16[336,256]{1,0:T(8,128)(2,1)S(1)}, bf16[336,256]{1,0:T(8,128)(2,1)S(1)}, u32[]{:S(2)}, u32[]{:S(2)}) collective-permute-start(bf16[336,256]{1,0:T(8,128)(2,1)S(1)} %shard_map.57), channel_id=1, source_target_pairs={{0,16},{4,20},{8,0},{12,4},{16,24},{20,28},{24,8},{28,12},{1,17},{... | collective-permute-start | bytes 516104 | tf_op jit(solution)/shard_map/ppermute | solution.py:425
  161.1 0.1 shard_map.59
  161.2 1.8 %collective-permute-start.29 = (bf16[336,256]{1,0:T(8,128)(2,1)S(1)}, bf16[336,256]{1,0:T(8,128)(2,1)S(1)}, u32[]{:S(2)}, u32[]{:S(2)}) collective-permute-start(bf16[336,256]{1,0:T(8,128)(2,1)S(1)} %shard_map.59), channel_id=1, source_target_pairs={{0,20},{4,16},{8,4},{12,0},{16,28},{20,24},{24,12},{28,8},{1,21},{... | collective-permute-start | bytes 516104 | tf_op jit(solution)/shard_map/ppermute | solution.py:425
  163.0 9.0 %collective-permute-done.19 = bf16[2,336,256]{2,1,0:T(8,128)(2,1)S(1)} collective-permute-done((bf16[2,336,256]{2,1,0:T(8,128)(2,1)S(1)}, bf16[2,336,256]{2,1,0:T(8,128)(2,1)S(1)}, u32[]{:S(2)}, u32[]{:S(2)}) %collective-permute-start.19) | collective-permute-done | bytes 344096 | tf_op jit(solution)/shard_map/ppermute | solution.py:331
  172.0 2.1 %shard_map.60 = bf16[256,2688]{1,0:T(8,128)(2,1)} custom-call(bf16[336,256]{1,0:T(8,128)(2,1)S(1)} %get-tuple-element.60.refs_0_, bf16[336,256]{1,0:T(8,128)(2,1)S(1)} %collective-permute-done.1.refs_2_.refs_1_, bf16[336,256]{1,0:T(8,128)(2,1)S(1)} %slice.37.refs_2_, bf16[336,256]{1,0:T(8,128)(2,1)S(1)} %get-tuple-element.57.refs_3_, ...), custom_call_target="tpu_custom_call" | custom-call | flops 688128 | bytes 2752512 | tf_op jit(solution)/shard_map/pallas_call | solution.py:245
  (31 shorter events, 0.3 us)
Async XLA Ops:
  0.0 11.9 %collective-permute-start = (bf16[256,14336]{1,0:T(8,128)(2,1)}, bf16[256,14336]{1,0:T(8,128)(2,1)S(1)}, u32[]{:S(2)}, u32[]{:S(2)}) collective-permute-start(bf16[256,14336]{1,0:T(8,128)(2,1)} %refs_0_.1), channel_id=1, source_target_pairs={{0,4},{4,0},{8,12},{12,8},{16,20},{20,16},{24,28},{28,24},{1,5},{5... | collective-permute-start | bytes 22020104 | tf_op jit(solution)/shard_map/ppermute | solution.py:319
  2.7 47.2 %collective-permute-start.2 = (bf16[256,3584]{1,0:T(8,128)(2,1)S(1)}, bf16[256,3584]{1,0:T(8,128)(2,1)S(1)}, u32[]{:S(2)}, u32[]{:S(2)}) collective-permute-start(bf16[256,3584]{1,0:T(8,128)(2,1)S(1)} %get-tuple-element.32.refs_1_.refs_0_), channel_id=1, source_target_pairs={{0,24},{4,28},{24,0},{28,4},{1,25},{5,29},{25,1},{29,5},{2,26},{6,... | collective-permute-start | bytes 5505032 | tf_op jit(solution)/shard_map/ppermute | solution.py:331
  9.2 56.1 %collective-permute-start.5 = (bf16[336,3584]{1,0:T(8,128)(2,1)S(1)}, bf16[336,3584]{1,0:T(8,128)(2,1)S(1)}, u32[]{:S(2)}, u32[]{:S(2)}) collective-permute-start(bf16[336,3584]{1,0:T(8,128)(2,1)S(1)} %get-tuple-element.30.refs_1_), channel_id=1, source_target_pairs={{0,3},{1,2},{2,1},{3,0},{4,7},{5,6},{6,5},{7,4},{8,11},{9,10},{10,... | collective-permute-start | bytes 7225352 | tf_op jit(solution)/shard_map/ppermute | solution.py:316
  21.1 28.8 %collective-permute-start.1 = (bf16[336,256]{1,0:T(8,128)(2,1)S(1)}, bf16[336,256]{1,0:T(8,128)(2,1)S(1)}, u32[]{:S(2)}, u32[]{:S(2)}) collective-permute-start(bf16[336,256]{1,0:T(8,128)(2,1)S(1)} %get-tuple-element.59), channel_id=1, source_target_pairs={{0,4},{4,0},{8,12},{12,8},{16,20},{20,16},{24,28},{28,24},{1,5},{5... | collective-permute-start | bytes 516104 | tf_op jit(solution)/shard_map/ppermute | solution.py:319
  50.0 41.9 %collective-permute-start.4 = (bf16[256,3584]{1,0:T(8,128)(2,1)S(1)}, bf16[256,3584]{1,0:T(8,128)(2,1)S(1)}, u32[]{:S(2)}, u32[]{:S(2)}) collective-permute-start(bf16[256,3584]{1,0:T(8,128)(2,1)S(1)} %shard_map.40), channel_id=1, source_target_pairs={{0,8},{4,12},{8,0},{12,4},{16,24},{20,28},{24,16},{28,20},{1,9},{5... | collective-permute-start | bytes 5505032 | tf_op jit(solution)/shard_map/ppermute | solution.py:331
  50.1 41.8 %collective-permute-start.3 = (bf16[256,3584]{1,0:T(8,128)(2,1)S(1)}, bf16[256,3584]{1,0:T(8,128)(2,1)S(1)}, u32[]{:S(2)}, u32[]{:S(2)}) collective-permute-start(bf16[256,3584]{1,0:T(8,128)(2,1)S(1)} %shard_map.40), channel_id=1, source_target_pairs={{8,16},{12,20},{16,8},{20,12},{9,17},{13,21},{17,9},{21,13},{10,18... | collective-permute-start | bytes 5505032 | tf_op jit(solution)/shard_map/ppermute | solution.py:331
  50.9 65.4 %collective-permute-start.8 = (bf16[336,3584]{1,0:T(8,128)(2,1)S(1)}, bf16[336,3584]{1,0:T(8,128)(2,1)S(1)}, u32[]{:S(2)}, u32[]{:S(2)}) collective-permute-start(bf16[336,3584]{1,0:T(8,128)(2,1)S(1)} %get-tuple-element.33), channel_id=1, source_target_pairs={{0,2},{1,3},{2,0},{3,1},{4,6},{5,7},{6,4},{7,5},{8,10},{9,11},{10,... | collective-permute-start | bytes 7225352 | tf_op jit(solution)/shard_map/ppermute | solution.py:316
  52.5 64.5 %collective-permute-start.9 = (bf16[336,3584]{1,0:T(8,128)(2,1)S(1)}, bf16[336,3584]{1,0:T(8,128)(2,1)S(1)}, u32[]{:S(2)}, u32[]{:S(2)}) collective-permute-start(bf16[336,3584]{1,0:T(8,128)(2,1)S(1)} %get-tuple-element.34), channel_id=1, source_target_pairs={{0,1},{1,0},{2,3},{3,2},{4,5},{5,4},{6,7},{7,6},{8,9},{9,8},{10,11... | collective-permute-start | bytes 7225352 | tf_op jit(solution)/shard_map/ppermute | solution.py:316
  92.1 5.3 %collective-permute-start.7 = (bf16[256,3584]{1,0:T(8,128)(2,1)S(1)}, bf16[256,3584]{1,0:T(8,128)(2,1)S(1)}, u32[]{:S(2)}, u32[]{:S(2)}) collective-permute-start(bf16[256,3584]{1,0:T(8,128)(2,1)S(1)} %shard_map.42.refs_3_.refs_4_), channel_id=1, source_target_pairs={{0,4},{4,0},{8,12},{12,8},{16,20},{20,16},{24,28},{28,24},{1,5},{5... | collective-permute-start | bytes 5505032 | tf_op jit(solution)/shard_map/ppermute | solution.py:319
  92.3 6.2 %collective-permute-start.6 = (bf16[256,3584]{1,0:T(8,128)(2,1)S(1)}, bf16[256,3584]{1,0:T(8,128)(2,1)S(1)}, u32[]{:S(2)}, u32[]{:S(2)}) collective-permute-start(bf16[256,3584]{1,0:T(8,128)(2,1)S(1)} %shard_map.41.refs_1_), channel_id=1, source_target_pairs={{0,4},{4,0},{8,12},{12,8},{16,20},{20,16},{24,28},{28,24},{1,5},{5... | collective-permute-start | bytes 5505032 | tf_op jit(solution)/shard_map/ppermute | solution.py:319
  93.0 45.6 %collective-permute-start.20 = (bf16[256,3584]{1,0:T(8,128)(2,1)S(1)}, bf16[256,3584]{1,0:T(8,128)(2,1)S(1)}, u32[]{:S(2)}, u32[]{:S(2)}) collective-permute-start(bf16[256,3584]{1,0:T(8,128)(2,1)S(1)} %shard_map.51), channel_id=1, source_target_pairs={{0,8},{4,12},{8,0},{12,4},{16,24},{20,28},{24,16},{28,20},{1,9},{5... | collective-permute-start | bytes 5505032 | tf_op jit(solution)/shard_map/ppermute | solution.py:331
  101.3 23.5 %collective-permute-start.11 = (bf16[1,336,512]{2,1,0:T(8,128)(2,1)S(1)}, bf16[1,336,512]{2,1,0:T(8,128)(2,1)S(1)}, u32[]{:S(2)}, u32[]{:S(2)}) collective-permute-start(bf16[1,336,512]{2,1,0:T(8,128)(2,1)S(1)} %get-tuple-element.35.refs_6_), channel_id=1, source_target_pairs={{0,1},{1,0},{2,3},{3,2},{4,5},{5,4},{6,7},{7,6},{8,9},{9,8},{10,11... | collective-permute-start | bytes 1032200 | tf_op jit(solution)/shard_map/ppermute | solution.py:316
  102.7 23.4 %collective-permute-start.16 = (bf16[1,336,512]{2,1,0:T(8,128)(2,1)S(1)}, bf16[1,336,512]{2,1,0:T(8,128)(2,1)S(1)}, u32[]{:S(2)}, u32[]{:S(2)}) collective-permute-start(bf16[1,336,512]{2,1,0:T(8,128)(2,1)S(1)} %get-tuple-element.44), channel_id=1, source_target_pairs={{0,2},{1,3},{2,0},{3,1},{4,6},{5,7},{6,4},{7,5},{8,10},{9,11},{10,... | collective-permute-start | bytes 1032200 | tf_op jit(solution)/shard_map/ppermute | solution.py:316
  119.7 18.7 %collective-permute-start.15 = (bf16[1,336,512]{2,1,0:T(8,128)(2,1)S(1)}, bf16[1,336,512]{2,1,0:T(8,128)(2,1)S(1)}, u32[]{:S(2)}, u32[]{:S(2)}) collective-permute-start(bf16[1,336,512]{2,1,0:T(8,128)(2,1)S(1)} %get-tuple-element.42), channel_id=1, source_target_pairs={{0,2},{1,3},{2,0},{3,1},{4,6},{5,7},{6,4},{7,5},{8,10},{9,11},{10,... | collective-permute-start | bytes 1032200 | tf_op jit(solution)/shard_map/ppermute | solution.py:316
  120.6 11.2 %collective-permute-start.10 = (bf16[1,336,512]{2,1,0:T(8,128)(2,1)S(1)}, bf16[1,336,512]{2,1,0:T(8,128)(2,1)S(1)}, u32[]{:S(2)}, u32[]{:S(2)}) collective-permute-start(bf16[1,336,512]{2,1,0:T(8,128)(2,1)S(1)} %get-tuple-element.36.refs_6_), channel_id=1, source_target_pairs={{0,1},{1,0},{2,3},{3,2},{4,5},{5,4},{6,7},{7,6},{8,9},{9,8},{10,11... | collective-permute-start | bytes 1032200 | tf_op jit(solution)/shard_map/ppermute | solution.py:316
  124.8 13.5 %collective-permute-start.12 = (bf16[1,336,512]{2,1,0:T(8,128)(2,1)S(1)}, bf16[1,336,512]{2,1,0:T(8,128)(2,1)S(1)}, u32[]{:S(2)}, u32[]{:S(2)}) collective-permute-start(bf16[1,336,512]{2,1,0:T(8,128)(2,1)S(1)} %shard_map.47), channel_id=1, source_target_pairs={{0,2},{1,3},{2,0},{3,1},{4,6},{5,7},{6,4},{7,5},{8,10},{9,11},{10,... | collective-permute-start | bytes 1032200 | tf_op jit(solution)/shard_map/ppermute | solution.py:316
  126.2 12.3 %collective-permute-start.17 = (bf16[1,336,512]{2,1,0:T(8,128)(2,1)S(1)}, bf16[1,336,512]{2,1,0:T(8,128)(2,1)S(1)}, u32[]{:S(2)}, u32[]{:S(2)}) collective-permute-start(bf16[1,336,512]{2,1,0:T(8,128)(2,1)S(1)} %shard_map.49), channel_id=1, source_target_pairs={{0,1},{1,0},{2,3},{3,2},{4,5},{5,4},{6,7},{7,6},{8,9},{9,8},{10,11... | collective-permute-start | bytes 1032200 | tf_op jit(solution)/shard_map/ppermute | solution.py:316
  138.9 5.0 %collective-permute-start.21 = (bf16[256,3584]{1,0:T(8,128)(2,1)S(1)}, bf16[256,3584]{1,0:T(8,128)(2,1)S(1)}, u32[]{:S(2)}, u32[]{:S(2)}) collective-permute-start(bf16[256,3584]{1,0:T(8,128)(2,1)S(1)} %shard_map.52.refs_1_), channel_id=1, source_target_pairs={{0,4},{4,0},{8,12},{12,8},{16,20},{20,16},{24,28},{28,24},{1,5},{5... | collective-permute-start | bytes 5505032 | tf_op jit(solution)/shard_map/ppermute | solution.py:319
  139.1 14.3 %collective-permute-start.13 = (bf16[2,336,256]{2,1,0:T(8,128)(2,1)S(1)}, bf16[2,336,256]{2,1,0:T(8,128)(2,1)S(1)}, u32[]{:S(2)}, u32[]{:S(2)}) collective-permute-start(bf16[2,336,256]{2,1,0:T(8,128)(2,1)S(1)} %pad_maximum_fusion), channel_id=1, source_target_pairs={{0,24},{4,28},{8,16},{12,20},{16,8},{20,12},{24,0},{28,4},{1,25},{... | collective-permute-start | bytes 1032200 | tf_op jit(solution)/shard_map/ppermute | solution.py:331
  140.8 6.8 %collective-permute-start.18 = (bf16[336,256]{1,0:T(8,128)(2,1)S(1)}, bf16[336,256]{1,0:T(8,128)(2,1)S(1)}, u32[]{:S(2)}, u32[]{:S(2)}) collective-permute-start(bf16[336,256]{1,0:T(8,128)(2,1)S(1)} %get-tuple-element.46.refs_4_), channel_id=1, source_target_pairs={{0,4},{4,0},{8,12},{12,8},{16,20},{20,16},{24,28},{28,24},{1,5},{5... | collective-permute-start | bytes 516104 | tf_op jit(solution)/shard_map/ppermute | solution.py:319
  142.4 8.7 %collective-permute-start.23 = (bf16[1,336,256]{2,1,0:T(8,128)(2,1)S(1)}, bf16[1,336,256]{2,1,0:T(8,128)(2,1)S(1)}, u32[]{:S(2)}, u32[]{:S(2)}) collective-permute-start(bf16[1,336,256]{2,1,0:T(8,128)(2,1)S(1)} %get-tuple-element.47.refs_3_), channel_id=1, source_target_pairs={{0,1},{1,0},{2,3},{3,2},{4,5},{5,4},{6,7},{7,6},{8,9},{9,8},{10,11... | collective-permute-start | bytes 516104 | tf_op jit(solution)/shard_map/ppermute | solution.py:316
  145.4 6.4 %collective-permute-start.27 = (bf16[1,336,256]{2,1,0:T(8,128)(2,1)S(1)}, bf16[1,336,256]{2,1,0:T(8,128)(2,1)S(1)}, u32[]{:S(2)}, u32[]{:S(2)}) collective-permute-start(bf16[1,336,256]{2,1,0:T(8,128)(2,1)S(1)} %get-tuple-element.48.refs_5_), channel_id=1, source_target_pairs={{0,2},{1,3},{2,0},{3,1},{4,6},{5,7},{6,4},{7,5},{8,10},{9,11},{10,... | collective-permute-start | bytes 516104 | tf_op jit(solution)/shard_map/ppermute | solution.py:316
  147.0 8.0 %collective-permute-start.22 = (bf16[1,336,256]{2,1,0:T(8,128)(2,1)S(1)}, bf16[1,336,256]{2,1,0:T(8,128)(2,1)S(1)}, u32[]{:S(2)}, u32[]{:S(2)}) collective-permute-start(bf16[1,336,256]{2,1,0:T(8,128)(2,1)S(1)} %get-tuple-element.50), channel_id=1, source_target_pairs={{0,1},{1,0},{2,3},{3,2},{4,5},{5,4},{6,7},{7,6},{8,9},{9,8},{10,11... | collective-permute-start | bytes 516104 | tf_op jit(solution)/shard_map/ppermute | solution.py:316
  147.6 24.4 %collective-permute-start.19 = (bf16[2,336,256]{2,1,0:T(8,128)(2,1)S(1)}, bf16[2,336,256]{2,1,0:T(8,128)(2,1)S(1)}, u32[]{:S(2)}, u32[]{:S(2)}) collective-permute-start(bf16[2,336,256]{2,1,0:T(8,128)(2,1)S(1)} %pad_maximum_fusion.1), channel_id=1, source_target_pairs={{0,8},{4,12},{8,24},{12,28},{16,0},{20,4},{24,16},{28,20},{1,9},{5... | collective-permute-start | bytes 1032200 | tf_op jit(solution)/shard_map/ppermute | solution.py:331
  151.1 3.9 %copy-start = (f32[2688]{0:T(1024)S(1)}, f32[2688]{0:T(1024)}, u32[]{:S(2)}) copy-start(f32[2688]{0:T(1024)} %param.5) | copy-start | bytes 32260
  151.2 7.4 %collective-permute-start.24 = (bf16[1,336,256]{2,1,0:T(8,128)(2,1)S(1)}, bf16[1,336,256]{2,1,0:T(8,128)(2,1)S(1)}, u32[]{:S(2)}, u32[]{:S(2)}) collective-permute-start(bf16[1,336,256]{2,1,0:T(8,128)(2,1)S(1)} %shard_map.56), channel_id=1, source_target_pairs={{0,2},{1,3},{2,0},{3,1},{4,6},{5,7},{6,4},{7,5},{8,10},{9,11},{10,... | collective-permute-start | bytes 516104 | tf_op jit(solution)/shard_map/ppermute | solution.py:316
  151.8 9.3 %collective-permute-start.26 = (bf16[1,336,256]{2,1,0:T(8,128)(2,1)S(1)}, bf16[1,336,256]{2,1,0:T(8,128)(2,1)S(1)}, u32[]{:S(2)}, u32[]{:S(2)}) collective-permute-start(bf16[1,336,256]{2,1,0:T(8,128)(2,1)S(1)} %get-tuple-element.53), channel_id=1, source_target_pairs={{0,2},{1,3},{2,0},{3,1},{4,6},{5,7},{6,4},{7,5},{8,10},{9,11},{10,... | collective-permute-start | bytes 516104 | tf_op jit(solution)/shard_map/ppermute | solution.py:316
  153.4 7.7 %collective-permute-start.28 = (bf16[1,336,256]{2,1,0:T(8,128)(2,1)S(1)}, bf16[1,336,256]{2,1,0:T(8,128)(2,1)S(1)}, u32[]{:S(2)}, u32[]{:S(2)}) collective-permute-start(bf16[1,336,256]{2,1,0:T(8,128)(2,1)S(1)} %shard_map.58), channel_id=1, source_target_pairs={{0,1},{1,0},{2,3},{3,2},{4,5},{5,4},{6,7},{7,6},{8,9},{9,8},{10,11... | collective-permute-start | bytes 516104 | tf_op jit(solution)/shard_map/ppermute | solution.py:316
  155.0 17.0 %collective-permute-start.14 = (bf16[336,384]{1,0:T(8,128)(2,1)S(1)}, bf16[336,384]{1,0:T(8,128)(2,1)S(1)}, u32[]{:S(2)}, u32[]{:S(2)}) collective-permute-start(bf16[336,384]{1,0:T(8,128)(2,1)S(1)} %pad_maximum_fusion.2), channel_id=1, source_target_pairs={{0,4},{4,0},{8,12},{12,8},{16,20},{20,16},{24,28},{28,24},{1,5},{5... | collective-permute-start | bytes 774152 | tf_op jit(solution)/shard_map/ppermute | solution.py:319
  158.7 13.3 %collective-permute-start.25 = (bf16[336,256]{1,0:T(8,128)(2,1)S(1)}, bf16[336,256]{1,0:T(8,128)(2,1)S(1)}, u32[]{:S(2)}, u32[]{:S(2)}) collective-permute-start(bf16[336,256]{1,0:T(8,128)(2,1)S(1)} %shard_map.57), channel_id=1, source_target_pairs={{0,16},{4,20},{8,0},{12,4},{16,24},{20,28},{24,8},{28,12},{1,17},{... | collective-permute-start | bytes 516104 | tf_op jit(solution)/shard_map/ppermute | solution.py:425
  161.2 10.8 %collective-permute-start.29 = (bf16[336,256]{1,0:T(8,128)(2,1)S(1)}, bf16[336,256]{1,0:T(8,128)(2,1)S(1)}, u32[]{:S(2)}, u32[]{:S(2)}) collective-permute-start(bf16[336,256]{1,0:T(8,128)(2,1)S(1)} %shard_map.59), channel_id=1, source_target_pairs={{0,20},{4,16},{8,4},{12,0},{16,28},{20,24},{24,12},{28,8},{1,21},{... | collective-permute-start | bytes 516104 | tf_op jit(solution)/shard_map/ppermute | solution.py:425

commit v6 on v5

--- a/solution.py
+++ b/solution.py
@@ -10,6 +10,8 @@
 ROOM = 14 * 1024 * 1024
 KEPT = 0
 BACKS = 0
+CUTS = 1
+XCUTS = 2
 IN_VMEM = pl.BlockSpec(memory_space=pltpu.VMEM)
 IN_HBM = pl.BlockSpec(memory_space=pltpu.HBM)
 ANYWHERE = pl.BlockSpec(memory_space=pl.ANY)
@@ -20,16 +22,14 @@
     return max(d for d in range(128, most + 1, 128) if size % d == 0)
 
 
-def bands_kernel(pieces, n_col, n_x, *refs):
+def bands_kernel(pieces, n_col, *refs):
     outs, sems = refs[-1 - len(pieces) : -1], refs[-1]
     col = lax.axis_index("col")
     copies = []
-    for i, (which, j, first, rows) in enumerate(pieces):
-        band = refs[which].shape[1] // n_col
-        start = pl.multiple_of((col ^ j) * band, 128)
-        copies.append(
-            pltpu.make_async_copy(refs[which].at[pl.ds(first, rows), pl.ds(start, band)], outs[i], sems.at[i])
-        )
+    for i, (which, j, part) in enumerate(pieces):
+        band, width = refs[which].shape[1] // n_col, outs[i].shape[1]
+        start = pl.multiple_of((col ^ j) * band + part * width, 128)
+        copies.append(pltpu.make_async_copy(refs[which].at[:, pl.ds(start, width)], outs[i], sems.at[i]))
     for copy in copies:
         copy.start()
     for copy in copies:
@@ -37,11 +37,10 @@
 
 
 def bands(xs, pieces, n_col, after):
-    return pl.pallas_call(
-        functools.partial(bands_kernel, pieces, n_col, len(xs)),
-        out_shape=[
-            jax.ShapeDtypeStruct((rows, xs[which].shape[1] // n_col), xs[which].dtype) for which, _, _, rows in pieces
-        ],
+    shapes = [(xs[which].shape[0], xs[which].shape[1] // n_col // parts) for which, _, _, parts in pieces]
+    return pl.pallas_call(
+        functools.partial(bands_kernel, [piece[:3] for piece in pieces], n_col),
+        out_shape=[jax.ShapeDtypeStruct(shape, xs[piece[0]].dtype) for shape, piece in zip(shapes, pieces)],
         in_specs=[IN_HBM] * len(xs) + [ANYWHERE] * len(after),
         out_specs=[IN_VMEM] * len(pieces),
         scratch_shapes=[pltpu.SemaphoreType.DMA((len(pieces),))],
@@ -49,35 +48,46 @@
     )(*[pltpu.with_memory_space_constraint(x, pltpu.HBM) for x in xs], *after)
 
 
-def choose_kernel(wanted, n, *refs):
-    x_refs, outs, sem = refs[:n], refs[n:-1], refs[-1]
+def choose_kernel(wanted, counts, cuts, *refs):
+    outs, sem = refs[-1 - cuts : -1], refs[-1]
     plane = lax.axis_index("row") // 2
-    for i, x in enumerate(x_refs):
+    at = 0
+    for i, count in enumerate(counts):
+        pieces = refs[at : at + count]
+        at += count
         here = functools.reduce(jnp.logical_or, [plane == p for p, w in enumerate(wanted) if w == i])
 
         @pl.when(here)
         def _():
-            first, copies = 0, []
-            for k, out in enumerate(outs):
-                width = out.shape[1]
-                copies.append(pltpu.make_async_copy(x.at[:, pl.ds(first, width)], out, sem.at[k]))
-                first += width
+            n = max(count, cuts)
+            width = pieces[0].shape[1] * count // n
+            copies = []
+            for k in range(n):
+                source, from_col = k * count // n, k * width % pieces[0].shape[1]
+                target, to_col = k * cuts // n, k * width % outs[0].shape[1]
+                copies.append(
+                    pltpu.make_async_copy(
+                        pieces[source].at[:, pl.ds(from_col, width)], outs[target].at[:, pl.ds(to_col, width)], sem.at[k]
+                    )
+                )
             for copy in copies:
                 copy.start()
             for copy in copies:
                 copy.wait()
 
 
-def choose(xs, wanted, after, cuts):
-    rows, width = xs[0].shape
-    return pl.pallas_call(
-        lambda *refs: choose_kernel(wanted, len(xs), *refs[: len(xs)], *refs[len(xs) + len(after) :]),
-        out_shape=[jax.ShapeDtypeStruct((rows, width // cuts), xs[0].dtype)] * cuts,
-        in_specs=[ANYWHERE] * (len(xs) + len(after)),
+def choose(xs, wanted, after, cuts=1):
+    flat = [piece for x in xs for piece in x]
+    counts = [len(x) for x in xs]
+    shape = (flat[0].shape[0], sum(piece.shape[1] for piece in xs[0]) // cuts)
+    return pl.pallas_call(
+        lambda *refs: choose_kernel(wanted, counts, cuts, *refs[: len(flat)], *refs[len(flat) + len(after) :]),
+        out_shape=[jax.ShapeDtypeStruct(shape, flat[0].dtype)] * cuts,
+        in_specs=[ANYWHERE] * (len(flat) + len(after)),
         out_specs=[IN_VMEM] * cuts,
-        scratch_shapes=[pltpu.SemaphoreType.DMA((cuts,))],
-        compiler_params=pltpu.CompilerParams(vmem_limit_bytes=ROOM),
-    )(*xs, *after)
+        scratch_shapes=[pltpu.SemaphoreType.DMA((max(counts + [cuts]),))],
+        compiler_params=pltpu.CompilerParams(vmem_limit_bytes=ROOM),
+    )(*flat, *after)
 
 
 def pass_kernel(*refs):
@@ -146,34 +156,44 @@
     )(*[pltpu.with_memory_space_constraint(x, pltpu.HBM) for x in (w, t0)], t1)
 
 
-def product_kernel(plan, n_in, *refs):
+def product_kernel(plan, *refs):
     outs = refs[len(refs) - len(plan) :]
     for out, (ws, ts) in zip(outs, plan):
-        for i, w in enumerate(ws):
-            for k, t in enumerate(ts):
-                rows = refs[t].shape[0]
-                out[i, :, k * rows : (k + 1) * rows] = lax.dot_general(
-                    refs[w][...], refs[t][...], BOTH_LAST, preferred_element_type=jnp.float32
-                ).astype(out.dtype)
+        for i, (w,) in enumerate(ws):
+            for k, pieces in enumerate(ts):
+                total, start = 0.0, 0
+                for t in pieces:
+                    rows, width = refs[t].shape
+                    total += lax.dot_general(
+                        refs[w][:, start : start + width],
+                        refs[t][...],
+                        BOTH_LAST,
+                        preferred_element_type=jnp.float32,
+                    )
+                    start += width
+                out[i, :, k * rows : (k + 1) * rows] = total.astype(out.dtype)
 
 
 def products(jobs, dtype, after, flops=0):
     arrays, plan, shapes = [], [], []
     for ws, ts in jobs:
         places = []
-        for group in (ws, ts):
+        for group in ([(w,) for w in ws], ts):
             place = []
             for x in group:
-                known = [i for i, y in enumerate(arrays) if y is x]
-                if not known:
-                    arrays.append(x)
-                place.append(known[0] if known else len(arrays) - 1)
+                at = []
+                for piece in x:
+                    known = [i for i, y in enumerate(arrays) if y is piece]
+                    if not known:
+                        arrays.append(piece)
+                    at.append(known[0] if known else len(arrays) - 1)
+                place.append(tuple(at))
             places.append(place)
         plan.append(tuple(places))
-        shapes.append((len(ws), ws[0].shape[0], sum(t.shape[0] for t in ts)))
+        shapes.append((len(ws), ws[0].shape[0], sum(t[0].shape[0] for t in ts)))
     size = sum(a * b * c for a, b, c in shapes)
     return pl.pallas_call(
-        functools.partial(product_kernel, plan, len(arrays)),
+        functools.partial(product_kernel, plan),
         in_specs=[IN_VMEM] * len(arrays) + [ANYWHERE] * len(after),
         out_specs=[IN_VMEM] * len(jobs),
         out_shape=[jax.ShapeDtypeStruct(shape, dtype) for shape in shapes],
@@ -254,6 +274,7 @@
 
 
 def chain(own, planes, send, after):
+    (own,) = own
     held = []
     last = {0: own, 1: own}
     second = []
@@ -284,23 +305,23 @@
     for d in slots + [planes - 1]:
         wanted = [next(i for i, (_, came) in enumerate(held) if came.get(p) == p ^ d) for p in range(planes)]
         used = sorted(set(wanted))
-        found.append(([held[i][0] for i in used], [used.index(i) for i in wanted], [p ^ d for p in range(planes)]))
+        found.append(([[held[i][0]] for i in used], [used.index(i) for i in wanted], [p ^ d for p in range(planes)]))
     return found, second
 
 
 def line_of_four(own, send, after):
     ends = [0, 1, 1, 0]
     swap = [(0, 1), (1, 0), (2, 3), (3, 2)]
-    cross = send(own, [(0, 3), (3, 0)])
-    (out,) = choose([cross, own], ends, after, 1)
+    cross = [send(piece, [(0, 3), (3, 0)]) for piece in own]
+    (out,) = choose([cross, own], ends, after)
     near = send(out, swap)
     inner = send(out, [(1, 2), (2, 1)])
-    (out,) = choose([own, inner], ends, [near], 1)
+    (out,) = choose([own, [inner]], ends, [])
     final = send(out, swap)
     slots = [
-        ([cross, inner], ends, [3, 2, 1, 0]),
-        ([near], [0, 0, 0, 0], [1, 3, 0, 2]),
-        ([final], [0, 0, 0, 0], [2, 0, 3, 1]),
+        ([cross, [inner]], ends, [3, 2, 1, 0]),
+        ([[near]], [0, 0, 0, 0], [1, 3, 0, 2]),
+        ([[final]], [0, 0, 0, 0], [2, 0, 3, 1]),
     ]
     return slots, [near, inner]
 
@@ -319,8 +340,11 @@
         return lax.ppermute(x, "row", [(i, i ^ j) for i in range(n_row)])
 
     js = list(range(n_col))
-    own, far = bands([tokens, weight], [(0, 0, 0, half), (1, n_col - 1, 0, columns)], n_col, [])
-    near = bands([weight], [(0, j, 0, columns) for j in js[:-1]], n_col, [far])
+    cuts = CUTS if n_row == 8 else 1
+    *own, far = bands(
+        [tokens, weight], [(0, 0, part, cuts) for part in range(cuts)] + [(1, n_col - 1, 0, 1)], n_col, []
+    )
+    near = bands([weight], [(0, j, 0, 1) for j in js[:-1]], n_col, [far])
     w_band = [near[0]] + [flip_col(x, j) for j, x in zip(js[1:], list(near[1:]) + [far])]
     here = deep_product(weight, tokens, flip_row(tokens, 1))
     here_other = flip_row(here[:, half:], 1)
@@ -335,10 +359,10 @@
     else:
         slots, second = chain(own, planes, send, [here_other, near[0]])
 
-    def arrived(slot, after):
+    def arrived(slot, after, cuts=1):
         arrays, wanted, _ = slot
-        (value,) = choose(arrays, wanted, after, 1)
-        return [value, flip_row(value, 1)]
+        value = choose(arrays, wanted, after, cuts)
+        return [tuple(value), tuple(flip_row(x, 1) for x in value)]
 
     def apart(x):
         return [x] if x.shape[0] == 1 else [x[i : i + 1] for i in range(x.shape[0])]
@@ -361,7 +385,8 @@
     last_j = n_col - 1
 
     early = list(range(planes - 2))
-    blocks = {d: arrived(slots[d], second + [w_band[last_j]]) for d in early}
+    late_in = flip_row(choose([[second[-1]]], [0] * planes, [], 14)[0], 1)
+    blocks = {d: arrived(slots[d], second + [w_band[last_j]] + [late_in] * (not d), XCUTS if d else 1) for d in early}
     firsts = products([([w_band[last_j]], blocks[d]) for d in early], jnp.bfloat16, [])
     got_first = [flip_col(x, orders[i][0]) for i, x in enumerate(firsts)]
     nexts = products(

time: 174 us -> 171 us (0.983)
  starting transfers between devices: 40.5 us -> 34.6 us
    ppermute x6, starting transfers between devices: 14.3 us -> 8.42 us  [send(): lax.ppermute(x, 'row', [(2 * a + c, 2 * b + c) for a, b in pairs for c in...]
    ppermute x6, waiting for transfers between devices: 60.7 us -> 56 us  [send(): lax.ppermute(x, 'row', [(2 * a + c, 2 * b + c) for a, b in pairs for c in...]
    ppermute x7 -> x9, waiting for transfers between devices: 1.39 us -> 5.28 us  [flip_row(): return lax.ppermute(x, 'row', [(i, i ^ j) for i in range(n_row)])]
    ppermute x2, waiting for transfers between devices: 0.01 us -> 3.78 us  [shards(): parts.append((source, core, lax.ppermute(done, 'row', home)))]
    ppermute x15, waiting for transfers between devices: 36.6 us -> 33.9 us  [flip_col(): return lax.ppermute(x, 'col', [(i, i ^ j) for i in range(n_col)])]
    pallas_call x14 -> x15, Pallas kernels: 22.5 us -> 24 us  [the longest x7 16.2 us: products(): pl.pallas_call(functools.partial(product_kernel, plan), in_specs=[IN_VMEM...]
  transfers between devices with their start and end apart: 30 -> 32, of which waited for: 11 -> 14; matrix products, arithmetic and copies ran while one was open for 0% -> 0% of each run, Pallas kernels for 18% -> 20%
where the time goes in v6:
time: 171 us; the launch traced here: 170 us
  waiting for transfers between devices  99 us (58%)
  Pallas kernels  35.7 us (21%)
  starting transfers between devices  34.6 us (20%)
    ppermute x6, waiting for transfers between devices, send(): lax.ppermute(x, 'row', [(2 * a + c, 2 * b + c) for a, b in pairs for c in...  56 us
    ppermute x15, waiting for transfers between devices, flip_col(): return lax.ppermute(x, 'col', [(i, i ^ j) for i in range(n_col)])  33.9 us
    ppermute x15, starting transfers between devices, flip_col(): return lax.ppermute(x, 'col', [(i, i ^ j) for i in range(n_col)])  21.1 us
    pallas_call x7, Pallas kernels, products(): pl.pallas_call(functools.partial(product_kernel, plan), in_specs=[IN_VMEM...  16.2 us
    pallas_call x1, Pallas kernels, deep_product(): pl.pallas_call(deep_kernel, grid=(depth // block,), in_specs=[pl.BlockSpe...  9.13 us
    ppermute x6, starting transfers between devices, send(): lax.ppermute(x, 'row', [(2 * a + c, 2 * b + c) for a, b in pairs for c in...  8.42 us
    pallas_call x2, Pallas kernels, bands(): pl.pallas_call(functools.partial(bands_kernel, [piece[:3] for piece in pi...  5.41 us
    ppermute x9, waiting for transfers between devices, flip_row(): return lax.ppermute(x, 'row', [(i, i ^ j) for i in range(n_row)])  5.28 us
  transfers between devices with their start and end apart: 32, of which 14 were waited for; matrix products, arithmetic and copies ran while one was open for 0% of the time, Pallas kernels for 20%

profile of v6, /device:TPU:0, one launch (start us, length us, event | category | flops | bytes accessed | tf_op | source)
XLA Modules:
  0.0 169.9 jit_solution(1529472932691113950)
XLA Ops:
  0.0 0.5 collective-permute-start
  0.5 2.2 %shard_map.38 = (bf16[256,3584]{1,0:T(8,128)(2,1)S(1)}, bf16[336,3584]{1,0:T(8,128)(2,1)S(1)}) custom-call(bf16[256,14336]{1,0:T(8,128)(2,1)} %refs_0_.1, bf16[336,14336]{1,0:T(8,128)(2,1)} %bitcast.18), custom_call_target="tpu_custom_call" | custom-call | tf_op jit(solution)/shard_map/pallas_call | solution.py:41
  2.7 6.5 %collective-permute-start.2 = (bf16[256,3584]{1,0:T(8,128)(2,1)S(1)}, bf16[256,3584]{1,0:T(8,128)(2,1)S(1)}, u32[]{:S(2)}, u32[]{:S(2)}) collective-permute-start(bf16[256,3584]{1,0:T(8,128)(2,1)S(1)} %get-tuple-element.35.refs_1_.refs_0_), channel_id=1, source_target_pairs={{0,24},{4,28},{24,0},{28,4},{1,25},{5,29},{25,1},{29,5},{2,26},{6,... | collective-permute-start | bytes 5505032 | tf_op jit(solution)/shard_map/ppermute | solution.py:355
  9.2 2.5 %collective-permute-start.5 = (bf16[336,3584]{1,0:T(8,128)(2,1)S(1)}, bf16[336,3584]{1,0:T(8,128)(2,1)S(1)}, u32[]{:S(2)}, u32[]{:S(2)}) collective-permute-start(bf16[336,3584]{1,0:T(8,128)(2,1)S(1)} %get-tuple-element.33.refs_1_), channel_id=1, source_target_pairs={{0,3},{1,2},{2,1},{3,0},{4,7},{5,6},{6,5},{7,4},{8,11},{9,10},{10,... | collective-permute-start | bytes 7225352 | tf_op jit(solution)/shard_map/ppermute | solution.py:337
  11.7 0.2 collective-permute-done.t1
  11.9 9.1 %shard_map.37 = bf16[336,512]{1,0:T(8,128)(2,1)S(1)} custom-call(bf16[336,14336]{1,0:T(8,128)(2,1)} %bitcast.19, bf16[256,14336]{1,0:T(8,128)(2,1)} %refs_0_.1, bf16[256,14336]{1,0:T(8,128)(2,1)S(1)} %collective-permute-done.t1), custom_call_target="tpu_custom_call" | custom-call | flops 4932501504 | bytes 24313856 | tf_op jit(solution)/shard_map/pallas_call | solution.py:145
  21.1 0.4 collective-permute-start.1
  21.6 3.2 %shard_map.39 = (bf16[336,3584]{1,0:T(8,128)(2,1)S(1)}, bf16[336,3584]{1,0:T(8,128)(2,1)S(1)}, bf16[336,3584]{1,0:T(8,128)(2,1)S(1)}) custom-call(bf16[336,14336]{1,0:T(8,128)(2,1)} %bitcast.20, bf16[336,3584]{1,0:T(8,128)(2,1)S(1)} %get-tuple-element.33.refs_1_), custom_call_target="tpu_custom_call" | custom-call | tf_op jit(solution)/shard_map/pallas_call | solution.py:41
  24.7 25.3 %collective-permute-done.2.refs_0_ = bf16[256,3584]{1,0:T(8,128)(2,1)S(1)} collective-permute-done((bf16[256,3584]{1,0:T(8,128)(2,1)S(1)}, bf16[256,3584]{1,0:T(8,128)(2,1)S(1)}, u32[]{:S(2)}, u32[]{:S(2)}) %collective-permute-start.2) | collective-permute-done | bytes 1835040 | tf_op jit(solution)/shard_map/ppermute | solution.py:355
  50.0 0.1 shard_map.40
  50.1 0.8 collective-permute-start.3
  50.9 0.1 collective-permute-start.4
  51.0 1.6 collective-permute-start.10
  52.6 1.5 collective-permute-start.11
  54.1 1.5 shard_map.41
  55.6 0.1 collective-permute-start.6
  55.6 9.7 %collective-permute-done.5.refs_4_.refs_3_.refs_0_ = bf16[336,3584]{1,0:T(8,128)(2,1)S(1)} collective-permute-done((bf16[336,3584]{1,0:T(8,128)(2,1)S(1)}, bf16[336,3584]{1,0:T(8,128)(2,1)S(1)}, u32[]{:S(2)}, u32[]{:S(2)}) %collective-permute-start.5) | collective-permute-done | bytes 2408480 | tf_op jit(solution)/shard_map/ppermute | solution.py:337
  65.4 27.4 %collective-permute-done.4.refs_2_.refs_0_.refs_1_ = bf16[256,3584]{1,0:T(8,128)(2,1)S(1)} collective-permute-done((bf16[256,3584]{1,0:T(8,128)(2,1)S(1)}, bf16[256,3584]{1,0:T(8,128)(2,1)S(1)}, u32[]{:S(2)}, u32[]{:S(2)}) %collective-permute-start.4) | collective-permute-done | bytes 1835040 | tf_op jit(solution)/shard_map/ppermute | solution.py:355
  92.8 0.1 shard_map.43
  92.9 0.1 collective-permute-start.8
  93.0 0.2 shard_map.42.refs_1_
  93.2 0.5 collective-permute-start.7
  93.7 0.1 shard_map.52
  93.9 0.3 collective-permute-start.22
  94.2 1.3 collective-permute-done.8.refs_5_.refs_6_
  95.5 0.1 collective-permute-start.9
  95.6 3.8 %collective-permute-done.9.refs_6_.refs_7_ = bf16[256,1792]{1,0:T(8,128)(2,1)S(1)} collective-permute-done((bf16[256,1792]{1,0:T(8,128)(2,1)S(1)}, bf16[256,1792]{1,0:T(8,128)(2,1)S(1)}, u32[]{:S(2)}, u32[]{:S(2)}) %collective-permute-start.9) | collective-permute-done | bytes 917536 | tf_op jit(solution)/shard_map/ppermute | solution.py:340
  99.4 2.7 %shard_map.44 = (bf16[1,336,512]{2,1,0:T(8,128)(2,1)S(1)}, bf16[1,336,512]{2,1,0:T(8,128)(2,1)S(1)}) custom-call(bf16[336,3584]{1,0:T(8,128)(2,1)S(1)} %collective-permute-done.5.refs_4_.refs_3_.refs_0_, bf16[256,3584]{1,0:T(8,128)(2,1)S(1)} %shard_map.42.refs_1_, bf16[256,3584]{1,0:T(8,128)(2,1)S(1)} %collective-permute-done.7.refs_2_, ...), custom_call_target="tpu_custom_call" | custom-call | flops 344064 | bytes 344064 | tf_op jit(solution)/shard_map/pallas_call | solution.py:195
  102.1 1.4 collective-permute-start.13
  103.5 1.5 collective-permute-start.18
  105.1 11.3 %collective-permute-done.10.refs_3_.refs_0_.refs_2_ = bf16[336,3584]{1,0:T(8,128)(2,1)S(1)} collective-permute-done((bf16[336,3584]{1,0:T(8,128)(2,1)S(1)}, bf16[336,3584]{1,0:T(8,128)(2,1)S(1)}, u32[]{:S(2)}, u32[]{:S(2)}) %collective-permute-start.10) | collective-permute-done | bytes 2408480 | tf_op jit(solution)/shard_map/ppermute | solution.py:337
  116.3 0.7 collective-permute-done.11.refs_0_.refs_3_.refs_2_.refs_4_
  117.0 2.7 %shard_map.45 = (bf16[1,336,512]{2,1,0:T(8,128)(2,1)S(1)}, bf16[1,336,512]{2,1,0:T(8,128)(2,1)S(1)}) custom-call(bf16[336,3584]{1,0:T(8,128)(2,1)S(1)} %collective-permute-done.11.refs_0_.refs_3_.refs_2_.refs_4_, bf16[256,3584]{1,0:T(8,128)(2,1)S(1)} %shard_map.42.refs_1_, bf16[256,3584]{1,0:T(8,128)(2,1)S(1)} %collective-permute-done.7.refs_2_, ...), custom_call_target="tpu_custom_call" | custom-call | flops 344064 | bytes 344064 | tf_op jit(solution)/shard_map/pallas_call | solution.py:195
  119.7 0.9 collective-permute-start.17
  120.6 1.5 collective-permute-start.12
  122.1 2.7 %shard_map.46 = (f32[1,336,512]{2,1,0:T(8,128)S(1)}, f32[1,336,512]{2,1,0:T(8,128)S(1)}) custom-call(bf16[336,3584]{1,0:T(8,128)(2,1)S(1)} %collective-permute-done.10.refs_3_.refs_0_.refs_2_, bf16[256,3584]{1,0:T(8,128)(2,1)S(1)} %shard_map.42.refs_1_, bf16[256,3584]{1,0:T(8,128)(2,1)S(1)} %collective-permute-done.7.refs_2_, ...), custom_call_target="tpu_custom_call" | custom-call | flops 344064 | bytes 344064 | tf_op jit(solution)/shard_map/pallas_call | solution.py:195
  124.8 1.3 collective-permute-start.14
  126.2 0.6 collective-permute-start.19
  126.8 2.7 %shard_map.47 = (f32[1,336,512]{2,1,0:T(8,128)S(1)}, f32[1,336,512]{2,1,0:T(8,128)S(1)}) custom-call(bf16[336,3584]{1,0:T(8,128)(2,1)S(1)} %get-tuple-element.34.refs_3_.refs_0_, bf16[256,3584]{1,0:T(8,128)(2,1)S(1)} %shard_map.42.refs_1_, bf16[256,3584]{1,0:T(8,128)(2,1)S(1)} %collective-permute-done.7.refs_2_, ...), custom_call_target="tpu_custom_call" | custom-call | flops 344064 | bytes 344064 | tf_op jit(solution)/shard_map/pallas_call | solution.py:195
  129.5 2.3 %collective-permute-done.12.refs_1_ = bf16[1,336,512]{2,1,0:T(8,128)(2,1)S(1)} collective-permute-done((bf16[1,336,512]{2,1,0:T(8,128)(2,1)S(1)}, bf16[1,336,512]{2,1,0:T(8,128)(2,1)S(1)}, u32[]{:S(2)}, u32[]{:S(2)}) %collective-permute-start.12) | collective-permute-done | bytes 344096 | tf_op jit(solution)/shard_map/ppermute | solution.py:337
  131.8 6.6 %collective-permute-done.14.refs_2_ = bf16[1,336,512]{2,1,0:T(8,128)(2,1)S(1)} collective-permute-done((bf16[1,336,512]{2,1,0:T(8,128)(2,1)S(1)}, bf16[1,336,512]{2,1,0:T(8,128)(2,1)S(1)}, u32[]{:S(2)}, u32[]{:S(2)}) %collective-permute-start.14) | collective-permute-done | bytes 344096 | tf_op jit(solution)/shard_map/ppermute | solution.py:337
  138.4 0.1 shard_map.49
  138.5 0.1 shard_map.51
  138.6 0.3 shard_map.53.refs_1_
  138.9 0.1 collective-permute-start.23
  139.1 0.7 collective-permute-start.15
  139.7 0.2 collective-permute-start.20
  139.9 1.4 shard_map.54
  141.4 1.6 collective-permute-start.25
  142.9 1.4 shard_map.55
  144.4 1.6 collective-permute-start.29
  146.0 1.4 collective-permute-start.24
  147.4 2.7 %shard_map.56 = (f32[1,336,256]{2,1,0:T(8,128)S(1)}, f32[1,336,256]{2,1,0:T(8,128)S(1)}, f32[1,336,256]{2,1,0:T(8,128)S(1)}, f32[1,336,256]{2,1,0:T(8,128)S(1)}) custom-call(bf16[336,3584]{1,0:T(8,128)(2,1)S(1)} %get-tuple-element.34.refs_3_.refs_0_, bf16[256,3584]{1,0:T(8,128)(2,1)S(1)} %shard_map.53.refs_1_, ...), custom_call_target="tpu_custom_call" | custom-call | flops 344064 | bytes 344064 | tf_op jit(solution)/shard_map/pallas_call | solution.py:195
  150.2 0.6 collective-permute-start.26
  150.8 1.5 collective-permute-start.28
  152.3 1.7 %collective-permute-start.30 = (bf16[1,336,256]{2,1,0:T(8,128)(2,1)S(1)}, bf16[1,336,256]{2,1,0:T(8,128)(2,1)S(1)}, u32[]{:S(2)}, u32[]{:S(2)}) collective-permute-start(bf16[1,336,256]{2,1,0:T(8,128)(2,1)S(1)} %shard_map.59), channel_id=1, source_target_pairs={{0,1},{1,0},{2,3},{3,2},{4,5},{5,4},{6,7},{7,6},{8,9},{9,8},{10,11... | collective-permute-start | bytes 516104 | tf_op jit(solution)/shard_map/ppermute | solution.py:337
  154.1 0.1 collective-permute-start.16
  154.2 3.3 %collective-permute-done.26.refs_2_ = bf16[1,336,256]{2,1,0:T(8,128)(2,1)S(1)} collective-permute-done((bf16[1,336,256]{2,1,0:T(8,128)(2,1)S(1)}, bf16[1,336,256]{2,1,0:T(8,128)(2,1)S(1)}, u32[]{:S(2)}, u32[]{:S(2)}) %collective-permute-start.26) | collective-permute-done | bytes 172064 | tf_op jit(solution)/shard_map/ppermute | solution.py:337
  157.5 0.1 shard_map.58
  157.6 3.0 %collective-permute-start.27 = (bf16[336,256]{1,0:T(8,128)(2,1)S(1)}, bf16[336,256]{1,0:T(8,128)(2,1)S(1)}, u32[]{:S(2)}, u32[]{:S(2)}) collective-permute-start(bf16[336,256]{1,0:T(8,128)(2,1)S(1)} %shard_map.58), channel_id=1, source_target_pairs={{0,16},{4,20},{8,0},{12,4},{16,24},{20,28},{24,8},{28,12},{1,17},{... | collective-permute-start | bytes 516104 | tf_op jit(solution)/shard_map/ppermute | solution.py:450
  160.7 3.3 %collective-permute-done.21 = bf16[2,336,256]{2,1,0:T(8,128)(2,1)S(1)} collective-permute-done((bf16[2,336,256]{2,1,0:T(8,128)(2,1)S(1)}, bf16[2,336,256]{2,1,0:T(8,128)(2,1)S(1)}, u32[]{:S(2)}, u32[]{:S(2)}) %collective-permute-start.21) | collective-permute-done | bytes 344096 | tf_op jit(solution)/shard_map/ppermute | solution.py:355
  164.1 3.2 %collective-permute-done.27.refs_6_ = bf16[336,256]{1,0:T(8,128)(2,1)S(1)} collective-permute-done((bf16[336,256]{1,0:T(8,128)(2,1)S(1)}, bf16[336,256]{1,0:T(8,128)(2,1)S(1)}, u32[]{:S(2)}, u32[]{:S(2)}) %collective-permute-start.27) | collective-permute-done | bytes 172064 | tf_op jit(solution)/shard_map/ppermute | solution.py:450
  167.2 0.6 collective-permute-done.31.refs_7_
  167.8 2.1 %shard_map.61 = bf16[256,2688]{1,0:T(8,128)(2,1)} custom-call(bf16[336,256]{1,0:T(8,128)(2,1)S(1)} %get-tuple-element.66.refs_0_, bf16[336,256]{1,0:T(8,128)(2,1)S(1)} %collective-permute-done.1.refs_2_.refs_1_, bf16[336,256]{1,0:T(8,128)(2,1)S(1)} %slice.37.refs_2_, bf16[336,256]{1,0:T(8,128)(2,1)S(1)} %get-tuple-element.63.refs_3_, ...), custom_call_target="tpu_custom_call" | custom-call | flops 688128 | bytes 2752512 | tf_op jit(solution)/shard_map/pallas_call | solution.py:265
  (36 shorter events, 0.6 us)
Async XLA Ops:
  0.0 11.9 %collective-permute-start = (bf16[256,14336]{1,0:T(8,128)(2,1)}, bf16[256,14336]{1,0:T(8,128)(2,1)S(1)}, u32[]{:S(2)}, u32[]{:S(2)}) collective-permute-start(bf16[256,14336]{1,0:T(8,128)(2,1)} %refs_0_.1), channel_id=1, source_target_pairs={{0,4},{4,0},{8,12},{12,8},{16,20},{20,16},{24,28},{28,24},{1,5},{5... | collective-permute-start | bytes 22020104 | tf_op jit(solution)/shard_map/ppermute | solution.py:340
  2.7 47.3 %collective-permute-start.2 = (bf16[256,3584]{1,0:T(8,128)(2,1)S(1)}, bf16[256,3584]{1,0:T(8,128)(2,1)S(1)}, u32[]{:S(2)}, u32[]{:S(2)}) collective-permute-start(bf16[256,3584]{1,0:T(8,128)(2,1)S(1)} %get-tuple-element.35.refs_1_.refs_0_), channel_id=1, source_target_pairs={{0,24},{4,28},{24,0},{28,4},{1,25},{5,29},{25,1},{29,5},{2,26},{6,... | collective-permute-start | bytes 5505032 | tf_op jit(solution)/shard_map/ppermute | solution.py:355
  9.2 56.1 %collective-permute-start.5 = (bf16[336,3584]{1,0:T(8,128)(2,1)S(1)}, bf16[336,3584]{1,0:T(8,128)(2,1)S(1)}, u32[]{:S(2)}, u32[]{:S(2)}) collective-permute-start(bf16[336,3584]{1,0:T(8,128)(2,1)S(1)} %get-tuple-element.33.refs_1_), channel_id=1, source_target_pairs={{0,3},{1,2},{2,1},{3,0},{4,7},{5,6},{6,5},{7,4},{8,11},{9,10},{10,... | collective-permute-start | bytes 7225352 | tf_op jit(solution)/shard_map/ppermute | solution.py:337
  21.1 28.9 %collective-permute-start.1 = (bf16[336,256]{1,0:T(8,128)(2,1)S(1)}, bf16[336,256]{1,0:T(8,128)(2,1)S(1)}, u32[]{:S(2)}, u32[]{:S(2)}) collective-permute-start(bf16[336,256]{1,0:T(8,128)(2,1)S(1)} %get-tuple-element.65), channel_id=1, source_target_pairs={{0,4},{4,0},{8,12},{12,8},{16,20},{20,16},{24,28},{28,24},{1,5},{5... | collective-permute-start | bytes 516104 | tf_op jit(solution)/shard_map/ppermute | solution.py:340
  50.1 3.9 %collective-permute-start.3 = (bf16[256,3584]{1,0:T(8,128)(2,1)S(1)}, bf16[256,3584]{1,0:T(8,128)(2,1)S(1)}, u32[]{:S(2)}, u32[]{:S(2)}) collective-permute-start(bf16[256,3584]{1,0:T(8,128)(2,1)S(1)} %shard_map.40), channel_id=1, source_target_pairs={{8,16},{12,20},{16,8},{20,12},{9,17},{13,21},{17,9},{21,13},{10,18... | collective-permute-start | bytes 5505032 | tf_op jit(solution)/shard_map/ppermute | solution.py:355
  50.9 41.9 %collective-permute-start.4 = (bf16[256,3584]{1,0:T(8,128)(2,1)S(1)}, bf16[256,3584]{1,0:T(8,128)(2,1)S(1)}, u32[]{:S(2)}, u32[]{:S(2)}) collective-permute-start(bf16[256,3584]{1,0:T(8,128)(2,1)S(1)} %shard_map.40), channel_id=1, source_target_pairs={{0,8},{4,12},{8,0},{12,4},{16,24},{20,28},{24,16},{28,20},{1,9},{5... | collective-permute-start | bytes 5505032 | tf_op jit(solution)/shard_map/ppermute | solution.py:355
  51.0 65.3 %collective-permute-start.10 = (bf16[336,3584]{1,0:T(8,128)(2,1)S(1)}, bf16[336,3584]{1,0:T(8,128)(2,1)S(1)}, u32[]{:S(2)}, u32[]{:S(2)}) collective-permute-start(bf16[336,3584]{1,0:T(8,128)(2,1)S(1)} %get-tuple-element.39), channel_id=1, source_target_pairs={{0,2},{1,3},{2,0},{3,1},{4,6},{5,7},{6,4},{7,5},{8,10},{9,11},{10,... | collective-permute-start | bytes 7225352 | tf_op jit(solution)/shard_map/ppermute | solution.py:337
  52.6 64.4 %collective-permute-start.11 = (bf16[336,3584]{1,0:T(8,128)(2,1)S(1)}, bf16[336,3584]{1,0:T(8,128)(2,1)S(1)}, u32[]{:S(2)}, u32[]{:S(2)}) collective-permute-start(bf16[336,3584]{1,0:T(8,128)(2,1)S(1)} %get-tuple-element.40), channel_id=1, source_target_pairs={{0,1},{1,0},{2,3},{3,2},{4,5},{5,4},{6,7},{7,6},{8,9},{9,8},{10,11... | collective-permute-start | bytes 7225352 | tf_op jit(solution)/shard_map/ppermute | solution.py:337
  55.6 37.5 %collective-permute-start.6 = (bf16[256,256]{1,0:T(8,128)(2,1)S(1)}, bf16[256,256]{1,0:T(8,128)(2,1)S(1)}, u32[]{:S(2)}, u32[]{:S(2)}) collective-permute-start(bf16[256,256]{1,0:T(8,128)(2,1)S(1)} %get-tuple-element.36), channel_id=1, source_target_pairs={{0,4},{4,0},{8,12},{12,8},{16,20},{20,16},{24,28},{28,24},{1,5},{5... | collective-permute-start | bytes 393224 | tf_op jit(solution)/shard_map/ppermute | solution.py:340
  92.9 2.5 %collective-permute-start.8 = (bf16[256,1792]{1,0:T(8,128)(2,1)S(1)}, bf16[256,1792]{1,0:T(8,128)(2,1)S(1)}, u32[]{:S(2)}, u32[]{:S(2)}) collective-permute-start(bf16[256,1792]{1,0:T(8,128)(2,1)S(1)} %get-tuple-element.37.refs_3_.refs_4_), channel_id=1, source_target_pairs={{0,4},{4,0},{8,12},{12,8},{16,20},{20,16},{24,28},{28,24},{1,5},{5... | collective-permute-start | bytes 2752520 | tf_op jit(solution)/shard_map/ppermute | solution.py:340
  93.2 6.2 %collective-permute-start.7 = (bf16[256,3584]{1,0:T(8,128)(2,1)S(1)}, bf16[256,3584]{1,0:T(8,128)(2,1)S(1)}, u32[]{:S(2)}, u32[]{:S(2)}) collective-permute-start(bf16[256,3584]{1,0:T(8,128)(2,1)S(1)} %shard_map.42.refs_1_), channel_id=1, source_target_pairs={{0,4},{4,0},{8,12},{12,8},{16,20},{20,16},{24,28},{28,24},{1,5},{5... | collective-permute-start | bytes 5505032 | tf_op jit(solution)/shard_map/ppermute | solution.py:340
  93.9 44.7 %collective-permute-start.22 = (bf16[256,3584]{1,0:T(8,128)(2,1)S(1)}, bf16[256,3584]{1,0:T(8,128)(2,1)S(1)}, u32[]{:S(2)}, u32[]{:S(2)}) collective-permute-start(bf16[256,3584]{1,0:T(8,128)(2,1)S(1)} %shard_map.52), channel_id=1, source_target_pairs={{0,8},{4,12},{8,0},{12,4},{16,24},{20,28},{24,16},{28,20},{1,9},{5... | collective-permute-start | bytes 5505032 | tf_op jit(solution)/shard_map/ppermute | solution.py:355
  95.5 3.9 %collective-permute-start.9 = (bf16[256,1792]{1,0:T(8,128)(2,1)S(1)}, bf16[256,1792]{1,0:T(8,128)(2,1)S(1)}, u32[]{:S(2)}, u32[]{:S(2)}) collective-permute-start(bf16[256,1792]{1,0:T(8,128)(2,1)S(1)} %get-tuple-element.38.refs_4_.refs_5_), channel_id=1, source_target_pairs={{0,4},{4,0},{8,12},{12,8},{16,20},{20,16},{24,28},{28,24},{1,5},{5... | collective-permute-start | bytes 2752520 | tf_op jit(solution)/shard_map/ppermute | solution.py:340
  102.1 22.7 %collective-permute-start.13 = (bf16[1,336,512]{2,1,0:T(8,128)(2,1)S(1)}, bf16[1,336,512]{2,1,0:T(8,128)(2,1)S(1)}, u32[]{:S(2)}, u32[]{:S(2)}) collective-permute-start(bf16[1,336,512]{2,1,0:T(8,128)(2,1)S(1)} %get-tuple-element.41.refs_8_), channel_id=1, source_target_pairs={{0,1},{1,0},{2,3},{3,2},{4,5},{5,4},{6,7},{7,6},{8,9},{9,8},{10,11... | collective-permute-start | bytes 1032200 | tf_op jit(solution)/shard_map/ppermute | solution.py:337
  103.5 22.6 %collective-permute-start.18 = (bf16[1,336,512]{2,1,0:T(8,128)(2,1)S(1)}, bf16[1,336,512]{2,1,0:T(8,128)(2,1)S(1)}, u32[]{:S(2)}, u32[]{:S(2)}) collective-permute-start(bf16[1,336,512]{2,1,0:T(8,128)(2,1)S(1)} %get-tuple-element.50), channel_id=1, source_target_pairs={{0,2},{1,3},{2,0},{3,1},{4,6},{5,7},{6,4},{7,5},{8,10},{9,11},{10,... | collective-permute-start | bytes 1032200 | tf_op jit(solution)/shard_map/ppermute | solution.py:337
  119.7 18.7 %collective-permute-start.17 = (bf16[1,336,512]{2,1,0:T(8,128)(2,1)S(1)}, bf16[1,336,512]{2,1,0:T(8,128)(2,1)S(1)}, u32[]{:S(2)}, u32[]{:S(2)}) collective-permute-start(bf16[1,336,512]{2,1,0:T(8,128)(2,1)S(1)} %get-tuple-element.48), channel_id=1, source_target_pairs={{0,2},{1,3},{2,0},{3,1},{4,6},{5,7},{6,4},{7,5},{8,10},{9,11},{10,... | collective-permute-start | bytes 1032200 | tf_op jit(solution)/shard_map/ppermute | solution.py:337
  120.6 11.2 %collective-permute-start.12 = (bf16[1,336,512]{2,1,0:T(8,128)(2,1)S(1)}, bf16[1,336,512]{2,1,0:T(8,128)(2,1)S(1)}, u32[]{:S(2)}, u32[]{:S(2)}) collective-permute-start(bf16[1,336,512]{2,1,0:T(8,128)(2,1)S(1)} %get-tuple-element.42.refs_8_), channel_id=1, source_target_pairs={{0,1},{1,0},{2,3},{3,2},{4,5},{5,4},{6,7},{7,6},{8,9},{9,8},{10,11... | collective-permute-start | bytes 1032200 | tf_op jit(solution)/shard_map/ppermute | solution.py:337
  124.8 13.5 %collective-permute-start.14 = (bf16[1,336,512]{2,1,0:T(8,128)(2,1)S(1)}, bf16[1,336,512]{2,1,0:T(8,128)(2,1)S(1)}, u32[]{:S(2)}, u32[]{:S(2)}) collective-permute-start(bf16[1,336,512]{2,1,0:T(8,128)(2,1)S(1)} %shard_map.48), channel_id=1, source_target_pairs={{0,2},{1,3},{2,0},{3,1},{4,6},{5,7},{6,4},{7,5},{8,10},{9,11},{10,... | collective-permute-start | bytes 1032200 | tf_op jit(solution)/shard_map/ppermute | solution.py:337
  126.2 12.3 %collective-permute-start.19 = (bf16[1,336,512]{2,1,0:T(8,128)(2,1)S(1)}, bf16[1,336,512]{2,1,0:T(8,128)(2,1)S(1)}, u32[]{:S(2)}, u32[]{:S(2)}) collective-permute-start(bf16[1,336,512]{2,1,0:T(8,128)(2,1)S(1)} %shard_map.50), channel_id=1, source_target_pairs={{0,1},{1,0},{2,3},{3,2},{4,5},{5,4},{6,7},{7,6},{8,9},{9,8},{10,11... | collective-permute-start | bytes 1032200 | tf_op jit(solution)/shard_map/ppermute | solution.py:337
  138.9 4.0 %collective-permute-start.23 = (bf16[256,3584]{1,0:T(8,128)(2,1)S(1)}, bf16[256,3584]{1,0:T(8,128)(2,1)S(1)}, u32[]{:S(2)}, u32[]{:S(2)}) collective-permute-start(bf16[256,3584]{1,0:T(8,128)(2,1)S(1)} %shard_map.53.refs_1_), channel_id=1, source_target_pairs={{0,4},{4,0},{8,12},{12,8},{16,20},{20,16},{24,28},{28,24},{1,5},{5... | collective-permute-start | bytes 5505032 | tf_op jit(solution)/shard_map/ppermute | solution.py:340
  139.1 13.3 %collective-permute-start.15 = (bf16[2,336,256]{2,1,0:T(8,128)(2,1)S(1)}, bf16[2,336,256]{2,1,0:T(8,128)(2,1)S(1)}, u32[]{:S(2)}, u32[]{:S(2)}) collective-permute-start(bf16[2,336,256]{2,1,0:T(8,128)(2,1)S(1)} %pad_maximum_fusion), channel_id=1, source_target_pairs={{0,24},{4,28},{8,16},{12,20},{16,8},{20,12},{24,0},{28,4},{1,25},{... | collective-permute-start | bytes 1032200 | tf_op jit(solution)/shard_map/ppermute | solution.py:355
  139.7 7.6 %collective-permute-start.20 = (bf16[336,256]{1,0:T(8,128)(2,1)S(1)}, bf16[336,256]{1,0:T(8,128)(2,1)S(1)}, u32[]{:S(2)}, u32[]{:S(2)}) collective-permute-start(bf16[336,256]{1,0:T(8,128)(2,1)S(1)} %get-tuple-element.52.refs_4_), channel_id=1, source_target_pairs={{0,4},{4,0},{8,12},{12,8},{16,20},{20,16},{24,28},{28,24},{1,5},{5... | collective-permute-start | bytes 516104 | tf_op jit(solution)/shard_map/ppermute | solution.py:340
  141.4 8.8 %collective-permute-start.25 = (bf16[1,336,256]{2,1,0:T(8,128)(2,1)S(1)}, bf16[1,336,256]{2,1,0:T(8,128)(2,1)S(1)}, u32[]{:S(2)}, u32[]{:S(2)}) collective-permute-start(bf16[1,336,256]{2,1,0:T(8,128)(2,1)S(1)} %get-tuple-element.53.refs_3_), channel_id=1, source_target_pairs={{0,1},{1,0},{2,3},{3,2},{4,5},{5,4},{6,7},{7,6},{8,9},{9,8},{10,11... | collective-permute-start | bytes 516104 | tf_op jit(solution)/shard_map/ppermute | solution.py:337
  144.4 6.4 %collective-permute-start.29 = (bf16[1,336,256]{2,1,0:T(8,128)(2,1)S(1)}, bf16[1,336,256]{2,1,0:T(8,128)(2,1)S(1)}, u32[]{:S(2)}, u32[]{:S(2)}) collective-permute-start(bf16[1,336,256]{2,1,0:T(8,128)(2,1)S(1)} %get-tuple-element.54.refs_5_), channel_id=1, source_target_pairs={{0,2},{1,3},{2,0},{3,1},{4,6},{5,7},{6,4},{7,5},{8,10},{9,11},{10,... | collective-permute-start | bytes 516104 | tf_op jit(solution)/shard_map/ppermute | solution.py:337
  146.0 8.2 %collective-permute-start.24 = (bf16[1,336,256]{2,1,0:T(8,128)(2,1)S(1)}, bf16[1,336,256]{2,1,0:T(8,128)(2,1)S(1)}, u32[]{:S(2)}, u32[]{:S(2)}) collective-permute-start(bf16[1,336,256]{2,1,0:T(8,128)(2,1)S(1)} %get-tuple-element.56), channel_id=1, source_target_pairs={{0,1},{1,0},{2,3},{3,2},{4,5},{5,4},{6,7},{7,6},{8,9},{9,8},{10,11... | collective-permute-start | bytes 516104 | tf_op jit(solution)/shard_map/ppermute | solution.py:337
  147.4 16.6 %collective-permute-start.21 = (bf16[2,336,256]{2,1,0:T(8,128)(2,1)S(1)}, bf16[2,336,256]{2,1,0:T(8,128)(2,1)S(1)}, u32[]{:S(2)}, u32[]{:S(2)}) collective-permute-start(bf16[2,336,256]{2,1,0:T(8,128)(2,1)S(1)} %pad_maximum_fusion.1), channel_id=1, source_target_pairs={{0,8},{4,12},{8,24},{12,28},{16,0},{20,4},{24,16},{28,20},{1,9},{5... | collective-permute-start | bytes 1032200 | tf_op jit(solution)/shard_map/ppermute | solution.py:355
  150.1 4.1 %copy-start = (f32[2688]{0:T(1024)S(1)}, f32[2688]{0:T(1024)}, u32[]{:S(2)}) copy-start(f32[2688]{0:T(1024)} %param.5) | copy-start | bytes 32260
  150.2 7.4 %collective-permute-start.26 = (bf16[1,336,256]{2,1,0:T(8,128)(2,1)S(1)}, bf16[1,336,256]{2,1,0:T(8,128)(2,1)S(1)}, u32[]{:S(2)}, u32[]{:S(2)}) collective-permute-start(bf16[1,336,256]{2,1,0:T(8,128)(2,1)S(1)} %shard_map.57), channel_id=1, source_target_pairs={{0,2},{1,3},{2,0},{3,1},{4,6},{5,7},{6,4},{7,5},{8,10},{9,11},{10,... | collective-permute-start | bytes 516104 | tf_op jit(solution)/shard_map/ppermute | solution.py:337
  150.8 9.8 %collective-permute-start.28 = (bf16[1,336,256]{2,1,0:T(8,128)(2,1)S(1)}, bf16[1,336,256]{2,1,0:T(8,128)(2,1)S(1)}, u32[]{:S(2)}, u32[]{:S(2)}) collective-permute-start(bf16[1,336,256]{2,1,0:T(8,128)(2,1)S(1)} %get-tuple-element.59), channel_id=1, source_target_pairs={{0,2},{1,3},{2,0},{3,1},{4,6},{5,7},{6,4},{7,5},{8,10},{9,11},{10,... | collective-permute-start | bytes 516104 | tf_op jit(solution)/shard_map/ppermute | solution.py:337
  152.3 8.3 %collective-permute-start.30 = (bf16[1,336,256]{2,1,0:T(8,128)(2,1)S(1)}, bf16[1,336,256]{2,1,0:T(8,128)(2,1)S(1)}, u32[]{:S(2)}, u32[]{:S(2)}) collective-permute-start(bf16[1,336,256]{2,1,0:T(8,128)(2,1)S(1)} %shard_map.59), channel_id=1, source_target_pairs={{0,1},{1,0},{2,3},{3,2},{4,5},{5,4},{6,7},{7,6},{8,9},{9,8},{10,11... | collective-permute-start | bytes 516104 | tf_op jit(solution)/shard_map/ppermute | solution.py:337
  154.1 9.9 %collective-permute-start.16 = (bf16[336,384]{1,0:T(8,128)(2,1)S(1)}, bf16[336,384]{1,0:T(8,128)(2,1)S(1)}, u32[]{:S(2)}, u32[]{:S(2)}) collective-permute-start(bf16[336,384]{1,0:T(8,128)(2,1)S(1)} %pad_maximum_fusion.2), channel_id=1, source_target_pairs={{0,4},{4,0},{8,12},{12,8},{16,20},{20,16},{24,28},{28,24},{1,5},{5... | collective-permute-start | bytes 774152 | tf_op jit(solution)/shard_map/ppermute | solution.py:340
  157.6 9.6 %collective-permute-start.27 = (bf16[336,256]{1,0:T(8,128)(2,1)S(1)}, bf16[336,256]{1,0:T(8,128)(2,1)S(1)}, u32[]{:S(2)}, u32[]{:S(2)}) collective-permute-start(bf16[336,256]{1,0:T(8,128)(2,1)S(1)} %shard_map.58), channel_id=1, source_target_pairs={{0,16},{4,20},{8,0},{12,4},{16,24},{20,28},{24,8},{28,12},{1,17},{... | collective-permute-start | bytes 516104 | tf_op jit(solution)/shard_map/ppermute | solution.py:450
  160.7 7.2 %collective-permute-start.31 = (bf16[336,256]{1,0:T(8,128)(2,1)S(1)}, bf16[336,256]{1,0:T(8,128)(2,1)S(1)}, u32[]{:S(2)}, u32[]{:S(2)}) collective-permute-start(bf16[336,256]{1,0:T(8,128)(2,1)S(1)} %shard_map.60), channel_id=1, source_target_pairs={{0,20},{4,16},{8,4},{12,0},{16,28},{20,24},{24,12},{28,8},{1,21},{... | collective-permute-start | bytes 516104 | tf_op jit(solution)/shard_map/ppermute | solution.py:450

commit v7 on v6

--- a/solution.py
+++ b/solution.py
@@ -11,7 +11,7 @@
 KEPT = 0
 BACKS = 0
 CUTS = 1
-XCUTS = 2
+XCUTS = 1
 IN_VMEM = pl.BlockSpec(memory_space=pltpu.VMEM)
 IN_HBM = pl.BlockSpec(memory_space=pltpu.HBM)
 ANYWHERE = pl.BlockSpec(memory_space=pl.ANY)

time: 171 us -> 171 us (level)
    ppermute x9 -> x8, waiting for transfers between devices: 5.28 us -> 5.42 us  [flip_row(): return lax.ppermute(x, 'row', [(i, i ^ j) for i in range(n_row)])]
  transfers between devices with their start and end apart: 32 -> 31, of which waited for: 14 -> 14; matrix products, arithmetic and copies ran while one was open for 0% -> 0% of each run, Pallas kernels for 20% -> 20%
where the time goes in v7:
time: 171 us; the launch traced here: 170 us
  waiting for transfers between devices  99.1 us (58%)
  Pallas kernels  35.7 us (21%)
  starting transfers between devices  34.5 us (20%)
    ppermute x6, waiting for transfers between devices, send(): lax.ppermute(x, 'row', [(2 * a + c, 2 * b + c) for a, b in pairs for c in...  56 us
    ppermute x15, waiting for transfers between devices, flip_col(): return lax.ppermute(x, 'col', [(i, i ^ j) for i in range(n_col)])  34 us
    ppermute x15, starting transfers between devices, flip_col(): return lax.ppermute(x, 'col', [(i, i ^ j) for i in range(n_col)])  21.1 us
    pallas_call x7, Pallas kernels, products(): pl.pallas_call(functools.partial(product_kernel, plan), in_specs=[IN_VMEM...  16.2 us
    pallas_call x1, Pallas kernels, deep_product(): pl.pallas_call(deep_kernel, grid=(depth // block,), in_specs=[pl.BlockSpe...  9.13 us
    ppermute x6, starting transfers between devices, send(): lax.ppermute(x, 'row', [(2 * a + c, 2 * b + c) for a, b in pairs for c in...  8.41 us
    ppermute x8, waiting for transfers between devices, flip_row(): return lax.ppermute(x, 'row', [(i, i ^ j) for i in range(n_row)])  5.42 us
    pallas_call x2, Pallas kernels, bands(): pl.pallas_call(functools.partial(bands_kernel, [piece[:3] for piece in pi...  5.41 us
  transfers between devices with their start and end apart: 31, of which 14 were waited for; matrix products, arithmetic and copies ran while one was open for 0% of the time, Pallas kernels for 20%

profile of v7, /device:TPU:0, one launch (start us, length us, event | category | flops | bytes accessed | tf_op | source)
XLA Modules:
  0.0 169.9 jit_solution(1775125943327781394)
XLA Ops:
  0.0 0.5 collective-permute-start
  0.5 2.2 %shard_map.38 = (bf16[256,3584]{1,0:T(8,128)(2,1)S(1)}, bf16[336,3584]{1,0:T(8,128)(2,1)S(1)}) custom-call(bf16[256,14336]{1,0:T(8,128)(2,1)} %refs_0_.1, bf16[336,14336]{1,0:T(8,128)(2,1)} %bitcast.18), custom_call_target="tpu_custom_call" | custom-call | tf_op jit(solution)/shard_map/pallas_call | solution.py:41
  2.7 6.5 %collective-permute-start.2 = (bf16[256,3584]{1,0:T(8,128)(2,1)S(1)}, bf16[256,3584]{1,0:T(8,128)(2,1)S(1)}, u32[]{:S(2)}, u32[]{:S(2)}) collective-permute-start(bf16[256,3584]{1,0:T(8,128)(2,1)S(1)} %get-tuple-element.33.refs_1_.refs_0_), channel_id=1, source_target_pairs={{0,24},{4,28},{24,0},{28,4},{1,25},{5,29},{25,1},{29,5},{2,26},{6,... | collective-permute-start | bytes 5505032 | tf_op jit(solution)/shard_map/ppermute | solution.py:355
  9.2 2.5 %collective-permute-start.5 = (bf16[336,3584]{1,0:T(8,128)(2,1)S(1)}, bf16[336,3584]{1,0:T(8,128)(2,1)S(1)}, u32[]{:S(2)}, u32[]{:S(2)}) collective-permute-start(bf16[336,3584]{1,0:T(8,128)(2,1)S(1)} %get-tuple-element.31.refs_1_), channel_id=1, source_target_pairs={{0,3},{1,2},{2,1},{3,0},{4,7},{5,6},{6,5},{7,4},{8,11},{9,10},{10,... | collective-permute-start | bytes 7225352 | tf_op jit(solution)/shard_map/ppermute | solution.py:337
  11.7 0.2 collective-permute-done.t1
  11.9 9.1 %shard_map.37 = bf16[336,512]{1,0:T(8,128)(2,1)S(1)} custom-call(bf16[336,14336]{1,0:T(8,128)(2,1)} %bitcast.19, bf16[256,14336]{1,0:T(8,128)(2,1)} %refs_0_.1, bf16[256,14336]{1,0:T(8,128)(2,1)S(1)} %collective-permute-done.t1), custom_call_target="tpu_custom_call" | custom-call | flops 4932501504 | bytes 24313856 | tf_op jit(solution)/shard_map/pallas_call | solution.py:145
  21.1 0.4 collective-permute-start.1
  21.6 3.2 %shard_map.39 = (bf16[336,3584]{1,0:T(8,128)(2,1)S(1)}, bf16[336,3584]{1,0:T(8,128)(2,1)S(1)}, bf16[336,3584]{1,0:T(8,128)(2,1)S(1)}) custom-call(bf16[336,14336]{1,0:T(8,128)(2,1)} %bitcast.20, bf16[336,3584]{1,0:T(8,128)(2,1)S(1)} %get-tuple-element.31.refs_1_), custom_call_target="tpu_custom_call" | custom-call | tf_op jit(solution)/shard_map/pallas_call | solution.py:41
  24.7 25.3 %collective-permute-done.2.refs_0_ = bf16[256,3584]{1,0:T(8,128)(2,1)S(1)} collective-permute-done((bf16[256,3584]{1,0:T(8,128)(2,1)S(1)}, bf16[256,3584]{1,0:T(8,128)(2,1)S(1)}, u32[]{:S(2)}, u32[]{:S(2)}) %collective-permute-start.2) | collective-permute-done | bytes 1835040 | tf_op jit(solution)/shard_map/ppermute | solution.py:355
  50.0 0.1 shard_map.40
  50.1 0.8 collective-permute-start.3
  50.9 0.1 collective-permute-start.4
  51.0 1.6 collective-permute-start.9
  52.6 1.5 collective-permute-start.10
  54.1 1.4 shard_map.41
  55.5 0.1 collective-permute-start.6
  55.6 9.7 %collective-permute-done.5.refs_4_.refs_3_.refs_0_ = bf16[336,3584]{1,0:T(8,128)(2,1)S(1)} collective-permute-done((bf16[336,3584]{1,0:T(8,128)(2,1)S(1)}, bf16[336,3584]{1,0:T(8,128)(2,1)S(1)}, u32[]{:S(2)}, u32[]{:S(2)}) %collective-permute-start.5) | collective-permute-done | bytes 2408480 | tf_op jit(solution)/shard_map/ppermute | solution.py:337
  65.4 27.4 %collective-permute-done.4.refs_2_.refs_0_.refs_1_ = bf16[256,3584]{1,0:T(8,128)(2,1)S(1)} collective-permute-done((bf16[256,3584]{1,0:T(8,128)(2,1)S(1)}, bf16[256,3584]{1,0:T(8,128)(2,1)S(1)}, u32[]{:S(2)}, u32[]{:S(2)}) %collective-permute-start.4) | collective-permute-done | bytes 1835040 | tf_op jit(solution)/shard_map/ppermute | solution.py:355
  92.8 0.1 shard_map.43.refs_3_.refs_4_
  92.9 0.1 collective-permute-start.8
  93.0 0.2 shard_map.42.refs_1_
  93.2 0.5 collective-permute-start.7
  93.7 0.1 shard_map.52
  93.9 0.3 collective-permute-start.21
  94.2 2.6 %collective-permute-done.8.refs_4_.refs_5_ = bf16[256,3584]{1,0:T(8,128)(2,1)S(1)} collective-permute-done((bf16[256,3584]{1,0:T(8,128)(2,1)S(1)}, bf16[256,3584]{1,0:T(8,128)(2,1)S(1)}, u32[]{:S(2)}, u32[]{:S(2)}) %collective-permute-start.8) | collective-permute-done | bytes 1835040 | tf_op jit(solution)/shard_map/ppermute | solution.py:340
  96.8 2.6 %collective-permute-done.7.refs_2_ = bf16[256,3584]{1,0:T(8,128)(2,1)S(1)} collective-permute-done((bf16[256,3584]{1,0:T(8,128)(2,1)S(1)}, bf16[256,3584]{1,0:T(8,128)(2,1)S(1)}, u32[]{:S(2)}, u32[]{:S(2)}) %collective-permute-start.7) | collective-permute-done | bytes 1835040 | tf_op jit(solution)/shard_map/ppermute | solution.py:340
  99.4 2.7 %shard_map.44 = (bf16[1,336,512]{2,1,0:T(8,128)(2,1)S(1)}, bf16[1,336,512]{2,1,0:T(8,128)(2,1)S(1)}) custom-call(bf16[336,3584]{1,0:T(8,128)(2,1)S(1)} %collective-permute-done.5.refs_4_.refs_3_.refs_0_, bf16[256,3584]{1,0:T(8,128)(2,1)S(1)} %shard_map.42.refs_1_, bf16[256,3584]{1,0:T(8,128)(2,1)S(1)} %collective-permute-done.7.refs_2_, ...), custom_call_target="tpu_custom_call" | custom-call | flops 344064 | bytes 344064 | tf_op jit(solution)/shard_map/pallas_call | solution.py:195
  102.1 1.4 collective-permute-start.12
  103.5 1.5 collective-permute-start.17
  105.0 11.3 %collective-permute-done.9.refs_3_.refs_0_.refs_2_ = bf16[336,3584]{1,0:T(8,128)(2,1)S(1)} collective-permute-done((bf16[336,3584]{1,0:T(8,128)(2,1)S(1)}, bf16[336,3584]{1,0:T(8,128)(2,1)S(1)}, u32[]{:S(2)}, u32[]{:S(2)}) %collective-permute-start.9) | collective-permute-done | bytes 2408480 | tf_op jit(solution)/shard_map/ppermute | solution.py:337
  116.3 0.7 collective-permute-done.10.refs_0_.refs_3_.refs_2_.refs_4_
  117.0 2.7 %shard_map.45 = (bf16[1,336,512]{2,1,0:T(8,128)(2,1)S(1)}, bf16[1,336,512]{2,1,0:T(8,128)(2,1)S(1)}) custom-call(bf16[336,3584]{1,0:T(8,128)(2,1)S(1)} %collective-permute-done.10.refs_0_.refs_3_.refs_2_.refs_4_, bf16[256,3584]{1,0:T(8,128)(2,1)S(1)} %shard_map.42.refs_1_, bf16[256,3584]{1,0:T(8,128)(2,1)S(1)} %collective-permute-done.7.refs_2_, ...), custom_call_target="tpu_custom_call" | custom-call | flops 344064 | bytes 344064 | tf_op jit(solution)/shard_map/pallas_call | solution.py:195
  119.7 0.9 collective-permute-start.16
  120.6 1.5 collective-permute-start.11
  122.1 2.7 %shard_map.46 = (f32[1,336,512]{2,1,0:T(8,128)S(1)}, f32[1,336,512]{2,1,0:T(8,128)S(1)}) custom-call(bf16[336,3584]{1,0:T(8,128)(2,1)S(1)} %collective-permute-done.9.refs_3_.refs_0_.refs_2_, bf16[256,3584]{1,0:T(8,128)(2,1)S(1)} %shard_map.42.refs_1_, bf16[256,3584]{1,0:T(8,128)(2,1)S(1)} %collective-permute-done.7.refs_2_, ...), custom_call_target="tpu_custom_call" | custom-call | flops 344064 | bytes 344064 | tf_op jit(solution)/shard_map/pallas_call | solution.py:195
  124.8 0.1 shard_map.48
  124.8 1.3 collective-permute-start.13
  126.2 0.6 collective-permute-start.18
  126.8 2.7 %shard_map.47 = (f32[1,336,512]{2,1,0:T(8,128)S(1)}, f32[1,336,512]{2,1,0:T(8,128)S(1)}) custom-call(bf16[336,3584]{1,0:T(8,128)(2,1)S(1)} %get-tuple-element.32.refs_3_.refs_0_, bf16[256,3584]{1,0:T(8,128)(2,1)S(1)} %shard_map.42.refs_1_, bf16[256,3584]{1,0:T(8,128)(2,1)S(1)} %collective-permute-done.7.refs_2_, ...), custom_call_target="tpu_custom_call" | custom-call | flops 344064 | bytes 344064 | tf_op jit(solution)/shard_map/pallas_call | solution.py:195
  129.5 2.3 %collective-permute-done.11.refs_1_ = bf16[1,336,512]{2,1,0:T(8,128)(2,1)S(1)} collective-permute-done((bf16[1,336,512]{2,1,0:T(8,128)(2,1)S(1)}, bf16[1,336,512]{2,1,0:T(8,128)(2,1)S(1)}, u32[]{:S(2)}, u32[]{:S(2)}) %collective-permute-start.11) | collective-permute-done | bytes 344096 | tf_op jit(solution)/shard_map/ppermute | solution.py:337
  131.8 6.6 %collective-permute-done.13.refs_2_ = bf16[1,336,512]{2,1,0:T(8,128)(2,1)S(1)} collective-permute-done((bf16[1,336,512]{2,1,0:T(8,128)(2,1)S(1)}, bf16[1,336,512]{2,1,0:T(8,128)(2,1)S(1)}, u32[]{:S(2)}, u32[]{:S(2)}) %collective-permute-start.13) | collective-permute-done | bytes 344096 | tf_op jit(solution)/shard_map/ppermute | solution.py:337
  138.4 0.1 shard_map.49
  138.5 0.1 shard_map.51
  138.6 0.3 shard_map.53.refs_1_
  138.9 0.1 collective-permute-start.22
  139.1 0.6 collective-permute-start.14
  139.7 0.2 collective-permute-start.19
  139.9 1.4 shard_map.54
  141.4 1.5 collective-permute-start.24
  142.9 1.4 shard_map.55
  144.4 1.6 collective-permute-start.28
  145.9 1.4 collective-permute-start.23
  147.4 2.7 %shard_map.56 = (f32[1,336,256]{2,1,0:T(8,128)S(1)}, f32[1,336,256]{2,1,0:T(8,128)S(1)}, f32[1,336,256]{2,1,0:T(8,128)S(1)}, f32[1,336,256]{2,1,0:T(8,128)S(1)}) custom-call(bf16[336,3584]{1,0:T(8,128)(2,1)S(1)} %get-tuple-element.32.refs_3_.refs_0_, bf16[256,3584]{1,0:T(8,128)(2,1)S(1)} %shard_map.53.refs_1_, ...), custom_call_target="tpu_custom_call" | custom-call | flops 344064 | bytes 344064 | tf_op jit(solution)/shard_map/pallas_call | solution.py:195
  150.2 0.6 collective-permute-start.25
  150.8 1.5 collective-permute-start.27
  152.3 1.7 %collective-permute-start.29 = (bf16[1,336,256]{2,1,0:T(8,128)(2,1)S(1)}, bf16[1,336,256]{2,1,0:T(8,128)(2,1)S(1)}, u32[]{:S(2)}, u32[]{:S(2)}) collective-permute-start(bf16[1,336,256]{2,1,0:T(8,128)(2,1)S(1)} %shard_map.59), channel_id=1, source_target_pairs={{0,1},{1,0},{2,3},{3,2},{4,5},{5,4},{6,7},{7,6},{8,9},{9,8},{10,11... | collective-permute-start | bytes 516104 | tf_op jit(solution)/shard_map/ppermute | solution.py:337
  154.1 0.1 collective-permute-start.15
  154.2 3.3 %collective-permute-done.25.refs_2_ = bf16[1,336,256]{2,1,0:T(8,128)(2,1)S(1)} collective-permute-done((bf16[1,336,256]{2,1,0:T(8,128)(2,1)S(1)}, bf16[1,336,256]{2,1,0:T(8,128)(2,1)S(1)}, u32[]{:S(2)}, u32[]{:S(2)}) %collective-permute-start.25) | collective-permute-done | bytes 172064 | tf_op jit(solution)/shard_map/ppermute | solution.py:337
  157.5 0.1 shard_map.58
  157.6 3.0 %collective-permute-start.26 = (bf16[336,256]{1,0:T(8,128)(2,1)S(1)}, bf16[336,256]{1,0:T(8,128)(2,1)S(1)}, u32[]{:S(2)}, u32[]{:S(2)}) collective-permute-start(bf16[336,256]{1,0:T(8,128)(2,1)S(1)} %shard_map.58), channel_id=1, source_target_pairs={{0,16},{4,20},{8,0},{12,4},{16,24},{20,28},{24,8},{28,12},{1,17},{... | collective-permute-start | bytes 516104 | tf_op jit(solution)/shard_map/ppermute | solution.py:450
  160.7 3.3 %collective-permute-done.20 = bf16[2,336,256]{2,1,0:T(8,128)(2,1)S(1)} collective-permute-done((bf16[2,336,256]{2,1,0:T(8,128)(2,1)S(1)}, bf16[2,336,256]{2,1,0:T(8,128)(2,1)S(1)}, u32[]{:S(2)}, u32[]{:S(2)}) %collective-permute-start.20) | collective-permute-done | bytes 344096 | tf_op jit(solution)/shard_map/ppermute | solution.py:355
  164.1 3.2 %collective-permute-done.26.refs_6_ = bf16[336,256]{1,0:T(8,128)(2,1)S(1)} collective-permute-done((bf16[336,256]{1,0:T(8,128)(2,1)S(1)}, bf16[336,256]{1,0:T(8,128)(2,1)S(1)}, u32[]{:S(2)}, u32[]{:S(2)}) %collective-permute-start.26) | collective-permute-done | bytes 172064 | tf_op jit(solution)/shard_map/ppermute | solution.py:450
  167.2 0.6 collective-permute-done.30.refs_7_
  167.8 2.1 %shard_map.61 = bf16[256,2688]{1,0:T(8,128)(2,1)} custom-call(bf16[336,256]{1,0:T(8,128)(2,1)S(1)} %get-tuple-element.62.refs_0_, bf16[336,256]{1,0:T(8,128)(2,1)S(1)} %collective-permute-done.1.refs_2_.refs_1_, bf16[336,256]{1,0:T(8,128)(2,1)S(1)} %slice.37.refs_2_, bf16[336,256]{1,0:T(8,128)(2,1)S(1)} %get-tuple-element.59.refs_3_, ...), custom_call_target="tpu_custom_call" | custom-call | flops 688128 | bytes 2752512 | tf_op jit(solution)/shard_map/pallas_call | solution.py:265
  (34 shorter events, 0.6 us)
Async XLA Ops:
  0.0 11.9 %collective-permute-start = (bf16[256,14336]{1,0:T(8,128)(2,1)}, bf16[256,14336]{1,0:T(8,128)(2,1)S(1)}, u32[]{:S(2)}, u32[]{:S(2)}) collective-permute-start(bf16[256,14336]{1,0:T(8,128)(2,1)} %refs_0_.1), channel_id=1, source_target_pairs={{0,4},{4,0},{8,12},{12,8},{16,20},{20,16},{24,28},{28,24},{1,5},{5... | collective-permute-start | bytes 22020104 | tf_op jit(solution)/shard_map/ppermute | solution.py:340
  2.7 47.3 %collective-permute-start.2 = (bf16[256,3584]{1,0:T(8,128)(2,1)S(1)}, bf16[256,3584]{1,0:T(8,128)(2,1)S(1)}, u32[]{:S(2)}, u32[]{:S(2)}) collective-permute-start(bf16[256,3584]{1,0:T(8,128)(2,1)S(1)} %get-tuple-element.33.refs_1_.refs_0_), channel_id=1, source_target_pairs={{0,24},{4,28},{24,0},{28,4},{1,25},{5,29},{25,1},{29,5},{2,26},{6,... | collective-permute-start | bytes 5505032 | tf_op jit(solution)/shard_map/ppermute | solution.py:355
  9.2 56.1 %collective-permute-start.5 = (bf16[336,3584]{1,0:T(8,128)(2,1)S(1)}, bf16[336,3584]{1,0:T(8,128)(2,1)S(1)}, u32[]{:S(2)}, u32[]{:S(2)}) collective-permute-start(bf16[336,3584]{1,0:T(8,128)(2,1)S(1)} %get-tuple-element.31.refs_1_), channel_id=1, source_target_pairs={{0,3},{1,2},{2,1},{3,0},{4,7},{5,6},{6,5},{7,4},{8,11},{9,10},{10,... | collective-permute-start | bytes 7225352 | tf_op jit(solution)/shard_map/ppermute | solution.py:337
  21.1 28.9 %collective-permute-start.1 = (bf16[336,256]{1,0:T(8,128)(2,1)S(1)}, bf16[336,256]{1,0:T(8,128)(2,1)S(1)}, u32[]{:S(2)}, u32[]{:S(2)}) collective-permute-start(bf16[336,256]{1,0:T(8,128)(2,1)S(1)} %get-tuple-element.61), channel_id=1, source_target_pairs={{0,4},{4,0},{8,12},{12,8},{16,20},{20,16},{24,28},{28,24},{1,5},{5... | collective-permute-start | bytes 516104 | tf_op jit(solution)/shard_map/ppermute | solution.py:340
  50.1 3.9 %collective-permute-start.3 = (bf16[256,3584]{1,0:T(8,128)(2,1)S(1)}, bf16[256,3584]{1,0:T(8,128)(2,1)S(1)}, u32[]{:S(2)}, u32[]{:S(2)}) collective-permute-start(bf16[256,3584]{1,0:T(8,128)(2,1)S(1)} %shard_map.40), channel_id=1, source_target_pairs={{8,16},{12,20},{16,8},{20,12},{9,17},{13,21},{17,9},{21,13},{10,18... | collective-permute-start | bytes 5505032 | tf_op jit(solution)/shard_map/ppermute | solution.py:355
  50.9 41.9 %collective-permute-start.4 = (bf16[256,3584]{1,0:T(8,128)(2,1)S(1)}, bf16[256,3584]{1,0:T(8,128)(2,1)S(1)}, u32[]{:S(2)}, u32[]{:S(2)}) collective-permute-start(bf16[256,3584]{1,0:T(8,128)(2,1)S(1)} %shard_map.40), channel_id=1, source_target_pairs={{0,8},{4,12},{8,0},{12,4},{16,24},{20,28},{24,16},{28,20},{1,9},{5... | collective-permute-start | bytes 5505032 | tf_op jit(solution)/shard_map/ppermute | solution.py:355
  51.0 65.3 %collective-permute-start.9 = (bf16[336,3584]{1,0:T(8,128)(2,1)S(1)}, bf16[336,3584]{1,0:T(8,128)(2,1)S(1)}, u32[]{:S(2)}, u32[]{:S(2)}) collective-permute-start(bf16[336,3584]{1,0:T(8,128)(2,1)S(1)} %get-tuple-element.35), channel_id=1, source_target_pairs={{0,2},{1,3},{2,0},{3,1},{4,6},{5,7},{6,4},{7,5},{8,10},{9,11},{10,... | collective-permute-start | bytes 7225352 | tf_op jit(solution)/shard_map/ppermute | solution.py:337
  52.6 64.4 %collective-permute-start.10 = (bf16[336,3584]{1,0:T(8,128)(2,1)S(1)}, bf16[336,3584]{1,0:T(8,128)(2,1)S(1)}, u32[]{:S(2)}, u32[]{:S(2)}) collective-permute-start(bf16[336,3584]{1,0:T(8,128)(2,1)S(1)} %get-tuple-element.36), channel_id=1, source_target_pairs={{0,1},{1,0},{2,3},{3,2},{4,5},{5,4},{6,7},{7,6},{8,9},{9,8},{10,11... | collective-permute-start | bytes 7225352 | tf_op jit(solution)/shard_map/ppermute | solution.py:337
  55.5 37.5 %collective-permute-start.6 = (bf16[256,256]{1,0:T(8,128)(2,1)S(1)}, bf16[256,256]{1,0:T(8,128)(2,1)S(1)}, u32[]{:S(2)}, u32[]{:S(2)}) collective-permute-start(bf16[256,256]{1,0:T(8,128)(2,1)S(1)} %get-tuple-element.34), channel_id=1, source_target_pairs={{0,4},{4,0},{8,12},{12,8},{16,20},{20,16},{24,28},{28,24},{1,5},{5... | collective-permute-start | bytes 393224 | tf_op jit(solution)/shard_map/ppermute | solution.py:340
  92.9 3.9 %collective-permute-start.8 = (bf16[256,3584]{1,0:T(8,128)(2,1)S(1)}, bf16[256,3584]{1,0:T(8,128)(2,1)S(1)}, u32[]{:S(2)}, u32[]{:S(2)}) collective-permute-start(bf16[256,3584]{1,0:T(8,128)(2,1)S(1)} %shard_map.43.refs_3_.refs_4_), channel_id=1, source_target_pairs={{0,4},{4,0},{8,12},{12,8},{16,20},{20,16},{24,28},{28,24},{1,5},{5... | collective-permute-start | bytes 5505032 | tf_op jit(solution)/shard_map/ppermute | solution.py:340
  93.2 6.2 %collective-permute-start.7 = (bf16[256,3584]{1,0:T(8,128)(2,1)S(1)}, bf16[256,3584]{1,0:T(8,128)(2,1)S(1)}, u32[]{:S(2)}, u32[]{:S(2)}) collective-permute-start(bf16[256,3584]{1,0:T(8,128)(2,1)S(1)} %shard_map.42.refs_1_), channel_id=1, source_target_pairs={{0,4},{4,0},{8,12},{12,8},{16,20},{20,16},{24,28},{28,24},{1,5},{5... | collective-permute-start | bytes 5505032 | tf_op jit(solution)/shard_map/ppermute | solution.py:340
  93.9 44.7 %collective-permute-start.21 = (bf16[256,3584]{1,0:T(8,128)(2,1)S(1)}, bf16[256,3584]{1,0:T(8,128)(2,1)S(1)}, u32[]{:S(2)}, u32[]{:S(2)}) collective-permute-start(bf16[256,3584]{1,0:T(8,128)(2,1)S(1)} %shard_map.52), channel_id=1, source_target_pairs={{0,8},{4,12},{8,0},{12,4},{16,24},{20,28},{24,16},{28,20},{1,9},{5... | collective-permute-start | bytes 5505032 | tf_op jit(solution)/shard_map/ppermute | solution.py:355
  102.1 22.7 %collective-permute-start.12 = (bf16[1,336,512]{2,1,0:T(8,128)(2,1)S(1)}, bf16[1,336,512]{2,1,0:T(8,128)(2,1)S(1)}, u32[]{:S(2)}, u32[]{:S(2)}) collective-permute-start(bf16[1,336,512]{2,1,0:T(8,128)(2,1)S(1)} %get-tuple-element.37.refs_6_), channel_id=1, source_target_pairs={{0,1},{1,0},{2,3},{3,2},{4,5},{5,4},{6,7},{7,6},{8,9},{9,8},{10,11... | collective-permute-start | bytes 1032200 | tf_op jit(solution)/shard_map/ppermute | solution.py:337
  103.5 22.6 %collective-permute-start.17 = (bf16[1,336,512]{2,1,0:T(8,128)(2,1)S(1)}, bf16[1,336,512]{2,1,0:T(8,128)(2,1)S(1)}, u32[]{:S(2)}, u32[]{:S(2)}) collective-permute-start(bf16[1,336,512]{2,1,0:T(8,128)(2,1)S(1)} %get-tuple-element.46), channel_id=1, source_target_pairs={{0,2},{1,3},{2,0},{3,1},{4,6},{5,7},{6,4},{7,5},{8,10},{9,11},{10,... | collective-permute-start | bytes 1032200 | tf_op jit(solution)/shard_map/ppermute | solution.py:337
  119.7 18.7 %collective-permute-start.16 = (bf16[1,336,512]{2,1,0:T(8,128)(2,1)S(1)}, bf16[1,336,512]{2,1,0:T(8,128)(2,1)S(1)}, u32[]{:S(2)}, u32[]{:S(2)}) collective-permute-start(bf16[1,336,512]{2,1,0:T(8,128)(2,1)S(1)} %get-tuple-element.44), channel_id=1, source_target_pairs={{0,2},{1,3},{2,0},{3,1},{4,6},{5,7},{6,4},{7,5},{8,10},{9,11},{10,... | collective-permute-start | bytes 1032200 | tf_op jit(solution)/shard_map/ppermute | solution.py:337
  120.6 11.2 %collective-permute-start.11 = (bf16[1,336,512]{2,1,0:T(8,128)(2,1)S(1)}, bf16[1,336,512]{2,1,0:T(8,128)(2,1)S(1)}, u32[]{:S(2)}, u32[]{:S(2)}) collective-permute-start(bf16[1,336,512]{2,1,0:T(8,128)(2,1)S(1)} %get-tuple-element.38.refs_6_), channel_id=1, source_target_pairs={{0,1},{1,0},{2,3},{3,2},{4,5},{5,4},{6,7},{7,6},{8,9},{9,8},{10,11... | collective-permute-start | bytes 1032200 | tf_op jit(solution)/shard_map/ppermute | solution.py:337
  124.8 13.5 %collective-permute-start.13 = (bf16[1,336,512]{2,1,0:T(8,128)(2,1)S(1)}, bf16[1,336,512]{2,1,0:T(8,128)(2,1)S(1)}, u32[]{:S(2)}, u32[]{:S(2)}) collective-permute-start(bf16[1,336,512]{2,1,0:T(8,128)(2,1)S(1)} %shard_map.48), channel_id=1, source_target_pairs={{0,2},{1,3},{2,0},{3,1},{4,6},{5,7},{6,4},{7,5},{8,10},{9,11},{10,... | collective-permute-start | bytes 1032200 | tf_op jit(solution)/shard_map/ppermute | solution.py:337
  126.2 12.3 %collective-permute-start.18 = (bf16[1,336,512]{2,1,0:T(8,128)(2,1)S(1)}, bf16[1,336,512]{2,1,0:T(8,128)(2,1)S(1)}, u32[]{:S(2)}, u32[]{:S(2)}) collective-permute-start(bf16[1,336,512]{2,1,0:T(8,128)(2,1)S(1)} %shard_map.50), channel_id=1, source_target_pairs={{0,1},{1,0},{2,3},{3,2},{4,5},{5,4},{6,7},{7,6},{8,9},{9,8},{10,11... | collective-permute-start | bytes 1032200 | tf_op jit(solution)/shard_map/ppermute | solution.py:337
  138.9 4.0 %collective-permute-start.22 = (bf16[256,3584]{1,0:T(8,128)(2,1)S(1)}, bf16[256,3584]{1,0:T(8,128)(2,1)S(1)}, u32[]{:S(2)}, u32[]{:S(2)}) collective-permute-start(bf16[256,3584]{1,0:T(8,128)(2,1)S(1)} %shard_map.53.refs_1_), channel_id=1, source_target_pairs={{0,4},{4,0},{8,12},{12,8},{16,20},{20,16},{24,28},{28,24},{1,5},{5... | collective-permute-start | bytes 5505032 | tf_op jit(solution)/shard_map/ppermute | solution.py:340
  139.1 13.2 %collective-permute-start.14 = (bf16[2,336,256]{2,1,0:T(8,128)(2,1)S(1)}, bf16[2,336,256]{2,1,0:T(8,128)(2,1)S(1)}, u32[]{:S(2)}, u32[]{:S(2)}) collective-permute-start(bf16[2,336,256]{2,1,0:T(8,128)(2,1)S(1)} %pad_maximum_fusion), channel_id=1, source_target_pairs={{0,24},{4,28},{8,16},{12,20},{16,8},{20,12},{24,0},{28,4},{1,25},{... | collective-permute-start | bytes 1032200 | tf_op jit(solution)/shard_map/ppermute | solution.py:355
  139.7 7.6 %collective-permute-start.19 = (bf16[336,256]{1,0:T(8,128)(2,1)S(1)}, bf16[336,256]{1,0:T(8,128)(2,1)S(1)}, u32[]{:S(2)}, u32[]{:S(2)}) collective-permute-start(bf16[336,256]{1,0:T(8,128)(2,1)S(1)} %get-tuple-element.48.refs_4_), channel_id=1, source_target_pairs={{0,4},{4,0},{8,12},{12,8},{16,20},{20,16},{24,28},{28,24},{1,5},{5... | collective-permute-start | bytes 516104 | tf_op jit(solution)/shard_map/ppermute | solution.py:340
  141.4 8.7 %collective-permute-start.24 = (bf16[1,336,256]{2,1,0:T(8,128)(2,1)S(1)}, bf16[1,336,256]{2,1,0:T(8,128)(2,1)S(1)}, u32[]{:S(2)}, u32[]{:S(2)}) collective-permute-start(bf16[1,336,256]{2,1,0:T(8,128)(2,1)S(1)} %get-tuple-element.49.refs_3_), channel_id=1, source_target_pairs={{0,1},{1,0},{2,3},{3,2},{4,5},{5,4},{6,7},{7,6},{8,9},{9,8},{10,11... | collective-permute-start | bytes 516104 | tf_op jit(solution)/shard_map/ppermute | solution.py:337
  144.4 6.4 %collective-permute-start.28 = (bf16[1,336,256]{2,1,0:T(8,128)(2,1)S(1)}, bf16[1,336,256]{2,1,0:T(8,128)(2,1)S(1)}, u32[]{:S(2)}, u32[]{:S(2)}) collective-permute-start(bf16[1,336,256]{2,1,0:T(8,128)(2,1)S(1)} %get-tuple-element.50.refs_5_), channel_id=1, source_target_pairs={{0,2},{1,3},{2,0},{3,1},{4,6},{5,7},{6,4},{7,5},{8,10},{9,11},{10,... | collective-permute-start | bytes 516104 | tf_op jit(solution)/shard_map/ppermute | solution.py:337
  145.9 8.2 %collective-permute-start.23 = (bf16[1,336,256]{2,1,0:T(8,128)(2,1)S(1)}, bf16[1,336,256]{2,1,0:T(8,128)(2,1)S(1)}, u32[]{:S(2)}, u32[]{:S(2)}) collective-permute-start(bf16[1,336,256]{2,1,0:T(8,128)(2,1)S(1)} %get-tuple-element.52), channel_id=1, source_target_pairs={{0,1},{1,0},{2,3},{3,2},{4,5},{5,4},{6,7},{7,6},{8,9},{9,8},{10,11... | collective-permute-start | bytes 516104 | tf_op jit(solution)/shard_map/ppermute | solution.py:337
  147.4 16.6 %collective-permute-start.20 = (bf16[2,336,256]{2,1,0:T(8,128)(2,1)S(1)}, bf16[2,336,256]{2,1,0:T(8,128)(2,1)S(1)}, u32[]{:S(2)}, u32[]{:S(2)}) collective-permute-start(bf16[2,336,256]{2,1,0:T(8,128)(2,1)S(1)} %pad_maximum_fusion.1), channel_id=1, source_target_pairs={{0,8},{4,12},{8,24},{12,28},{16,0},{20,4},{24,16},{28,20},{1,9},{5... | collective-permute-start | bytes 1032200 | tf_op jit(solution)/shard_map/ppermute | solution.py:355
  150.1 4.1 %copy-start = (f32[2688]{0:T(1024)S(1)}, f32[2688]{0:T(1024)}, u32[]{:S(2)}) copy-start(f32[2688]{0:T(1024)} %param.5) | copy-start | bytes 32260
  150.2 7.4 %collective-permute-start.25 = (bf16[1,336,256]{2,1,0:T(8,128)(2,1)S(1)}, bf16[1,336,256]{2,1,0:T(8,128)(2,1)S(1)}, u32[]{:S(2)}, u32[]{:S(2)}) collective-permute-start(bf16[1,336,256]{2,1,0:T(8,128)(2,1)S(1)} %shard_map.57), channel_id=1, source_target_pairs={{0,2},{1,3},{2,0},{3,1},{4,6},{5,7},{6,4},{7,5},{8,10},{9,11},{10,... | collective-permute-start | bytes 516104 | tf_op jit(solution)/shard_map/ppermute | solution.py:337
  150.8 9.8 %collective-permute-start.27 = (bf16[1,336,256]{2,1,0:T(8,128)(2,1)S(1)}, bf16[1,336,256]{2,1,0:T(8,128)(2,1)S(1)}, u32[]{:S(2)}, u32[]{:S(2)}) collective-permute-start(bf16[1,336,256]{2,1,0:T(8,128)(2,1)S(1)} %get-tuple-element.55), channel_id=1, source_target_pairs={{0,2},{1,3},{2,0},{3,1},{4,6},{5,7},{6,4},{7,5},{8,10},{9,11},{10,... | collective-permute-start | bytes 516104 | tf_op jit(solution)/shard_map/ppermute | solution.py:337
  152.3 8.3 %collective-permute-start.29 = (bf16[1,336,256]{2,1,0:T(8,128)(2,1)S(1)}, bf16[1,336,256]{2,1,0:T(8,128)(2,1)S(1)}, u32[]{:S(2)}, u32[]{:S(2)}) collective-permute-start(bf16[1,336,256]{2,1,0:T(8,128)(2,1)S(1)} %shard_map.59), channel_id=1, source_target_pairs={{0,1},{1,0},{2,3},{3,2},{4,5},{5,4},{6,7},{7,6},{8,9},{9,8},{10,11... | collective-permute-start | bytes 516104 | tf_op jit(solution)/shard_map/ppermute | solution.py:337
  154.1 9.9 %collective-permute-start.15 = (bf16[336,384]{1,0:T(8,128)(2,1)S(1)}, bf16[336,384]{1,0:T(8,128)(2,1)S(1)}, u32[]{:S(2)}, u32[]{:S(2)}) collective-permute-start(bf16[336,384]{1,0:T(8,128)(2,1)S(1)} %pad_maximum_fusion.2), channel_id=1, source_target_pairs={{0,4},{4,0},{8,12},{12,8},{16,20},{20,16},{24,28},{28,24},{1,5},{5... | collective-permute-start | bytes 774152 | tf_op jit(solution)/shard_map/ppermute | solution.py:340
  157.6 9.6 %collective-permute-start.26 = (bf16[336,256]{1,0:T(8,128)(2,1)S(1)}, bf16[336,256]{1,0:T(8,128)(2,1)S(1)}, u32[]{:S(2)}, u32[]{:S(2)}) collective-permute-start(bf16[336,256]{1,0:T(8,128)(2,1)S(1)} %shard_map.58), channel_id=1, source_target_pairs={{0,16},{4,20},{8,0},{12,4},{16,24},{20,28},{24,8},{28,12},{1,17},{... | collective-permute-start | bytes 516104 | tf_op jit(solution)/shard_map/ppermute | solution.py:450
  160.7 7.2 %collective-permute-start.30 = (bf16[336,256]{1,0:T(8,128)(2,1)S(1)}, bf16[336,256]{1,0:T(8,128)(2,1)S(1)}, u32[]{:S(2)}, u32[]{:S(2)}) collective-permute-start(bf16[336,256]{1,0:T(8,128)(2,1)S(1)} %shard_map.60), channel_id=1, source_target_pairs={{0,20},{4,16},{8,4},{12,0},{16,28},{20,24},{24,12},{28,8},{1,21},{... | collective-permute-start | bytes 516104 | tf_op jit(solution)/shard_map/ppermute | solution.py:450
